TPU v7x, 256 devices: a whole 4x4x8 slice. The times are simulated.
256 devices in a mesh: seg: 8 (over z), tile: 32 (over x, y, core).
Axes of the slice: x: 4, y: 4, z: 8, core: 2. Of those that a mesh axis runs over, the one named last changes fastest.
Arguments:
- samples: bfloat16 [8, 4096, 2048], P('seg', 'tile'), may hold values from -512 to 512
- pair_list: int32 [2, 8192], P(None, 'tile'), may hold values from 0 to 4095, as said below
- sensor_home: int32 [4096], replicated, may hold values from 0 to 4095, as said below
Outputs:
- correlations: bfloat16 [2048, 8192], P('seg', 'tile')
Inputs may be any that keep to these rules, and one draw needn't show every extreme that they name: `pair_list`: row 0 and row 1 name the two sensors of a pair, never the same one. Among the pairs of one index of tile (256 consecutive columns), the sensors whose stored rows lie in one block of 128 consecutive rows are at most 8 different ones. `sensor_home`: each number appears once.
All inputs are finite; a program needn't handle non-finite values.
Results may differ from a plain program's by a relative error of at most 0.019.
Values may be sent and summed in bfloat16 or wider, within the bound.
No kernel may reach another device: no remote copies, remote signals or barrier semaphores. Data moves between devices by JAX's collectives and lax.ppermute only.
A program may use at most 192 MiB of HBM per device.

v0:
```python
import math

import jax
import jax.numpy as jnp
from jax import lax
from jax.sharding import PartitionSpec as P

NFFT = 4096
NF = 2048
BAND = 64
NLAG = 2048
CAP = 8


def whiten_rows(seg_rows):
    row_count = seg_rows.shape[0]
    seg_len = seg_rows.shape[1]
    block_width = min(NF, 256)
    sample_idx = jnp.arange(seg_len, dtype=jnp.int32)[:, None]
    real_parts = []
    imag_parts = []
    for first_bin in range(0, NF, block_width):
        freq_idx = first_bin + jnp.arange(block_width, dtype=jnp.int32)[None, :]
        phase_angle = (sample_idx * freq_idx % NFFT).astype(jnp.float32) * (2.0 * math.pi / NFFT)
        dft_table = jnp.concatenate([jnp.cos(phase_angle), -jnp.sin(phase_angle)], axis=1)
        table_high = lax.optimization_barrier(dft_table.astype(jnp.bfloat16))
        table_low = (dft_table - table_high.astype(jnp.float32)).astype(jnp.bfloat16)
        spectra = jnp.dot(seg_rows, table_high, preferred_element_type=jnp.float32)
        spectra = spectra + jnp.dot(seg_rows, table_low, preferred_element_type=jnp.float32)
        real_part = spectra[:, :block_width].reshape(row_count, block_width // BAND, BAND)
        imag_part = spectra[:, block_width:].reshape(row_count, block_width // BAND, BAND)
        band_power = (
            jnp.mean(real_part * real_part + imag_part * imag_part, axis=2, keepdims=True) + 1e-05
        )
        band_norm = jnp.sqrt(band_power)
        real_parts.append(
            (real_part / band_norm).reshape(row_count, block_width).astype(jnp.bfloat16)
        )
        imag_parts.append(
            (imag_part / band_norm).reshape(row_count, block_width).astype(jnp.bfloat16)
        )
    return jnp.concatenate(real_parts + imag_parts, axis=1)


def lag_table(lag_count, segments):
    lag_idx = jnp.arange(lag_count, dtype=jnp.int32)[:, None] - NLAG // 2
    freq_idx = jnp.arange(NF, dtype=jnp.int32)[None, :]
    phase_angle = (lag_idx * freq_idx % NFFT).astype(jnp.float32) * (2.0 * math.pi / NFFT)
    weight = jnp.where(freq_idx == 0, 1.0, 2.0).astype(jnp.float32) / math.sqrt(NFFT * segments)
    return jnp.concatenate([weight * jnp.cos(phase_angle), -weight * jnp.sin(phase_angle)], axis=1)


def project_lags(lag_count, spectra, segments):
    table = lag_table(lag_count, segments)
    return lax.dot_general(
        table,
        spectra,
        (((1,), (1,)), ((), ())),
        precision=lax.Precision.HIGH,
        preferred_element_type=jnp.float32,
    )


def shards(samples, pair_list, sensor_home):
    tile_count = lax.axis_size("tile")
    segments = lax.axis_size("seg")
    local_samples = samples[0]
    sens_dev = local_samples.shape[0]
    stored = jnp.take(sensor_home, pair_list, axis=0)
    owner_of = stored // sens_dev
    needed = (
        jnp.zeros((tile_count * sens_dev,), jnp.int32)
        .at[stored.reshape(-1)]
        .set(1)
        .reshape(tile_count, sens_dev)
    )
    slot_of = jnp.cumsum(needed, axis=1) - 1
    chosen = (needed[:, :, None] == 1) & (
        slot_of[:, :, None] == jnp.arange(CAP, dtype=jnp.int32)[None, None, :]
    )
    request = jnp.sum(
        jnp.where(chosen, jnp.arange(sens_dev, dtype=jnp.int32)[None, :, None], 0), axis=1
    )
    position = owner_of * CAP + jnp.take(slot_of.reshape(-1), stored, axis=0)
    whitened = whiten_rows(local_samples)
    arrived = lax.all_to_all(
        jnp.take(
            whitened,
            lax.all_to_all(request, "tile", split_axis=0, concat_axis=0, tiled=True),
            axis=0,
        ),
        "tile",
        split_axis=0,
        concat_axis=0,
        tiled=True,
    )
    arrived = arrived.reshape(tile_count * CAP, 2 * NF)
    first_ends = jnp.take(arrived, position[0], axis=0)
    second = jnp.take(arrived, position[1], axis=0)
    re_first = first_ends[:, :NF].astype(jnp.float32)
    im_first = first_ends[:, NF:].astype(jnp.float32)
    re_second = second[:, :NF].astype(jnp.float32)
    im_second = second[:, NF:].astype(jnp.float32)
    cross_spec = jnp.concatenate(
        [re_first * re_second + im_first * im_second, im_first * re_second - re_first * im_second],
        axis=1,
    )
    return lax.psum_scatter(
        project_lags(lax.axis_size("seg") * (NLAG // segments), cross_spec, segments).astype(
            jnp.bfloat16
        ),
        "seg",
        scatter_dimension=0,
        tiled=True,
    )


def solution(mesh):
    return jax.shard_map(
        shards,
        mesh=mesh,
        in_specs=(P("seg", "tile", None), P(None, "tile"), P()),
        out_specs=P("seg", "tile"),
        check_vma=False,
    )
```

profile of v0, /device:TPU:2, one launch (start us, length us, event | category | flops | bytes accessed | tf_op | source)
XLA Modules:
  0.0 273.4 jit_solution(17646132461981449708)
XLA Ops:
  6.5 0.8 fusion.138
  7.3 3.4 %gather_fusion.1 = s32[512]{0:T(512)S(1)} fusion(s32[4096]{0:T(1024)} %param.9, s32[1024]{0:T(1024)S(1)} %pad_clamp_fusion.4), kind=kCustom, calls=%fused_computation.clone | custom fusion | bytes 6144 | tf_op jit(solution)/shard_map/jit(_take)/gather | solution.py:69
  10.8 2.5 scatter_custom_fusion
  13.3 0.3 reduce_window_sum.11
  13.6 1.2 select_reduce_fusion
  14.8 7.6 %all-to-all-start = ((s32[32,1,8]{2,1,0:T(1,128)}), s32[32,1,8]{2,1,0:T(1,128)S(1)}, u32[]{:S(2)}, u32[]{:S(2)}) async-start(s32[32,1,8]{2,1,0:T(1,128)} %bitcast.5), calls=%async_computation | async-start | bytes 32768 | tf_op jit(solution)/shard_map/all_to_all | solution.py:89
  22.5 3.4 %gather_fusion.2 = s32[512]{0:T(512)S(1)} fusion(s32[4096]{0:T(1024)S(1)} %get-tuple-element.27, s32[1024]{0:T(1024)S(1)} %pad_clamp_fusion.3), kind=kCustom, calls=%fused_computation.2.clone | custom fusion | bytes 6144 | tf_op jit(solution)/shard_map/jit(_take)/gather | solution.py:84
  26.1 8.2 %sine_negate_fusion.7 = (f32[2048,256]{1,0:T(8,128)S(1)}, f32[2048,256]{1,0:T(8,128)S(1)}) fusion(), kind=kLoop, calls=%fused_computation.125 | loop fusion | flops 7864320 | bytes 4194304 | tf_op jit(solution)/shard_map/neg | solution.py:25
  34.3 8.8 %fusion.93 = (f32[2048,256]{1,0:T(8,128)S(1)}, f32[2048,256]{1,0:T(8,128)S(1)}) fusion(s32[256]{0:T(256)S(1)} %iota_add_fusion.1), kind=kLoop, calls=%fused_computation.163 | loop fusion | flops 7864320 | bytes 4195328 | tf_op jit(solution)/shard_map/cos | solution.py:25
  43.1 0.2 fusion.13
  43.3 1.0 fusion.75
  44.3 0.8 fusion.84
  45.1 8.4 %fusion.94 = (f32[2048,256]{1,0:T(8,128)S(1)}, f32[2048,256]{1,0:T(8,128)S(1)}) fusion(s32[256]{0:T(256)S(1)} %iota_add_fusion.2), kind=kLoop, calls=%fused_computation.164 | loop fusion | flops 7864320 | bytes 4195328 | tf_op jit(solution)/shard_map/cos | solution.py:25
  53.8 1.0 fusion.74
  54.7 0.8 fusion.85
  55.6 8.5 %fusion.95 = (f32[2048,256]{1,0:T(8,128)S(1)}, f32[2048,256]{1,0:T(8,128)S(1)}) fusion(s32[256]{0:T(256)S(1)} %iota_add_fusion.3), kind=kLoop, calls=%fused_computation.165 | loop fusion | flops 7864320 | bytes 4195328 | tf_op jit(solution)/shard_map/cos | solution.py:25
  64.2 1.0 fusion.73
  65.2 0.8 fusion.86
  66.0 8.6 %fusion.96 = (f32[2048,256]{1,0:T(8,128)S(1)}, f32[2048,256]{1,0:T(8,128)S(1)}) fusion(s32[256]{0:T(256)S(1)} %iota_add_fusion.4), kind=kLoop, calls=%fused_computation.166 | loop fusion | flops 7864320 | bytes 4195328 | tf_op jit(solution)/shard_map/cos | solution.py:25
  74.9 1.0 fusion.72
  75.9 0.8 fusion.87
  76.7 8.2 %fusion.97 = (f32[2048,256]{1,0:T(8,128)S(1)}, f32[2048,256]{1,0:T(8,128)S(1)}) fusion(s32[256]{0:T(256)S(1)} %iota_add_fusion.5), kind=kLoop, calls=%fused_computation.167 | loop fusion | flops 7864320 | bytes 4195328 | tf_op jit(solution)/shard_map/cos | solution.py:25
  85.0 0.2 fusion.17
  85.2 1.1 fusion.71
  86.3 0.8 fusion.88
  87.2 8.2 %fusion.98 = (f32[2048,256]{1,0:T(8,128)S(1)}, f32[2048,256]{1,0:T(8,128)S(1)}) fusion(s32[256]{0:T(256)S(1)} %iota_add_fusion.6), kind=kLoop, calls=%fused_computation.168 | loop fusion | flops 7864320 | bytes 4195328 | tf_op jit(solution)/shard_map/cos | solution.py:25
  95.6 0.9 fusion.70
  96.6 0.8 fusion.89
  97.4 8.5 %fusion.99 = (f32[2048,256]{1,0:T(8,128)S(1)}, f32[2048,256]{1,0:T(8,128)S(1)}) fusion(s32[256]{0:T(256)S(1)} %iota_add_fusion.7), kind=kLoop, calls=%fused_computation.169 | loop fusion | flops 7864320 | bytes 4195328 | tf_op jit(solution)/shard_map/cos | solution.py:25
  105.9 0.2 fusion.19
  106.1 0.9 fusion.69
  107.1 0.8 fusion.90
  107.9 0.2 fusion.20
  108.1 1.0 fusion.68
  109.1 1.2 fusion.91
  110.7 0.5 copy.8
  111.4 3.2 %gather_fusion = bf16[256,4096]{1,0:T(8,128)(2,1)} fusion(bf16[128,4096]{1,0:T(8,128)(2,1)S(1)} %copy.8, s32[1024]{0:T(1024)S(1)} %pad_clamp_fusion.2), kind=kCustom, calls=%fused_computation.4 | custom fusion | bytes 4195328 | tf_op jit(solution)/shard_map/jit(_take)/gather | solution.py:87
  114.6 3.2 %bitcast_select_fusion = bf16[32,8,4096]{2,1,0:T(8,128)(2,1)} fusion(bf16[256,4096]{1,0:T(8,128)(2,1)} %gather_fusion, pred[32,8]{1,0:T(8,128)(4,1)S(1)} %compare_and_fusion), kind=kLoop, calls=%fused_computation.103 | loop fusion | flops 1048576 | bytes 4194560 | tf_op jit(solution)/shard_map/jit(_take)/select_n | solution.py:87
  117.7 7.4 %all-to-all-start.1 = ((bf16[32,8,4096]{2,1,0:T(8,128)(2,1)}), bf16[32,8,4096]{2,1,0:T(8,128)(2,1)S(1)}, u32[]{:S(2)}, u32[]{:S(2)}) async-start(bf16[32,8,4096]{2,1,0:T(8,128)(2,1)} %bitcast_select_fusion), calls=%async_computation.1 | async-start | bytes 4194304 | tf_op jit(solution)/shard_map/all_to_all | solution.py:86
  125.1 69.0 %cosine_multiply_fusion = (f32[2048,2048]{1,0:T(8,128)}, f32[2048,2048]{1,0:T(8,128)}) fusion(s32[2048]{0:T(1024)S(1)} %iota_add_fusion, f32[2048]{0:T(1024)S(1)} %get-tuple-element.51, f32[2048]{0:T(1024)S(1)} %get-tuple-element.52), kind=kLoop, calls=%fused_computation.17 | loop fusion | flops 67108864 | bytes 33579008 | tf_op jit(solution)/shard_map/mul | solution.py:50
  194.2 3.2 %gather_fusion.4 = bf16[256,4096]{1,0:T(8,128)(2,1)} fusion(bf16[256,4096]{1,0:T(8,128)(2,1)S(1)} %bitcast.157, s32[1024]{0:T(1024)S(1)} %get-tuple-element.49), kind=kCustom, calls=%fused_computation.3.clone | custom fusion | bytes 4195328 | tf_op jit(solution)/shard_map/jit(_take)/gather | solution.py:99
  197.4 3.2 %gather_fusion.3 = bf16[256,4096]{1,0:T(8,128)(2,1)} fusion(bf16[256,4096]{1,0:T(8,128)(2,1)S(1)} %bitcast.158, s32[1024]{0:T(1024)S(1)} %get-tuple-element.50), kind=kCustom, calls=%fused_computation.1.clone | custom fusion | bytes 4195328 | tf_op jit(solution)/shard_map/jit(_take)/gather | solution.py:98
  200.6 2.0 broadcast_select_fusion.1
  202.6 0.2 copy-done.2
  202.8 0.3 broadcast_select_fusion
  203.1 2.2 fusion.26
  205.2 19.6 %fusion.21 = bf16[2048,256]{1,0:T(8,128)(2,1)} fusion(f32[256,2048]{1,0:T(8,128)} %get-tuple-element.10, f32[256,2048]{1,0:T(8,128)S(1)} %get-tuple-element.9, f32[2048,2048]{1,0:T(8,128)} %get-tuple-element.30, f32[2048,2048]{1,0:T(8,128)} %get-tuple-element.29), kind=kOutput, calls=%fused_computation.76 | convolution fusion | flops 12894863360 | bytes 38797312 | tf_op jit(solution)/shard_map/dot_general | solution.py:55
  224.8 41.5 %reduce-scatter.2.cloned.1.call-done = bf16[256,256]{1,0:T(8,128)(2,1)} async-done(((bf16[2048,256]{1,0:T(8,128)(2,1)}), bf16[256,256]{1,0:T(8,128)(2,1)}) %reduce-scatter.2.cloned.1.call-update) | async-done | bytes 131088 | tf_op jit(solution)/shard_map/reduce_scatter | solution.py:108
  (87 shorter events, 2.0 us)
Async XLA Ops:
  6.5 36.8 %copy-start = (bf16[1,128,2048]{2,1,0:T(8,128)(2,1)S(1)}, bf16[1,128,2048]{2,1,0:T(8,128)(2,1)}, u32[]{:S(2)}) copy-start(bf16[1,128,2048]{2,1,0:T(8,128)(2,1)} %param.7) | copy-start | bytes 1572868
  6.5 4.2 %copy-start.3 = (s32[2,256]{1,0:T(2,128)S(1)}, s32[2,256]{1,0:T(2,128)}, u32[]{:S(2)}) copy-start(s32[2,256]{1,0:T(2,128)} %param.8) | copy-start | bytes 6148
  14.8 96.4 %all-to-all-start = ((s32[32,1,8]{2,1,0:T(1,128)}), s32[32,1,8]{2,1,0:T(1,128)S(1)}, u32[]{:S(2)}, u32[]{:S(2)}) async-start(s32[32,1,8]{2,1,0:T(1,128)} %bitcast.5), calls=%async_computation | async-start | bytes 32768 | tf_op jit(solution)/shard_map/all_to_all | solution.py:89
  117.7 76.5 %all-to-all-start.1 = ((bf16[32,8,4096]{2,1,0:T(8,128)(2,1)}), bf16[32,8,4096]{2,1,0:T(8,128)(2,1)S(1)}, u32[]{:S(2)}, u32[]{:S(2)}) async-start(bf16[32,8,4096]{2,1,0:T(8,128)(2,1)} %bitcast_select_fusion), calls=%async_computation.1 | async-start | bytes 4194304 | tf_op jit(solution)/shard_map/all_to_all | solution.py:86
  125.1 141.2 %reduce-scatter.2.cloned.1.call-start = ((), (), s32[]{:S(2)}) async-start(), calls=%async_computation.3 | async-start | bytes 1179648 | tf_op jit(solution)/shard_map/reduce_scatter | solution.py:108
  200.6 2.2 copy-start.2
  205.2 61.1 %copy-start.1 = (bf16[1,128,2048]{2,1,0:T(8,128)(2,1)S(1)}, bf16[1,128,2048]{2,1,0:T(8,128)(2,1)}, u32[]{:S(2)}) copy-start(bf16[1,128,2048]{2,1,0:T(8,128)(2,1)} %param.7) | copy-start | bytes 1572868
Sparse Core Ops, SparseCore 0:
  224.9 41.3 reduce-scatter.1
where the time goes:
time: 277 us; the launch traced here: 273 us
  other arithmetic  149 us (54%)
  waiting for transfers between devices  41.5 us (15%)
  matrix products  33.9 us (12%)
  local copies, waits for them, and re-layouts  20 us (7%)
  starting transfers between devices  15 us (5%)
  between operations  14.2 us (5%)
    mul x1, other arithmetic, lag_table(): weight * jnp.cos(phase_angle)  69 us
    cos x7, other arithmetic, whiten_rows(): jnp.cos(phase_angle)  59.2 us
    reduce_scatter x1, waiting for transfers between devices, shards(): lax.psum_scatter(project_lags(lax.axis_size('seg') * (NLAG // segments),...  41.5 us
    dot_general x1, matrix products, project_lags(): lax.dot_general(table, spectra, (((1,), (1,)), ((), ())), precision=lax.P...  19.6 us
    neg x1, other arithmetic, whiten_rows(): -jnp.sin(phase_angle)  8.24 us
    dot_general x8, matrix products, whiten_rows(): jnp.dot(seg_rows, table_low, preferred_element_type=jnp.float32)  7.79 us
    all_to_all x1, starting transfers between devices, shards(): lax.all_to_all(request, 'tile', split_axis=0, concat_axis=0, tiled=True)  7.62 us
    all_to_all x1, starting transfers between devices, shards(): lax.all_to_all(jnp.take(whitened, lax.all_to_all(request, 'tile', split_a...  7.37 us
  transfers between devices with their start and end apart: 3, of which 1 were waited for; matrix products, arithmetic and copies ran while one was open for 58% of the time, Pallas kernels for 0%

commit v1 on v0

v1 whole, which is shorter than its diff:
```python
import functools
import math

import jax
import jax.numpy as jnp
import numpy as np
from jax import lax
from jax.experimental import pallas as pl
from jax.experimental.pallas import tpu as pltpu
from jax.sharding import PartitionSpec as P

NFFT = 4096
NF = 2048
BAND = 64
NLAG = 2048
CAP = 8
RADIX = 32
LANES = 128
HALF = RADIX // 2
F32 = jnp.float32
BF16 = jnp.bfloat16


def _bins():
    k2 = np.arange(NF // RADIX)
    low = [np.arange(HALF), np.concatenate([[HALF], RADIX - np.arange(1, HALF)])]
    return np.concatenate([c[:, None] + RADIX * k2[None, :] for c in low], axis=1)


def _forward_tables():
    bins = _bins()
    n2 = np.arange(LANES)
    half = NF // RADIX
    tables = np.zeros((HALF, 2 * LANES, 2 * LANES))
    for j in range(HALF):
        angle = -2.0 * np.pi * ((n2[:, None] * bins[j][None, :]) % NFFT) / NFFT
        c, s = np.cos(angle), np.sin(angle)
        a, b = slice(0, half), slice(half, LANES)
        top, low = tables[j, :LANES], tables[j, LANES:]
        re, im = slice(0, LANES), slice(LANES, 2 * LANES)
        if j == 0:
            top[:, re][:, a], top[:, im][:, a] = c[:, a], s[:, a]
            low[:, re][:, b], low[:, im][:, b] = c[:, b], s[:, b]
        else:
            sign = np.where(np.arange(LANES) < half, 1.0, -1.0)[None, :]
            top[:, re], top[:, im] = c, s
            low[:, re], low[:, im] = -sign * s, sign * c
    return tables


def _inverse_tables(segments):
    bins = _bins()
    t2 = np.arange(LANES)
    half = NF // RADIX
    tables = np.zeros((HALF, 2 * LANES, 2 * LANES))
    for j in range(HALF):
        weight = np.where(bins[j] == 0, 1.0, 2.0) / math.sqrt(NFFT * segments)
        angle = 2.0 * np.pi * ((bins[j][:, None] * t2[None, :]) % NFFT) / NFFT
        wave = weight[:, None] * np.exp(1j * angle)
        if j == 0:
            for part, cols in ((slice(0, half), slice(0, LANES)), (slice(half, LANES), slice(LANES, 2 * LANES))):
                tables[0, :LANES, cols][part] = wave.real[part]
                tables[0, LANES:, cols][part] = -wave.imag[part]
        else:
            turn = (-1j) ** j
            first = (np.arange(LANES) < half)[:, None]
            of_re = turn * np.where(first, wave, np.conj(wave))
            of_im = turn * np.where(first, 1j * wave, np.conj(1j * wave))
            tables[j, :LANES, :LANES], tables[j, :LANES, LANES:] = of_re.real, of_re.imag
            tables[j, LANES:, :LANES], tables[j, LANES:, LANES:] = of_im.real, of_im.imag
    return tables


def _split(table):
    high = table.astype(BF16)
    low = (table - high.astype(np.float64)).astype(BF16)
    return high, low


def _band_table():
    lane = np.arange(LANES) % (NF // RADIX) // (BAND // RADIX)
    return (lane[:, None] == lane[None, :]).astype(np.float32) / BAND


def _turn(z, k, n, sign):
    re, im = z
    k = k % n
    if k == 0:
        return z
    if 4 * k == n:
        return (-im, re) if sign > 0 else (im, -re)
    if 2 * k == n:
        return (-re, -im)
    if 8 * k == n:
        r = math.sqrt(0.5)
        return ((re - im) * r, (re + im) * r) if sign > 0 else ((re + im) * r, (im - re) * r)
    c, s = math.cos(2 * math.pi * k / n), sign * math.sin(2 * math.pi * k / n)
    return (re * c - im * s, re * s + im * c)


def _add(a, b):
    return (a[0] + b[0], a[1] + b[1])


def _sub(a, b):
    return (a[0] - b[0], a[1] - b[1])


def _dft(z, sign):
    n = len(z)
    if n == 1:
        return list(z)
    half = n // 2
    even = _dft([_add(z[i], z[i + half]) for i in range(half)], sign)
    odd = _dft([_turn(_sub(z[i], z[i + half]), i, n, sign) for i in range(half)], sign)
    return [v for pair in zip(even, odd) for v in pair]


def _odd_bins(x):
    half = len(x) // 2
    z = [_turn((x[n], -x[n + half]), n, 4 * half, -1) if n else (x[0], -x[half]) for n in range(half)]
    return _dft(z, -1)


def _place_odd(out, d, n):
    for q, v in enumerate(d):
        k = 4 * q + 1
        if 2 * k <= n:
            out[k] = v
        else:
            out[n - k] = (v[0], -v[1])


def _rdft(x):
    n = len(x)
    if n == 2:
        return [(x[0] + x[1], None), (x[0] - x[1], None)]
    half = n // 2
    out = [None] * (half + 1)
    out[::2] = _rdft([x[i] + x[i + half] for i in range(half)])
    if n == 4:
        out[1] = (x[0] - x[2], x[3] - x[1])
    else:
        _place_odd(out, _odd_bins([x[i] - x[i + half] for i in range(half)]), n)
    return out


def _forward32(x):
    out = [None] * (HALF + 1)
    out[::2] = _rdft(x)
    _place_odd(out, _odd_bins(x), RADIX)
    return out


def _odd_adjoint(u, n):
    count = n // 4
    d = []
    for q in range(count):
        k = 4 * q + 1
        d.append(u[k] if 2 * k <= n else (u[n - k][0], -u[n - k][1]))
    z = _dft(d, 1)
    y = [_turn(z[i], i, n, 1) for i in range(count)]
    return [v[0] for v in y] + [-v[1] for v in y]


def _rdft_adjoint(u):
    n = 2 * (len(u) - 1)
    if n == 2:
        return [u[0][0] + u[1][0], u[0][0] - u[1][0]]
    a = _rdft_adjoint(u[::2])
    if n == 4:
        b = [u[1][0], -u[1][1]]
    else:
        b = _odd_adjoint(u, n)
    return [p + q for p, q in zip(a, b)] + [p - q for p, q in zip(a, b)]


def _inverse32(u):
    a = _rdft_adjoint(u[::2])
    b = _odd_adjoint(u, RADIX)
    return [p + q for p, q in zip(a, b)]


def _dot(a, b, dims=((1,), (0,))):
    return lax.dot_general(a, b, (dims, ((), ())), preferred_element_type=F32)


def _one_hot(index, rows):
    return (lax.broadcasted_iota(jnp.int32, (rows, index.shape[1]), 0) == index).astype(F32)


def request_kernel(holders, pair_ref, home_ref, want_ref, slot_ref, where_ref):
    pairs = jnp.concatenate([pair_ref[0:1, :], pair_ref[1:2, :]], axis=1)
    home = home_ref[...]
    high = _one_hot(pairs // LANES, home.shape[0]).astype(BF16)
    low = _one_hot(pairs % LANES, LANES)
    first = ((0,), (0,))
    owner = jnp.sum(_dot((home // LANES).astype(F32).astype(BF16), high, first) * low, axis=0, keepdims=True)
    place = jnp.sum(_dot((home % LANES).astype(F32).astype(BF16), high, first) * low, axis=0, keepdims=True)
    owner = owner.astype(jnp.int32)
    place = place.astype(jnp.int32)
    where_ref[0:1, :] = owner
    where_ref[1:2, :] = place
    owners = _one_hot(owner, holders).astype(BF16)
    places = _one_hot(place, LANES).astype(BF16)
    needed = jnp.minimum(_dot(owners, places, ((1,), (1,))), 1.0)
    row = lax.broadcasted_iota(jnp.int32, (LANES, LANES), 0)
    col = lax.broadcasted_iota(jnp.int32, (LANES, LANES), 1)
    slot = _dot(needed.astype(BF16), (row < col).astype(F32).astype(BF16))
    slot_ref[...] = slot
    marked = jnp.where(needed > 0.0, slot, -1.0)
    slots = lax.broadcasted_iota(jnp.int32, (CAP, LANES), 0).astype(F32)
    for holder in range(holders):
        want_ref[holder] = (marked[holder : holder + 1, :] == slots).astype(F32).astype(BF16)


def position_kernel(slot_ref, where_ref, pick_ref):
    owner = where_ref[0:1, :]
    place = where_ref[1:2, :]
    holders = slot_ref.shape[0]
    slot = jnp.minimum(slot_ref[...], CAP - 1.0)
    of_pair = _dot(slot.astype(BF16), _one_hot(owner, holders).astype(BF16), ((0,), (0,)))
    slot = jnp.sum(of_pair * _one_hot(place, LANES), axis=0, keepdims=True)
    position = owner * CAP + slot.astype(jnp.int32)
    pick_ref[...] = _one_hot(position, holders * CAP).T.astype(BF16)


ROWS = 16


def correlate_kernel(
    x_ref, pick_ref, band_ref, high_hbm, low_hbm, inverse_hbm,
    out_ref,
    high_ref, low_ref, inverse_ref, yh_ref, yl_ref, spec_ref, power_ref, u_ref, sems,
):
    copies = [
        pltpu.make_async_copy(src, dst, sems.at[i])
        for i, (src, dst) in enumerate(
            ((high_hbm, high_ref), (low_hbm, low_ref), (inverse_hbm, inverse_ref))
        )
    ]
    for copy in copies:
        copy.start()
    row_count = x_ref.shape[0]
    pair_count = pick_ref.shape[0] // 2
    re, im = slice(0, LANES), slice(LANES, 2 * LANES)

    def put(j, rows, cols, value):
        high = value.astype(BF16)
        yh_ref[j, rows, cols] = high
        yl_ref[j, rows, cols] = (value - high.astype(F32)).astype(BF16)

    @pl.loop(0, row_count // ROWS)
    def _(i):
        rows = pl.ds(pl.multiple_of(i * ROWS, ROWS), ROWS)
        x = [x_ref[rows, n * LANES : (n + 1) * LANES].astype(F32) for n in range(HALF)]
        y = _forward32(x)
        put(0, rows, re, y[0][0])
        put(0, rows, im, y[HALF][0])
        for j in range(1, HALF):
            put(j, rows, re, y[j][0])
            put(j, rows, im, y[j][1])

    copies[0].wait()
    copies[1].wait()
    power_ref[...] = jnp.zeros_like(power_ref)

    @pl.loop(0, HALF)
    def _(j):
        spec = _dot(yh_ref[j], high_ref[j]) + _dot(yh_ref[j], low_ref[j]) + _dot(yl_ref[j], high_ref[j])
        spec_ref[j] = spec
        power_ref[...] += spec[:, re] * spec[:, re] + spec[:, im] * spec[:, im]

    power = lax.dot_general(
        power_ref[...], band_ref[...], (((1,), (0,)), ((), ())),
        precision=lax.Precision.HIGHEST, preferred_element_type=F32,
    )
    power_ref[...] = 1.0 / jnp.sqrt(power + 1e-05)
    copies[2].wait()

    @pl.loop(0, HALF)
    def _(j):
        scale = power_ref[...]
        white = jnp.concatenate(
            [(spec_ref[j, :, re] * scale).astype(BF16), (spec_ref[j, :, im] * scale).astype(BF16)], axis=1
        )
        ends = _dot(pick_ref[...], white)
        a, c = ends[:pair_count], ends[pair_count:]
        cross = jnp.concatenate(
            [
                (a[:, re] * c[:, re] + a[:, im] * c[:, im]).astype(BF16),
                (a[:, im] * c[:, re] - a[:, re] * c[:, im]).astype(BF16),
            ],
            axis=1,
        )
        u_ref[j] = _dot(cross, inverse_ref[j])

    blocks = out_ref.shape[0]
    width = out_ref.shape[2] // LANES

    @pl.loop(0, pair_count // ROWS)
    def _(i):
        rows = pl.ds(pl.multiple_of(i * ROWS, ROWS), ROWS)
        u = [(u_ref[0, rows, re], None)]
        u += [(u_ref[j, rows, re], u_ref[j, rows, im]) for j in range(1, HALF)]
        u += [(u_ref[0, rows, im], None)]
        lags = _inverse32(u)
        for s in range(blocks):
            for h in range(width):
                out_ref[s, rows, h * LANES : (h + 1) * LANES] = lags[s * width + h].astype(BF16)


def sum_kernel(parts_ref, out_ref):
    total = parts_ref[0].astype(F32)
    for s in range(1, parts_ref.shape[0]):
        total = total + parts_ref[s].astype(F32)
    out_ref[...] = total.T.astype(BF16)


VMEM = pl.BlockSpec(memory_space=pltpu.VMEM)
ANY = pl.BlockSpec(memory_space=pl.ANY)


def shards(samples, pair_list, sensor_home):
    tiles = lax.axis_size("tile")
    segments = lax.axis_size("seg")
    local = samples[0]
    sens_dev, seg_len = local.shape
    pair_dev = pair_list.shape[1]
    rows = tiles * CAP
    shape = jax.ShapeDtypeStruct
    want, slot, where = pl.pallas_call(
        functools.partial(request_kernel, tiles),
        out_shape=(
            shape((tiles, CAP, sens_dev), BF16),
            shape((tiles, sens_dev), F32),
            shape((2, 2 * pair_dev), jnp.int32),
        ),
        in_specs=[VMEM] * 2,
        out_specs=(VMEM,) * 3,
        name="request",
    )(pair_list, sensor_home.reshape(-1, LANES))
    asked = lax.all_to_all(want, "tile", split_axis=0, concat_axis=0, tiled=True)
    pick = pl.pallas_call(
        position_kernel,
        out_shape=shape((2 * pair_dev, rows), BF16),
        in_specs=[VMEM] * 2,
        out_specs=VMEM,
        name="position",
    )(slot, where)
    outgoing = jnp.dot(asked.reshape(rows, sens_dev), local, preferred_element_type=F32).astype(BF16)
    arrived = lax.all_to_all(
        outgoing.reshape(tiles, CAP, seg_len), "tile", split_axis=0, concat_axis=0, tiled=True
    )
    high, low = _split(_forward_tables())
    inverse = _inverse_tables(segments).astype(BF16)
    block = (HALF, 2 * LANES, 2 * LANES)
    partial = pl.pallas_call(
        correlate_kernel,
        out_shape=shape((segments, pair_dev, NLAG // segments), BF16),
        in_specs=[VMEM, VMEM, VMEM, ANY, ANY, ANY],
        out_specs=VMEM,
        scratch_shapes=[
            pltpu.VMEM(block, BF16),
            pltpu.VMEM(block, BF16),
            pltpu.VMEM(block, BF16),
            pltpu.VMEM((HALF, rows, 2 * LANES), BF16),
            pltpu.VMEM((HALF, rows, 2 * LANES), BF16),
            pltpu.VMEM((HALF, rows, 2 * LANES), F32),
            pltpu.VMEM((rows, LANES), F32),
            pltpu.VMEM((HALF, pair_dev, 2 * LANES), F32),
            pltpu.SemaphoreType.DMA((3,)),
        ],
        compiler_params=pltpu.CompilerParams(vmem_limit_bytes=40 * 1024 * 1024),
        name="correlate",
    )(arrived.reshape(rows, seg_len), pick, jnp.asarray(_band_table()), jnp.asarray(high), jnp.asarray(low), jnp.asarray(inverse))
    parts = lax.all_to_all(partial, "seg", split_axis=0, concat_axis=0, tiled=True)
    return pl.pallas_call(
        sum_kernel,
        out_shape=shape((NLAG // segments, pair_dev), BF16),
        in_specs=[VMEM],
        out_specs=VMEM,
        name="stack",
    )(parts)


def solution(mesh):
    return jax.shard_map(
        shards,
        mesh=mesh,
        in_specs=(P("seg", "tile", None), P(None, "tile"), P()),
        out_specs=P("seg", "tile"),
        check_vma=False,
    )
```

time: 277 us -> 101 us (0.36)
  the two profiles are of different devices: /device:TPU:2 before, /device:TPU:1 now
where the time goes in v1:
time: 101 us; the launch traced here: 100 us
  blocking collectives  53.2 us (53%)
  Pallas kernels  20.6 us (20%)
  waiting for transfers between devices  15.2 us (15%)
  local copies, waits for them, and re-layouts  5.73 us (6%)
  starting transfers between devices  3.97 us (4%)
  matrix products  1.39 us (1%)
    all_to_all x1, blocking collectives, shards(): lax.all_to_all(partial, 'seg', split_axis=0, concat_axis=0, tiled=True)  37.2 us
    all_to_all x1, blocking collectives, shards(): lax.all_to_all(want, 'tile', split_axis=0, concat_axis=0, tiled=True)  16 us
    all_to_all x1, waiting for transfers between devices, shards(): lax.all_to_all(outgoing.reshape(tiles, CAP, seg_len), 'tile', split_axis=...  15.2 us
    pallas_call x1, Pallas kernels, shards(): pl.pallas_call(correlate_kernel, out_shape=shape((segments, pair_dev, NLA...  14.7 us
    unnamed x12, local copies, waits for them, and re-layouts  5.73 us
    all_to_all x1, starting transfers between devices, shards(): lax.all_to_all(outgoing.reshape(tiles, CAP, seg_len), 'tile', split_axis=...  3.97 us
    pallas_call x1, Pallas kernels, shards(): pl.pallas_call(sum_kernel, out_shape=shape((NLAG // segments, pair_dev),...  2.09 us
  transfers between devices with their start and end apart: 1, of which 1 were waited for; matrix products, arithmetic and copies ran while one was open for 0% of the time, Pallas kernels for 2%

profile of v1, /device:TPU:1, one launch (start us, length us, event | category | flops | bytes accessed | tf_op | source)
XLA Modules:
  0.0 100.1 jit_solution(2515953949163679754)
XLA Ops:
  0.0 0.0 copy-start
  0.0 0.0 copy-start.5
  0.0 2.0 %request.1 = (bf16[32,8,128]{2,1,0:T(8,128)(2,1)}, f32[32,128]{1,0:T(8,128)}, s32[2,512]{1,0:T(2,128)}) custom-call(s32[2,256]{1,0:T(2,128)} %pair_ref.1, s32[32,128]{1,0:T(8,128)} %bitcast.11), custom_call_target="tpu_custom_call" | custom-call | tf_op jit(solution)/shard_map/request/pallas_call | solution.py:332
  2.0 16.0 %all_to_all.15 = bf16[32,8,128]{2,1,0:T(8,128)(2,1)S(1)} all-to-all(bf16[32,8,128]{2,1,0:T(8,128)(2,1)} %get-tuple-element.8), channel_id=1, replica_groups=mesh['seg'=8,'tile'=32] {'tile'}, dimensions={0} | all-to-all | bytes 131072 | tf_op jit(solution)/shard_map/all_to_all | solution.py:343
  18.0 0.0 copy-done
  18.0 1.4 %fusion = bf16[32,8,2048]{2,1,0:T(8,128)(2,1)} fusion(bf16[1,128,2048]{2,1,0:T(8,128)(2,1)S(1)} %copy-done, bf16[32,8,128]{2,1,0:T(8,128)(2,1)S(1)} %all_to_all.15), kind=kOutput, calls=%fused_computation.1 | convolution fusion | flops 134742016 | bytes 1638400 | tf_op jit(solution)/shard_map/dot_general | solution.py:351
  19.4 4.0 %all-to-all-start.1 = ((bf16[32,8,2048]{2,1,0:T(8,128)(2,1)}), bf16[32,8,2048]{2,1,0:T(8,128)(2,1)S(1)}, u32[]{:S(2)}, u32[]{:S(2)}) async-start(bf16[32,8,2048]{2,1,0:T(8,128)(2,1)} %fusion), calls=%async_computation.1 | async-start | bytes 2097152 | tf_op jit(solution)/shard_map/all_to_all | solution.py:352
  23.3 1.8 %position.1.pick_ref = bf16[512,256]{1,0:T(8,128)(2,1)} custom-call(f32[32,128]{1,0:T(8,128)} %get-tuple-element.9.slot_ref, s32[2,512]{1,0:T(2,128)} %get-tuple-element.10.where_ref), custom_call_target="tpu_custom_call" | custom-call | tf_op jit(solution)/shard_map/position/pallas_call | solution.py:344
  25.1 15.2 %all-to-all-done.1 = bf16[32,8,2048]{2,1,0:T(8,128)(2,1)S(1)} async-done(((bf16[32,8,2048]{2,1,0:T(8,128)(2,1)}), bf16[32,8,2048]{2,1,0:T(8,128)(2,1)S(1)}, u32[]{:S(2)}, u32[]{:S(2)}) %all-to-all-start.1) | async-done | bytes 1048608 | tf_op jit(solution)/shard_map/all_to_all | solution.py:352
  40.3 0.0 copy-done.5
  40.3 0.0 copy-start.1
  40.3 1.6 %copy-done.1 = bf16[16,256,256]{2,1,0:T(8,128)(2,1)S(1)} copy-done((bf16[16,256,256]{2,1,0:T(8,128)(2,1)S(1)}, bf16[16,256,256]{2,1,0:T(8,128)(2,1)}, u32[]{:S(2)}) %copy-start.1) | copy-done | bytes 2097176
  41.9 0.0 copy-start.2
  41.9 1.6 %copy-done.2 = bf16[16,256,256]{2,1,0:T(8,128)(2,1)S(1)} copy-done((bf16[16,256,256]{2,1,0:T(8,128)(2,1)S(1)}, bf16[16,256,256]{2,1,0:T(8,128)(2,1)}, u32[]{:S(2)}) %copy-start.2) | copy-done | bytes 2097176
  43.5 0.0 copy-start.3
  43.5 1.6 %copy-done.3 = bf16[16,256,256]{2,1,0:T(8,128)(2,1)S(1)} copy-done((bf16[16,256,256]{2,1,0:T(8,128)(2,1)S(1)}, bf16[16,256,256]{2,1,0:T(8,128)(2,1)}, u32[]{:S(2)}) %copy-start.3) | copy-done | bytes 2097176
  45.1 0.0 copy-start.4
  45.1 0.9 copy-done.4
  46.1 14.7 %correlate.1 = bf16[8,256,256]{2,1,0:T(8,128)(2,1)S(1)} custom-call(bf16[256,2048]{1,0:T(8,128)(2,1)S(1)} %bitcast.10, bf16[512,256]{1,0:T(8,128)(2,1)S(1)} %copy-done.4, f32[128,128]{1,0:T(8,128)S(1)} %copy-done.5, bf16[16,256,256]{2,1,0:T(8,128)(2,1)S(1)} %copy-done.1, bf16[16,256,256]{2,1,0:T(8,128)(2,1)S(1)} %copy-done.2, bf16[16,256,256]{2,1,0:T(8,128)(2,1)S(1)} %copy-done.3), custom_call_target="tpu_custom_call" | custom-call | tf_op jit(solution)/shard_map/correlate/pallas_call | solution.py:358
  60.7 37.2 %all_to_all.16.parts_ref = bf16[8,256,256]{2,1,0:T(8,128)(2,1)} all-to-all(bf16[8,256,256]{2,1,0:T(8,128)(2,1)S(1)} %correlate.1), channel_id=1, replica_groups=mesh['seg'=8,'tile'=32] {'seg'}, dimensions={0} | all-to-all | bytes 2097152 | tf_op jit(solution)/shard_map/all_to_all | solution.py:377
  98.0 2.1 %stack.1 = bf16[256,256]{1,0:T(8,128)(2,1)} custom-call(bf16[8,256,256]{2,1,0:T(8,128)(2,1)} %all_to_all.16.parts_ref), custom_call_target="tpu_custom_call" | custom-call | tf_op jit(solution)/shard_map/stack/pallas_call | solution.py:378
Async XLA Ops:
  0.0 18.0 %copy-start = (bf16[1,128,2048]{2,1,0:T(8,128)(2,1)S(1)}, bf16[1,128,2048]{2,1,0:T(8,128)(2,1)}, u32[]{:S(2)}) copy-start(bf16[1,128,2048]{2,1,0:T(8,128)(2,1)} %param.7) | copy-start | bytes 1572868
  0.0 40.3 %copy-start.5 = (f32[128,128]{1,0:T(8,128)S(1)}, f32[128,128]{1,0:T(8,128)}, u32[]{:S(2)}) copy-start(f32[128,128]{1,0:T(8,128)} %constant.8.clone.band_ref) | copy-start | bytes 196612
  19.4 21.0 %all-to-all-start.1 = ((bf16[32,8,2048]{2,1,0:T(8,128)(2,1)}), bf16[32,8,2048]{2,1,0:T(8,128)(2,1)S(1)}, u32[]{:S(2)}, u32[]{:S(2)}) async-start(bf16[32,8,2048]{2,1,0:T(8,128)(2,1)} %fusion), calls=%async_computation.1 | async-start | bytes 2097152 | tf_op jit(solution)/shard_map/all_to_all | solution.py:352
  40.3 1.6 %copy-start.1 = (bf16[16,256,256]{2,1,0:T(8,128)(2,1)S(1)}, bf16[16,256,256]{2,1,0:T(8,128)(2,1)}, u32[]{:S(2)}) copy-start(bf16[16,256,256]{2,1,0:T(8,128)(2,1)} %constant.9.clone.high_hbm) | copy-start | bytes 6291460
  41.9 1.6 %copy-start.2 = (bf16[16,256,256]{2,1,0:T(8,128)(2,1)S(1)}, bf16[16,256,256]{2,1,0:T(8,128)(2,1)}, u32[]{:S(2)}) copy-start(bf16[16,256,256]{2,1,0:T(8,128)(2,1)} %constant.10.clone.low_hbm) | copy-start | bytes 6291460
  43.5 1.6 %copy-start.3 = (bf16[16,256,256]{2,1,0:T(8,128)(2,1)S(1)}, bf16[16,256,256]{2,1,0:T(8,128)(2,1)}, u32[]{:S(2)}) copy-start(bf16[16,256,256]{2,1,0:T(8,128)(2,1)} %constant.11.clone.inverse_hbm) | copy-start | bytes 6291460
  45.1 0.9 copy-start.4

commit v2 on v1

--- a/solution.py
+++ b/solution.py
@@ -77,11 +77,6 @@
     return high, low
 
 
-def _band_table():
-    lane = np.arange(LANES) % (NF // RADIX) // (BAND // RADIX)
-    return (lane[:, None] == lane[None, :]).astype(np.float32) / BAND
-
-
 def _turn(z, k, n, sign):
     re, im = z
     k = k % n
@@ -185,11 +180,28 @@
     return lax.dot_general(a, b, (dims, ((), ())), preferred_element_type=F32)
 
 
+def _band_mean(power):
+    row = lax.broadcasted_iota(jnp.int32, (LANES, LANES), 0) % (NF // RADIX) // (BAND // RADIX)
+    col = lax.broadcasted_iota(jnp.int32, (LANES, LANES), 1) % (NF // RADIX) // (BAND // RADIX)
+    share = jnp.where(row == col, 1.0 / BAND, 0.0)
+    return lax.dot_general(
+        power, share, (((1,), (0,)), ((), ())), precision=lax.Precision.HIGHEST, preferred_element_type=F32
+    )
+
+
 def _one_hot(index, rows):
     return (lax.broadcasted_iota(jnp.int32, (rows, index.shape[1]), 0) == index).astype(F32)
 
 
-def request_kernel(holders, pair_ref, home_ref, want_ref, slot_ref, where_ref):
+def request_kernel(holders, pair_hbm, home_hbm, want_ref, slot_ref, where_ref, pair_ref, home_ref, sems):
+    copies = [
+        pltpu.make_async_copy(pair_hbm, pair_ref, sems.at[0]),
+        pltpu.make_async_copy(home_hbm, home_ref, sems.at[1]),
+    ]
+    for copy in copies:
+        copy.start()
+    for copy in copies:
+        copy.wait()
     pairs = jnp.concatenate([pair_ref[0:1, :], pair_ref[1:2, :]], axis=1)
     home = home_ref[...]
     high = _one_hot(pairs // LANES, home.shape[0]).astype(BF16)
@@ -229,21 +241,19 @@
 
 
 def correlate_kernel(
-    x_ref, pick_ref, band_ref, high_hbm, low_hbm, inverse_hbm,
-    out_ref,
-    high_ref, low_ref, inverse_ref, yh_ref, yl_ref, spec_ref, power_ref, u_ref, sems,
+    x_ref, pick_ref, table_hbm,
+    lags_ref, far_ref,
+    table_ref, yh_ref, yl_ref, spec_ref, power_ref, u_ref, sems,
 ):
-    copies = [
-        pltpu.make_async_copy(src, dst, sems.at[i])
-        for i, (src, dst) in enumerate(
-            ((high_hbm, high_ref), (low_hbm, low_ref), (inverse_hbm, inverse_ref))
-        )
-    ]
-    for copy in copies:
-        copy.start()
     row_count = x_ref.shape[0]
     pair_count = pick_ref.shape[0] // 2
     re, im = slice(0, LANES), slice(LANES, 2 * LANES)
+    group = table_ref.shape[0] // sems.shape[0]
+    copies = []
+    for i in range(sems.shape[0]):
+        part = pl.ds(i * group, group)
+        copies.append(pltpu.make_async_copy(table_hbm.at[part], table_ref.at[part], sems.at[i]))
+        copies[i].start()
 
     def put(j, rows, cols, value):
         high = value.astype(BF16)
@@ -261,30 +271,32 @@
             put(j, rows, re, y[j][0])
             put(j, rows, im, y[j][1])
 
-    copies[0].wait()
-    copies[1].wait()
-    power_ref[...] = jnp.zeros_like(power_ref)
-
-    @pl.loop(0, HALF)
-    def _(j):
-        spec = _dot(yh_ref[j], high_ref[j]) + _dot(yh_ref[j], low_ref[j]) + _dot(yl_ref[j], high_ref[j])
+    for j in range(HALF):
+        if 2 * j % group == 0:
+            copies[2 * j // group].wait()
+        high, low = table_ref[2 * j], table_ref[2 * j + 1]
+        spec = _dot(yh_ref[j], high) + _dot(yh_ref[j], low) + _dot(yl_ref[j], high)
         spec_ref[j] = spec
-        power_ref[...] += spec[:, re] * spec[:, re] + spec[:, im] * spec[:, im]
-
-    power = lax.dot_general(
-        power_ref[...], band_ref[...], (((1,), (0,)), ((), ())),
-        precision=lax.Precision.HIGHEST, preferred_element_type=F32,
-    )
-    power_ref[...] = 1.0 / jnp.sqrt(power + 1e-05)
-    copies[2].wait()
-
-    @pl.loop(0, HALF)
-    def _(j):
+        power = spec[:, re] * spec[:, re] + spec[:, im] * spec[:, im]
+        power_ref[...] = power if j == 0 else power_ref[...] + power
+
+    power_ref[...] = 1.0 / jnp.sqrt(_band_mean(power_ref[...]) + 1e-05)
+
+    for copy in copies[2 * HALF // group :]:
+        copy.wait()
+
+    def ends_of(j):
         scale = power_ref[...]
         white = jnp.concatenate(
             [(spec_ref[j, :, re] * scale).astype(BF16), (spec_ref[j, :, im] * scale).astype(BF16)], axis=1
         )
-        ends = _dot(pick_ref[...], white)
+        return _dot(pick_ref[...], white)
+
+    ahead = ends_of(0)
+    for j in range(HALF):
+        ends = ahead
+        if j + 1 < HALF:
+            ahead = ends_of(j + 1)
         a, c = ends[:pair_count], ends[pair_count:]
         cross = jnp.concatenate(
             [
@@ -293,10 +305,11 @@
             ],
             axis=1,
         )
-        u_ref[j] = _dot(cross, inverse_ref[j])
-
-    blocks = out_ref.shape[0]
-    width = out_ref.shape[2] // LANES
+        u_ref[j] = _dot(cross, table_ref[2 * HALF + j])
+
+    me = lax.axis_index("seg")
+    blocks = lags_ref.shape[0]
+    width = lags_ref.shape[2] // LANES
 
     @pl.loop(0, pair_count // ROWS)
     def _(i):
@@ -306,19 +319,54 @@
         u += [(u_ref[0, rows, im], None)]
         lags = _inverse32(u)
         for s in range(blocks):
+            place = lax.rem(s - me + blocks, blocks)
             for h in range(width):
-                out_ref[s, rows, h * LANES : (h + 1) * LANES] = lags[s * width + h].astype(BF16)
-
-
-def sum_kernel(parts_ref, out_ref):
-    total = parts_ref[0].astype(F32)
-    for s in range(1, parts_ref.shape[0]):
-        total = total + parts_ref[s].astype(F32)
+                lags_ref[place, rows, h * LANES : (h + 1) * LANES] = lags[s * width + h].astype(BF16)
+
+    far_ref[...] = lags_ref[blocks // 2]
+
+
+def pack_kernel(lags_ref, up_ref, down_ref, keep_ref):
+    up_ref[0], up_ref[1] = lags_ref[3], lags_ref[1]
+    down_ref[0], down_ref[1] = lags_ref[5], lags_ref[7]
+    keep_ref[0], keep_ref[1], keep_ref[2] = lags_ref[2], lags_ref[6], lags_ref[0]
+
+
+def relay_kernel(keep_ref, up_ref, down_ref, far_ref, up_out_ref, down_out_ref):
+    even = lax.axis_index("tile") % 2 == 0
+    far = far_ref[...].astype(F32)
+    up = keep_ref[0].astype(F32) + up_ref[0].astype(F32) + jnp.where(even, far, 0.0)
+    down = keep_ref[1].astype(F32) + down_ref[0].astype(F32) + jnp.where(even, 0.0, far)
+    up_out_ref[...] = up.astype(BF16)
+    down_out_ref[...] = down.astype(BF16)
+
+
+def sum_kernel(keep_ref, up_ref, down_ref, far_up_ref, far_down_ref, out_ref):
+    total = keep_ref[2].astype(F32) + up_ref[1].astype(F32) + down_ref[1].astype(F32)
+    total = total + far_up_ref[...].astype(F32) + far_down_ref[...].astype(F32)
     out_ref[...] = total.T.astype(BF16)
 
 
 VMEM = pl.BlockSpec(memory_space=pltpu.VMEM)
 ANY = pl.BlockSpec(memory_space=pl.ANY)
+MIB = 1024 * 1024
+
+
+def _call(kernel, name, inputs, outputs, args, scratch=(), limit=4, cost=None):
+    return pl.pallas_call(
+        kernel,
+        out_shape=outputs,
+        in_specs=inputs,
+        out_specs=(VMEM,) * len(outputs),
+        scratch_shapes=scratch,
+        compiler_params=pltpu.CompilerParams(vmem_limit_bytes=limit * MIB),
+        cost_estimate=cost,
+        name=name,
+    )(*args)
+
+
+def _in_hbm(value):
+    return pltpu.with_memory_space_constraint(value, pltpu.HBM)
 
 
 def shards(samples, pair_list, sensor_home):
@@ -328,60 +376,91 @@
     sens_dev, seg_len = local.shape
     pair_dev = pair_list.shape[1]
     rows = tiles * CAP
+    lags = NLAG // segments
     shape = jax.ShapeDtypeStruct
-    want, slot, where = pl.pallas_call(
+    home = sensor_home.reshape(-1, LANES)
+    want, slot, where = _call(
         functools.partial(request_kernel, tiles),
-        out_shape=(
+        "request",
+        [ANY] * 2,
+        (
             shape((tiles, CAP, sens_dev), BF16),
             shape((tiles, sens_dev), F32),
             shape((2, 2 * pair_dev), jnp.int32),
         ),
-        in_specs=[VMEM] * 2,
-        out_specs=(VMEM,) * 3,
-        name="request",
-    )(pair_list, sensor_home.reshape(-1, LANES))
+        (_in_hbm(pair_list), _in_hbm(home)),
+        [
+            pltpu.VMEM(pair_list.shape, jnp.int32),
+            pltpu.VMEM(home.shape, jnp.int32),
+            pltpu.SemaphoreType.DMA((2,)),
+        ],
+    )
     asked = lax.all_to_all(want, "tile", split_axis=0, concat_axis=0, tiled=True)
-    pick = pl.pallas_call(
-        position_kernel,
-        out_shape=shape((2 * pair_dev, rows), BF16),
-        in_specs=[VMEM] * 2,
-        out_specs=VMEM,
-        name="position",
-    )(slot, where)
+    (pick,) = _call(
+        position_kernel, "position", [VMEM] * 2, (shape((2 * pair_dev, rows), BF16),), (slot, where)
+    )
+    asked, pick = lax.optimization_barrier((asked, pick))
     outgoing = jnp.dot(asked.reshape(rows, sens_dev), local, preferred_element_type=F32).astype(BF16)
     arrived = lax.all_to_all(
         outgoing.reshape(tiles, CAP, seg_len), "tile", split_axis=0, concat_axis=0, tiled=True
     )
     high, low = _split(_forward_tables())
+    tables = np.stack([high, low], axis=1).reshape(2 * HALF, 2 * LANES, 2 * LANES)
     inverse = _inverse_tables(segments).astype(BF16)
-    block = (HALF, 2 * LANES, 2 * LANES)
-    partial = pl.pallas_call(
+    tables = np.concatenate([tables, inverse])
+    lag_block = (pair_dev, lags)
+    blocks, far = _call(
         correlate_kernel,
-        out_shape=shape((segments, pair_dev, NLAG // segments), BF16),
-        in_specs=[VMEM, VMEM, VMEM, ANY, ANY, ANY],
-        out_specs=VMEM,
-        scratch_shapes=[
-            pltpu.VMEM(block, BF16),
-            pltpu.VMEM(block, BF16),
-            pltpu.VMEM(block, BF16),
+        "correlate",
+        [VMEM] * 2 + [ANY],
+        (pltpu.VMEM((segments,) + lag_block, BF16), pltpu.VMEM(lag_block, BF16)),
+        (arrived.reshape(rows, seg_len), pick, _in_hbm(jnp.asarray(tables))),
+        [
+            pltpu.VMEM(tables.shape, BF16),
             pltpu.VMEM((HALF, rows, 2 * LANES), BF16),
             pltpu.VMEM((HALF, rows, 2 * LANES), BF16),
             pltpu.VMEM((HALF, rows, 2 * LANES), F32),
             pltpu.VMEM((rows, LANES), F32),
             pltpu.VMEM((HALF, pair_dev, 2 * LANES), F32),
-            pltpu.SemaphoreType.DMA((3,)),
+            pltpu.SemaphoreType.DMA((12,)),
         ],
-        compiler_params=pltpu.CompilerParams(vmem_limit_bytes=40 * 1024 * 1024),
-        name="correlate",
-    )(arrived.reshape(rows, seg_len), pick, jnp.asarray(_band_table()), jnp.asarray(high), jnp.asarray(low), jnp.asarray(inverse))
-    parts = lax.all_to_all(partial, "seg", split_axis=0, concat_axis=0, tiled=True)
-    return pl.pallas_call(
+        limit=40,
+    )
+    up, down, keep = _call(
+        pack_kernel,
+        "pack",
+        [VMEM],
+        tuple(pltpu.VMEM((n,) + lag_block, BF16) for n in (2, 2, 3)),
+        (blocks,),
+        cost=pl.CostEstimate(flops=5_000_000_000, bytes_accessed=10_000_000, transcendentals=0),
+    )
+
+    def shift(value, even, odd):
+        ring = [
+            (s * tiles + t, (s + (odd if t % 2 else even)) % segments * tiles + t)
+            for s in range(segments)
+            for t in range(tiles)
+        ]
+        return lax.ppermute(value, ("seg", "tile"), ring)
+
+    up, down = shift(up, 1, 1), shift(down, -1, -1)
+    far = shift(far, 2, -2)
+    on_up, on_down = _call(
+        relay_kernel,
+        "relay",
+        [VMEM] * 4,
+        (pltpu.VMEM(lag_block, BF16),) * 2,
+        (keep, up, down, far),
+    )
+    on_up, on_down = shift(on_up, 2, 2), shift(on_down, -2, -2)
+    (out,) = _call(
         sum_kernel,
-        out_shape=shape((NLAG // segments, pair_dev), BF16),
-        in_specs=[VMEM],
-        out_specs=VMEM,
-        name="stack",
-    )(parts)
+        "stack",
+        [VMEM] * 5,
+        (shape((lags, pair_dev), BF16),),
+        (keep, up, down, on_up, on_down),
+    )
+    return out
 
 
 def solution(mesh):

time: 101 us -> 74.6 us (0.74)
  blocking collectives: 53.2 us -> 20.4 us
  starting transfers between devices: 3.97 us -> 20.9 us
  Pallas kernels: 20.6 us -> 12 us
  local copies, waits for them, and re-layouts: 5.73 us -> 0.01 us
  waiting for transfers between devices: 15.2 us -> 20.6 us
    all_to_all x2 -> x1, blocking collectives: 53.2 us -> 20.4 us  [shards(): lax.all_to_all(outgoing.reshape(tiles, CAP, seg_len), 'tile', split_axis=...]
    ppermute x0 -> x5, waiting for transfers between devices: none -> 13.6 us  [shift(): return lax.ppermute(value, ('seg', 'tile'), ring)]
    ppermute x0 -> x5, starting transfers between devices: none -> 12.3 us  [shift(): return lax.ppermute(value, ('seg', 'tile'), ring)]
    pallas_call x4 -> x6, Pallas kernels: 20.6 us -> 12 us  [_call(): pl.pallas_call(kernel, out_shape=outputs, in_specs=inputs, out_specs=(VME...]
    all_to_all x1, waiting for transfers between devices: 15.2 us -> 7 us  [shards(): lax.all_to_all(want, 'tile', split_axis=0, concat_axis=0, tiled=True)]
    unnamed x12 -> x2, local copies, waits for them, and re-layouts: 5.73 us -> 0.01 us
    all_to_all x1, starting transfers between devices: 3.97 us -> 8.6 us  [shards(): lax.all_to_all(want, 'tile', split_axis=0, concat_axis=0, tiled=True)]
  transfers between devices with their start and end apart: 1 -> 6, of which waited for: 1 -> 4; matrix products, arithmetic and copies ran while one was open for 0% -> 0% of each run, Pallas kernels for 2% -> 0%
where the time goes in v2:
time: 74.6 us; the launch traced here: 74.4 us
  starting transfers between devices  20.9 us (28%)
  waiting for transfers between devices  20.6 us (28%)
  blocking collectives  20.4 us (27%)
  Pallas kernels  12 us (16%)
    all_to_all x1, blocking collectives, shards(): lax.all_to_all(outgoing.reshape(tiles, CAP, seg_len), 'tile', split_axis=...  20.4 us
    ppermute x5, waiting for transfers between devices, shift(): return lax.ppermute(value, ('seg', 'tile'), ring)  13.6 us
    ppermute x5, starting transfers between devices, shift(): return lax.ppermute(value, ('seg', 'tile'), ring)  12.3 us
    pallas_call x6, Pallas kernels, _call(): pl.pallas_call(kernel, out_shape=outputs, in_specs=inputs, out_specs=(VME...  12 us
    all_to_all x1, starting transfers between devices, shards(): lax.all_to_all(want, 'tile', split_axis=0, concat_axis=0, tiled=True)  8.6 us
    all_to_all x1, waiting for transfers between devices, shards(): lax.all_to_all(want, 'tile', split_axis=0, concat_axis=0, tiled=True)  7 us
  transfers between devices with their start and end apart: 6, of which 4 were waited for; matrix products, arithmetic and copies ran while one was open for 0% of the time, Pallas kernels for 0%

profile of v2, /device:TPU:1, one launch (start us, length us, event | category | flops | bytes accessed | tf_op | source)
XLA Modules:
  0.0 74.4 jit_solution(711827164049873477)
XLA Ops:
  0.0 0.0 copy-start
  0.0 2.0 %request.1 = (bf16[32,8,128]{2,1,0:T(8,128)(2,1)}, f32[32,128]{1,0:T(8,128)S(1)}, s32[2,512]{1,0:T(2,128)S(1)}) custom-call(s32[2,256]{1,0:T(2,128)} %pair_hbm.1, s32[32,128]{1,0:T(8,128)} %bitcast.11), custom_call_target="tpu_custom_call" | custom-call | tf_op jit(solution)/shard_map/request/pallas_call | solution.py:356
  2.0 8.6 %all-to-all-start = ((bf16[32,8,128]{2,1,0:T(8,128)(2,1)}), bf16[32,8,128]{2,1,0:T(8,128)(2,1)S(1)}, u32[]{:S(2)}, u32[]{:S(2)}) async-start(bf16[32,8,128]{2,1,0:T(8,128)(2,1)} %get-tuple-element.17), calls=%async_computation | async-start | bytes 131072 | tf_op jit(solution)/shard_map/all_to_all | solution.py:398
  10.6 0.4 position.1.pick_ref
  11.0 7.0 %all-to-all-done = bf16[32,8,128]{2,1,0:T(8,128)(2,1)S(1)} async-done(((bf16[32,8,128]{2,1,0:T(8,128)(2,1)}), bf16[32,8,128]{2,1,0:T(8,128)(2,1)S(1)}, u32[]{:S(2)}, u32[]{:S(2)}) %all-to-all-start) | async-done | bytes 65568 | tf_op jit(solution)/shard_map/all_to_all | solution.py:398
  18.0 0.0 copy-done
  18.0 0.4 fusion
  18.4 20.4 %all_to_all.10 = bf16[32,8,2048]{2,1,0:T(8,128)(2,1)S(1)} all-to-all(bf16[32,8,2048]{2,1,0:T(8,128)(2,1)S(1)} %fusion), channel_id=1, replica_groups=mesh['seg'=8,'tile'=32] {'tile'}, dimensions={0} | all-to-all | bytes 2097152 | tf_op jit(solution)/shard_map/all_to_all | solution.py:404
  38.8 8.6 %correlate.1 = (bf16[8,256,256]{2,1,0:T(8,128)(2,1)S(1)}, bf16[256,256]{1,0:T(8,128)(2,1)S(1)}) custom-call(bf16[256,2048]{1,0:T(8,128)(2,1)S(1)} %bitcast.10, bf16[512,256]{1,0:T(8,128)(2,1)S(1)} %position.1.pick_ref, bf16[48,256,256]{2,1,0:T(8,128)(2,1)} %constant.2.clone.table_hbm), custom_call_target="tpu_custom_call" | custom-call | tf_op jit(solution)/shard_map/correlate/pallas_call | solution.py:356
  47.5 0.1 pack.1
  47.5 1.7 %collective-permute-start = (bf16[2,256,256]{2,1,0:T(8,128)(2,1)S(1)}, bf16[2,256,256]{2,1,0:T(8,128)(2,1)S(1)}, u32[]{:S(2)}, u32[]{:S(2)}) collective-permute-start(bf16[2,256,256]{2,1,0:T(8,128)(2,1)S(1)} %get-tuple-element.24), channel_id=1, source_target_pairs={{0,32},{1,33},{2,34},{3,35},{4,36},{5,37},{6,38},{7,39},{8,40},{9,... | collective-permute-start | bytes 786440 | tf_op jit(solution)/shard_map/ppermute | solution.py:444
  49.2 4.0 %collective-permute-start.1 = (bf16[2,256,256]{2,1,0:T(8,128)(2,1)S(1)}, bf16[2,256,256]{2,1,0:T(8,128)(2,1)S(1)}, u32[]{:S(2)}, u32[]{:S(2)}) collective-permute-start(bf16[2,256,256]{2,1,0:T(8,128)(2,1)S(1)} %get-tuple-element.25), channel_id=1, source_target_pairs={{0,224},{1,225},{2,226},{3,227},{4,228},{5,229},{6,230},{7,231},{8... | collective-permute-start | bytes 786440 | tf_op jit(solution)/shard_map/ppermute | solution.py:444
  53.3 1.8 %collective-permute-start.2 = (bf16[256,256]{1,0:T(8,128)(2,1)S(1)}, bf16[256,256]{1,0:T(8,128)(2,1)S(1)}, u32[]{:S(2)}, u32[]{:S(2)}) collective-permute-start(bf16[256,256]{1,0:T(8,128)(2,1)S(1)} %get-tuple-element.26), channel_id=1, source_target_pairs={{0,64},{1,193},{2,66},{3,195},{4,68},{5,197},{6,70},{7,199},{8,72}... | collective-permute-start | bytes 393224 | tf_op jit(solution)/shard_map/ppermute | solution.py:444
  55.1 7.1 %collective-permute-done.2.far_ref = bf16[256,256]{1,0:T(8,128)(2,1)S(1)} collective-permute-done((bf16[256,256]{1,0:T(8,128)(2,1)S(1)}, bf16[256,256]{1,0:T(8,128)(2,1)S(1)}, u32[]{:S(2)}, u32[]{:S(2)}) %collective-permute-start.2) | collective-permute-done | bytes 131104 | tf_op jit(solution)/shard_map/ppermute | solution.py:444
  62.2 0.0 collective-permute-done.up_ref
  62.2 0.0 collective-permute-done.1.down_ref
  62.2 0.1 relay.1
  62.3 4.7 %collective-permute-start.3 = (bf16[256,256]{1,0:T(8,128)(2,1)S(1)}, bf16[256,256]{1,0:T(8,128)(2,1)S(1)}, u32[]{:S(2)}, u32[]{:S(2)}) collective-permute-start(bf16[256,256]{1,0:T(8,128)(2,1)S(1)} %get-tuple-element.27), channel_id=1, source_target_pairs={{0,64},{1,65},{2,66},{3,67},{4,68},{5,69},{6,70},{7,71},{8,72},{9,... | collective-permute-start | bytes 393224 | tf_op jit(solution)/shard_map/ppermute | solution.py:444
  67.1 0.0 collective-permute-start.4
  67.1 4.9 %collective-permute-done.3.far_up_ref = bf16[256,256]{1,0:T(8,128)(2,1)S(1)} collective-permute-done((bf16[256,256]{1,0:T(8,128)(2,1)S(1)}, bf16[256,256]{1,0:T(8,128)(2,1)S(1)}, u32[]{:S(2)}, u32[]{:S(2)}) %collective-permute-start.3) | collective-permute-done | bytes 131104 | tf_op jit(solution)/shard_map/ppermute | solution.py:444
  72.0 1.6 %collective-permute-done.4.far_down_ref = bf16[256,256]{1,0:T(8,128)(2,1)S(1)} collective-permute-done((bf16[256,256]{1,0:T(8,128)(2,1)S(1)}, bf16[256,256]{1,0:T(8,128)(2,1)S(1)}, u32[]{:S(2)}, u32[]{:S(2)}) %collective-permute-start.4) | collective-permute-done | bytes 131104 | tf_op jit(solution)/shard_map/ppermute | solution.py:444
  73.6 0.8 %stack.1 = bf16[256,256]{1,0:T(8,128)(2,1)} custom-call(bf16[3,256,256]{2,1,0:T(8,128)(2,1)S(1)} %get-tuple-element.23.keep_ref, bf16[2,256,256]{2,1,0:T(8,128)(2,1)S(1)} %collective-permute-done.up_ref, bf16[2,256,256]{2,1,0:T(8,128)(2,1)S(1)} %collective-permute-done.1.down_ref, bf16[256,256]{1,0:T(8,128)(2,1)S(1)} %collective-permute-done.3.far_up_ref, ...), custom_call_target="tpu_custom_call" | custom-call | tf_op jit(solution)/shard_map/stack/pallas_call | solution.py:356
Async XLA Ops:
  0.0 18.0 %copy-start = (bf16[1,128,2048]{2,1,0:T(8,128)(2,1)S(1)}, bf16[1,128,2048]{2,1,0:T(8,128)(2,1)}, u32[]{:S(2)}) copy-start(bf16[1,128,2048]{2,1,0:T(8,128)(2,1)} %param.4) | copy-start | bytes 1572868
  2.0 16.0 %all-to-all-start = ((bf16[32,8,128]{2,1,0:T(8,128)(2,1)}), bf16[32,8,128]{2,1,0:T(8,128)(2,1)S(1)}, u32[]{:S(2)}, u32[]{:S(2)}) async-start(bf16[32,8,128]{2,1,0:T(8,128)(2,1)} %get-tuple-element.17), calls=%async_computation | async-start | bytes 131072 | tf_op jit(solution)/shard_map/all_to_all | solution.py:398
  47.5 14.7 %collective-permute-start = (bf16[2,256,256]{2,1,0:T(8,128)(2,1)S(1)}, bf16[2,256,256]{2,1,0:T(8,128)(2,1)S(1)}, u32[]{:S(2)}, u32[]{:S(2)}) collective-permute-start(bf16[2,256,256]{2,1,0:T(8,128)(2,1)S(1)} %get-tuple-element.24), channel_id=1, source_target_pairs={{0,32},{1,33},{2,34},{3,35},{4,36},{5,37},{6,38},{7,39},{8,40},{9,... | collective-permute-start | bytes 786440 | tf_op jit(solution)/shard_map/ppermute | solution.py:444
  49.2 13.0 %collective-permute-start.1 = (bf16[2,256,256]{2,1,0:T(8,128)(2,1)S(1)}, bf16[2,256,256]{2,1,0:T(8,128)(2,1)S(1)}, u32[]{:S(2)}, u32[]{:S(2)}) collective-permute-start(bf16[2,256,256]{2,1,0:T(8,128)(2,1)S(1)} %get-tuple-element.25), channel_id=1, source_target_pairs={{0,224},{1,225},{2,226},{3,227},{4,228},{5,229},{6,230},{7,231},{8... | collective-permute-start | bytes 786440 | tf_op jit(solution)/shard_map/ppermute | solution.py:444
  53.3 8.9 %collective-permute-start.2 = (bf16[256,256]{1,0:T(8,128)(2,1)S(1)}, bf16[256,256]{1,0:T(8,128)(2,1)S(1)}, u32[]{:S(2)}, u32[]{:S(2)}) collective-permute-start(bf16[256,256]{1,0:T(8,128)(2,1)S(1)} %get-tuple-element.26), channel_id=1, source_target_pairs={{0,64},{1,193},{2,66},{3,195},{4,68},{5,197},{6,70},{7,199},{8,72}... | collective-permute-start | bytes 393224 | tf_op jit(solution)/shard_map/ppermute | solution.py:444
  62.3 9.6 %collective-permute-start.3 = (bf16[256,256]{1,0:T(8,128)(2,1)S(1)}, bf16[256,256]{1,0:T(8,128)(2,1)S(1)}, u32[]{:S(2)}, u32[]{:S(2)}) collective-permute-start(bf16[256,256]{1,0:T(8,128)(2,1)S(1)} %get-tuple-element.27), channel_id=1, source_target_pairs={{0,64},{1,65},{2,66},{3,67},{4,68},{5,69},{6,70},{7,71},{8,72},{9,... | collective-permute-start | bytes 393224 | tf_op jit(solution)/shard_map/ppermute | solution.py:444
  67.1 6.5 %collective-permute-start.4 = (bf16[256,256]{1,0:T(8,128)(2,1)S(1)}, bf16[256,256]{1,0:T(8,128)(2,1)S(1)}, u32[]{:S(2)}, u32[]{:S(2)}) collective-permute-start(bf16[256,256]{1,0:T(8,128)(2,1)S(1)} %get-tuple-element.28), channel_id=1, source_target_pairs={{0,192},{1,193},{2,194},{3,195},{4,196},{5,197},{6,198},{7,199},{8... | collective-permute-start | bytes 393224 | tf_op jit(solution)/shard_map/ppermute | solution.py:444

commit v3 on v2

--- a/solution.py
+++ b/solution.py
@@ -69,6 +69,39 @@
             tables[j, :LANES, :LANES], tables[j, :LANES, LANES:] = of_re.real, of_re.imag
             tables[j, LANES:, :LANES], tables[j, LANES:, LANES:] = of_im.real, of_im.imag
     return tables
+
+
+def _upper_halves(tables, inverse):
+    upper = tables[:, :LANES].copy()
+    upper[0] += tables[0, LANES:]
+    inverse_upper = inverse[:, :LANES].copy()
+    folded = inverse[0, :, :LANES] + inverse[0, :, LANES:]
+    inverse_upper[0] = np.concatenate([folded[:LANES], folded[LANES:]], axis=1)
+    return upper, inverse_upper
+
+
+def _forward_whole(j, upper):
+    c, s = upper[:, :LANES], upper[:, LANES:]
+    first = lax.broadcasted_iota(jnp.int32, c.shape, 1) < NF // RADIX
+    none = jnp.zeros_like(c)
+    if j == 0:
+        above = [jnp.where(first, c, none), jnp.where(first, s, none)]
+        below = [jnp.where(first, none, c), jnp.where(first, none, s)]
+    else:
+        above = [c, s]
+        below = [jnp.where(first, -s, s), jnp.where(first, c, -c)]
+    return jnp.concatenate([jnp.concatenate(above, axis=1), jnp.concatenate(below, axis=1)], axis=0)
+
+
+def _inverse_whole(j, upper):
+    half = NF // RADIX
+    a, b = upper[:, :LANES], upper[:, LANES:]
+    none = jnp.zeros_like(a[:half])
+    if j == 0:
+        parts = [(a[:half], none), (none, a[half:]), (b[:half], none), (none, b[half:])]
+    else:
+        parts = [(a[:half], b[:half]), (a[half:], b[half:]), (-b[:half], a[:half]), (b[half:], -a[half:])]
+    return jnp.concatenate([jnp.concatenate(p, axis=1) for p in parts], axis=0)
 
 
 def _split(table):
@@ -240,20 +273,11 @@
 ROWS = 16
 
 
-def correlate_kernel(
-    x_ref, pick_ref, table_hbm,
-    lags_ref, far_ref,
-    table_ref, yh_ref, yl_ref, spec_ref, power_ref, u_ref, sems,
-):
+def transform_kernel(x_ref, table_hbm, yh_ref, yl_ref, table_ref, sem):
+    copy = pltpu.make_async_copy(table_hbm, table_ref, sem.at[0])
+    copy.start()
     row_count = x_ref.shape[0]
-    pair_count = pick_ref.shape[0] // 2
     re, im = slice(0, LANES), slice(LANES, 2 * LANES)
-    group = table_ref.shape[0] // sems.shape[0]
-    copies = []
-    for i in range(sems.shape[0]):
-        part = pl.ds(i * group, group)
-        copies.append(pltpu.make_async_copy(table_hbm.at[part], table_ref.at[part], sems.at[i]))
-        copies[i].start()
 
     def put(j, rows, cols, value):
         high = value.astype(BF16)
@@ -271,19 +295,20 @@
             put(j, rows, re, y[j][0])
             put(j, rows, im, y[j][1])
 
+    copy.wait()
+
+
+def correlate_kernel(yh_ref, yl_ref, table_ref, pick_ref, lags_ref, spec_ref, power_ref, u_ref):
+    pair_count = pick_ref.shape[0] // 2
+    re, im = slice(0, LANES), slice(LANES, 2 * LANES)
     for j in range(HALF):
-        if 2 * j % group == 0:
-            copies[2 * j // group].wait()
-        high, low = table_ref[2 * j], table_ref[2 * j + 1]
+        high, low = _forward_whole(j, table_ref[2 * j]), _forward_whole(j, table_ref[2 * j + 1])
         spec = _dot(yh_ref[j], high) + _dot(yh_ref[j], low) + _dot(yl_ref[j], high)
         spec_ref[j] = spec
         power = spec[:, re] * spec[:, re] + spec[:, im] * spec[:, im]
         power_ref[...] = power if j == 0 else power_ref[...] + power
 
     power_ref[...] = 1.0 / jnp.sqrt(_band_mean(power_ref[...]) + 1e-05)
-
-    for copy in copies[2 * HALF // group :]:
-        copy.wait()
 
     def ends_of(j):
         scale = power_ref[...]
@@ -305,9 +330,10 @@
             ],
             axis=1,
         )
-        u_ref[j] = _dot(cross, table_ref[2 * HALF + j])
+        u_ref[j] = _dot(cross, _inverse_whole(j, table_ref[2 * HALF + j]))
 
     me = lax.axis_index("seg")
+    even = lax.axis_index("tile") % 2 == 0
     blocks = lags_ref.shape[0]
     width = lags_ref.shape[2] // LANES
 
@@ -319,31 +345,28 @@
         u += [(u_ref[0, rows, im], None)]
         lags = _inverse32(u)
         for s in range(blocks):
-            place = lax.rem(s - me + blocks, blocks)
+            place = lax.rem(jnp.where(even, s - me, me - s) + blocks, blocks)
             for h in range(width):
                 lags_ref[place, rows, h * LANES : (h + 1) * LANES] = lags[s * width + h].astype(BF16)
 
-    far_ref[...] = lags_ref[blocks // 2]
-
-
-def pack_kernel(lags_ref, up_ref, down_ref, keep_ref):
-    up_ref[0], up_ref[1] = lags_ref[3], lags_ref[1]
-    down_ref[0], down_ref[1] = lags_ref[5], lags_ref[7]
-    keep_ref[0], keep_ref[1], keep_ref[2] = lags_ref[2], lags_ref[6], lags_ref[0]
-
-
-def relay_kernel(keep_ref, up_ref, down_ref, far_ref, up_out_ref, down_out_ref):
-    even = lax.axis_index("tile") % 2 == 0
-    far = far_ref[...].astype(F32)
-    up = keep_ref[0].astype(F32) + up_ref[0].astype(F32) + jnp.where(even, far, 0.0)
-    down = keep_ref[1].astype(F32) + down_ref[0].astype(F32) + jnp.where(even, 0.0, far)
-    up_out_ref[...] = up.astype(BF16)
-    down_out_ref[...] = down.astype(BF16)
-
-
-def sum_kernel(keep_ref, up_ref, down_ref, far_up_ref, far_down_ref, out_ref):
-    total = keep_ref[2].astype(F32) + up_ref[1].astype(F32) + down_ref[1].astype(F32)
-    total = total + far_up_ref[...].astype(F32) + far_down_ref[...].astype(F32)
+
+def pack_kernel(lags_ref, far_ref, ahead_ref, back_ref, ahead1_ref, back1_ref, keep_ref):
+    far_ref[...] = lags_ref[4]
+    ahead_ref[...], back_ref[...] = lags_ref[3], lags_ref[5]
+    ahead1_ref[...], back1_ref[...] = lags_ref[1], lags_ref[7]
+    keep_ref[0], keep_ref[1], keep_ref[2] = lags_ref[0], lags_ref[2], lags_ref[6]
+
+
+def relay_kernel(keep_ref, far_ref, ahead_ref, back_ref, ahead_out_ref, back_out_ref):
+    ahead = keep_ref[1].astype(F32) + far_ref[...].astype(F32) + ahead_ref[...].astype(F32)
+    back = keep_ref[2].astype(F32) + back_ref[...].astype(F32)
+    ahead_out_ref[...] = ahead.astype(BF16)
+    back_out_ref[...] = back.astype(BF16)
+
+
+def sum_kernel(keep_ref, ahead_ref, back_ref, ahead2_ref, back2_ref, out_ref):
+    total = keep_ref[0].astype(F32) + ahead_ref[...].astype(F32) + back_ref[...].astype(F32)
+    total = total + ahead2_ref[...].astype(F32) + back2_ref[...].astype(F32)
     out_ref[...] = total.T.astype(BF16)
 
 
@@ -352,7 +375,7 @@
 MIB = 1024 * 1024
 
 
-def _call(kernel, name, inputs, outputs, args, scratch=(), limit=4, cost=None):
+def _call(kernel, name, inputs, outputs, args, scratch=(), limit=4):
     return pl.pallas_call(
         kernel,
         out_shape=outputs,
@@ -360,7 +383,6 @@
         out_specs=(VMEM,) * len(outputs),
         scratch_shapes=scratch,
         compiler_params=pltpu.CompilerParams(vmem_limit_bytes=limit * MIB),
-        cost_estimate=cost,
         name=name,
     )(*args)
 
@@ -404,61 +426,65 @@
     arrived = lax.all_to_all(
         outgoing.reshape(tiles, CAP, seg_len), "tile", split_axis=0, concat_axis=0, tiled=True
     )
-    high, low = _split(_forward_tables())
-    tables = np.stack([high, low], axis=1).reshape(2 * HALF, 2 * LANES, 2 * LANES)
-    inverse = _inverse_tables(segments).astype(BF16)
-    tables = np.concatenate([tables, inverse])
+    forward, inverse = _upper_halves(_forward_tables(), _inverse_tables(segments))
+    tables = np.stack(_split(forward), axis=1).reshape(2 * HALF, LANES, 2 * LANES)
+    tables = np.concatenate([tables, inverse.astype(BF16)])
     lag_block = (pair_dev, lags)
-    blocks, far = _call(
+    spectra = pltpu.VMEM((HALF, rows, 2 * LANES), BF16)
+    yh, yl, tables = _call(
+        transform_kernel,
+        "transform",
+        [VMEM, ANY],
+        (spectra, spectra, pltpu.VMEM(tables.shape, BF16)),
+        (arrived.reshape(rows, seg_len), _in_hbm(jnp.asarray(tables))),
+        [pltpu.SemaphoreType.DMA((1,))],
+        limit=16,
+    )
+    (blocks,) = _call(
         correlate_kernel,
         "correlate",
-        [VMEM] * 2 + [ANY],
-        (pltpu.VMEM((segments,) + lag_block, BF16), pltpu.VMEM(lag_block, BF16)),
-        (arrived.reshape(rows, seg_len), pick, _in_hbm(jnp.asarray(tables))),
+        [VMEM] * 4,
+        (pltpu.VMEM((segments,) + lag_block, BF16),),
+        (yh, yl, tables, pick),
         [
-            pltpu.VMEM(tables.shape, BF16),
-            pltpu.VMEM((HALF, rows, 2 * LANES), BF16),
-            pltpu.VMEM((HALF, rows, 2 * LANES), BF16),
             pltpu.VMEM((HALF, rows, 2 * LANES), F32),
             pltpu.VMEM((rows, LANES), F32),
             pltpu.VMEM((HALF, pair_dev, 2 * LANES), F32),
-            pltpu.SemaphoreType.DMA((12,)),
         ],
-        limit=40,
-    )
-    up, down, keep = _call(
+        limit=24,
+    )
+    far, ahead, back, ahead1, back1, keep = _call(
         pack_kernel,
         "pack",
         [VMEM],
-        tuple(pltpu.VMEM((n,) + lag_block, BF16) for n in (2, 2, 3)),
+        tuple(pltpu.VMEM(n + lag_block, BF16) for n in ((), (), (), (), (), (3,))),
         (blocks,),
-        cost=pl.CostEstimate(flops=5_000_000_000, bytes_accessed=10_000_000, transcendentals=0),
-    )
-
-    def shift(value, even, odd):
+    )
+
+    def shift(value, steps):
         ring = [
-            (s * tiles + t, (s + (odd if t % 2 else even)) % segments * tiles + t)
+            (s * tiles + t, (s + (-steps if t % 2 else steps)) % segments * tiles + t)
             for s in range(segments)
             for t in range(tiles)
         ]
         return lax.ppermute(value, ("seg", "tile"), ring)
 
-    up, down = shift(up, 1, 1), shift(down, -1, -1)
-    far = shift(far, 2, -2)
-    on_up, on_down = _call(
+    far, ahead, back = shift(far, 2), shift(ahead, 1), shift(back, -1)
+    ahead1, back1 = shift(ahead1, 1), shift(back1, -1)
+    ahead2, back2 = _call(
         relay_kernel,
         "relay",
         [VMEM] * 4,
         (pltpu.VMEM(lag_block, BF16),) * 2,
-        (keep, up, down, far),
-    )
-    on_up, on_down = shift(on_up, 2, 2), shift(on_down, -2, -2)
+        (keep, far, ahead, back),
+    )
+    ahead2, back2 = shift(ahead2, 2), shift(back2, -2)
     (out,) = _call(
         sum_kernel,
         "stack",
         [VMEM] * 5,
         (shape((lags, pair_dev), BF16),),
-        (keep, up, down, on_up, on_down),
+        (keep, ahead1, back1, ahead2, back2),
     )
     return out
 

time: 74.6 us -> 70.8 us (0.949)
  waiting for transfers between devices: 20.6 us -> 17.7 us
  Pallas kernels: 12 us -> 11 us
    ppermute x5 -> x7, waiting for transfers between devices: 13.6 us -> 10.7 us  [shift(): return lax.ppermute(value, ('seg', 'tile'), ring)]
    pallas_call x6 -> x7, Pallas kernels: 12 us -> 11 us  [_call(): pl.pallas_call(kernel, out_shape=outputs, in_specs=inputs, out_specs=(VME...]
    ppermute x5 -> x7, starting transfers between devices: 12.3 us -> 11.9 us  [shift(): return lax.ppermute(value, ('seg', 'tile'), ring)]
  transfers between devices with their start and end apart: 6 -> 8, of which waited for: 4 -> 6; matrix products, arithmetic and copies ran while one was open for 0% -> 0% of each run, Pallas kernels for 0% -> 1%
where the time goes in v3:
time: 70.8 us; the launch traced here: 70.2 us
  starting transfers between devices  20.5 us (29%)
  blocking collectives  20.4 us (29%)
  waiting for transfers between devices  17.7 us (25%)
  Pallas kernels  11 us (16%)
    all_to_all x1, blocking collectives, shards(): lax.all_to_all(outgoing.reshape(tiles, CAP, seg_len), 'tile', split_axis=...  20.4 us
    ppermute x7, starting transfers between devices, shift(): return lax.ppermute(value, ('seg', 'tile'), ring)  11.9 us
    pallas_call x7, Pallas kernels, _call(): pl.pallas_call(kernel, out_shape=outputs, in_specs=inputs, out_specs=(VME...  11 us
    ppermute x7, waiting for transfers between devices, shift(): return lax.ppermute(value, ('seg', 'tile'), ring)  10.7 us
    all_to_all x1, starting transfers between devices, shards(): lax.all_to_all(want, 'tile', split_axis=0, concat_axis=0, tiled=True)  8.6 us
    all_to_all x1, waiting for transfers between devices, shards(): lax.all_to_all(want, 'tile', split_axis=0, concat_axis=0, tiled=True)  7 us
  transfers between devices with their start and end apart: 8, of which 6 were waited for; matrix products, arithmetic and copies ran while one was open for 0% of the time, Pallas kernels for 1%

profile of v3, /device:TPU:1, one launch (start us, length us, event | category | flops | bytes accessed | tf_op | source)
XLA Modules:
  0.0 70.2 jit_solution(13418109489773183219)
XLA Ops:
  0.0 0.0 copy-start
  0.0 2.0 %request.1 = (bf16[32,8,128]{2,1,0:T(8,128)(2,1)}, f32[32,128]{1,0:T(8,128)S(1)}, s32[2,512]{1,0:T(2,128)S(1)}) custom-call(s32[2,256]{1,0:T(2,128)} %pair_hbm.1, s32[32,128]{1,0:T(8,128)} %bitcast.11), custom_call_target="tpu_custom_call" | custom-call | tf_op jit(solution)/shard_map/request/pallas_call | solution.py:379
  2.0 8.6 %all-to-all-start = ((bf16[32,8,128]{2,1,0:T(8,128)(2,1)}), bf16[32,8,128]{2,1,0:T(8,128)(2,1)S(1)}, u32[]{:S(2)}, u32[]{:S(2)}) async-start(bf16[32,8,128]{2,1,0:T(8,128)(2,1)} %get-tuple-element.21), calls=%async_computation | async-start | bytes 131072 | tf_op jit(solution)/shard_map/all_to_all | solution.py:420
  10.6 0.4 position.1.pick_ref
  11.0 7.0 %all-to-all-done = bf16[32,8,128]{2,1,0:T(8,128)(2,1)S(1)} async-done(((bf16[32,8,128]{2,1,0:T(8,128)(2,1)}), bf16[32,8,128]{2,1,0:T(8,128)(2,1)S(1)}, u32[]{:S(2)}, u32[]{:S(2)}) %all-to-all-start) | async-done | bytes 65568 | tf_op jit(solution)/shard_map/all_to_all | solution.py:420
  18.0 0.0 copy-done
  18.0 0.4 fusion
  18.4 20.4 %all_to_all.10 = bf16[32,8,2048]{2,1,0:T(8,128)(2,1)S(1)} all-to-all(bf16[32,8,2048]{2,1,0:T(8,128)(2,1)S(1)} %fusion), channel_id=1, replica_groups=mesh['seg'=8,'tile'=32] {'tile'}, dimensions={0} | all-to-all | bytes 2097152 | tf_op jit(solution)/shard_map/all_to_all | solution.py:426
  38.8 1.9 %transform.1 = (bf16[16,256,256]{2,1,0:T(8,128)(2,1)S(1)}, bf16[16,256,256]{2,1,0:T(8,128)(2,1)S(1)}, bf16[48,128,256]{2,1,0:T(8,128)(2,1)S(1)}) custom-call(bf16[256,2048]{1,0:T(8,128)(2,1)S(1)} %bitcast.10, bf16[48,128,256]{2,1,0:T(8,128)(2,1)} %constant.2.clone.table_hbm), custom_call_target="tpu_custom_call" | custom-call | tf_op jit(solution)/shard_map/transform/pallas_call | solution.py:379
  40.8 5.8 %correlate.1.lags_ref = bf16[8,256,256]{2,1,0:T(8,128)(2,1)S(1)} custom-call(bf16[16,256,256]{2,1,0:T(8,128)(2,1)S(1)} %get-tuple-element.25.yh_ref, bf16[16,256,256]{2,1,0:T(8,128)(2,1)S(1)} %get-tuple-element.26.yl_ref, bf16[48,128,256]{2,1,0:T(8,128)(2,1)S(1)} %get-tuple-element.27.table_ref, bf16[512,256]{1,0:T(8,128)(2,1)S(1)} %position.1.pick_ref), custom_call_target="tpu_custom_call" | custom-call | tf_op jit(solution)/shard_map/correlate/pallas_call | solution.py:379
  46.5 0.1 pack.1
  46.6 6.1 %collective-permute-start.2 = (bf16[256,256]{1,0:T(8,128)(2,1)S(1)}, bf16[256,256]{1,0:T(8,128)(2,1)S(1)}, u32[]{:S(2)}, u32[]{:S(2)}) collective-permute-start(bf16[256,256]{1,0:T(8,128)(2,1)S(1)} %get-tuple-element.32), channel_id=1, source_target_pairs={{0,64},{1,193},{2,66},{3,195},{4,68},{5,197},{6,70},{7,199},{8,72}... | collective-permute-start | bytes 393224 | tf_op jit(solution)/shard_map/ppermute | solution.py:470
  52.7 0.7 %collective-permute-start.3 = (bf16[256,256]{1,0:T(8,128)(2,1)S(1)}, bf16[256,256]{1,0:T(8,128)(2,1)S(1)}, u32[]{:S(2)}, u32[]{:S(2)}) collective-permute-start(bf16[256,256]{1,0:T(8,128)(2,1)S(1)} %get-tuple-element.33), channel_id=1, source_target_pairs={{0,32},{1,225},{2,34},{3,227},{4,36},{5,229},{6,38},{7,231},{8,40}... | collective-permute-start | bytes 393224 | tf_op jit(solution)/shard_map/ppermute | solution.py:470
  53.4 0.7 %collective-permute-start.4 = (bf16[256,256]{1,0:T(8,128)(2,1)S(1)}, bf16[256,256]{1,0:T(8,128)(2,1)S(1)}, u32[]{:S(2)}, u32[]{:S(2)}) collective-permute-start(bf16[256,256]{1,0:T(8,128)(2,1)S(1)} %get-tuple-element.34), channel_id=1, source_target_pairs={{0,224},{1,33},{2,226},{3,35},{4,228},{5,37},{6,230},{7,39},{8,232... | collective-permute-start | bytes 393224 | tf_op jit(solution)/shard_map/ppermute | solution.py:470
  54.2 1.9 %collective-permute-start = (bf16[256,256]{1,0:T(8,128)(2,1)S(1)}, bf16[256,256]{1,0:T(8,128)(2,1)S(1)}, u32[]{:S(2)}, u32[]{:S(2)}) collective-permute-start(bf16[256,256]{1,0:T(8,128)(2,1)S(1)} %get-tuple-element.30), channel_id=1, source_target_pairs={{0,32},{1,225},{2,34},{3,227},{4,36},{5,229},{6,38},{7,231},{8,40}... | collective-permute-start | bytes 393224 | tf_op jit(solution)/shard_map/ppermute | solution.py:470
  56.1 0.0 collective-permute-start.1
  56.1 0.8 %collective-permute-done.2.far_ref = bf16[256,256]{1,0:T(8,128)(2,1)S(1)} collective-permute-done((bf16[256,256]{1,0:T(8,128)(2,1)S(1)}, bf16[256,256]{1,0:T(8,128)(2,1)S(1)}, u32[]{:S(2)}, u32[]{:S(2)}) %collective-permute-start.2) | collective-permute-done | bytes 131104 | tf_op jit(solution)/shard_map/ppermute | solution.py:470
  56.9 2.8 %collective-permute-done.3.ahead_ref = bf16[256,256]{1,0:T(8,128)(2,1)S(1)} collective-permute-done((bf16[256,256]{1,0:T(8,128)(2,1)S(1)}, bf16[256,256]{1,0:T(8,128)(2,1)S(1)}, u32[]{:S(2)}, u32[]{:S(2)}) %collective-permute-start.3) | collective-permute-done | bytes 131104 | tf_op jit(solution)/shard_map/ppermute | solution.py:470
  59.7 0.5 collective-permute-done.4.back_ref
  60.2 0.1 relay.1
  60.3 1.5 %collective-permute-start.5 = (bf16[256,256]{1,0:T(8,128)(2,1)S(1)}, bf16[256,256]{1,0:T(8,128)(2,1)S(1)}, u32[]{:S(2)}, u32[]{:S(2)}) collective-permute-start(bf16[256,256]{1,0:T(8,128)(2,1)S(1)} %get-tuple-element.35), channel_id=1, source_target_pairs={{0,64},{1,193},{2,66},{3,195},{4,68},{5,197},{6,70},{7,199},{8,72}... | collective-permute-start | bytes 393224 | tf_op jit(solution)/shard_map/ppermute | solution.py:470
  61.8 0.9 %collective-permute-start.6 = (bf16[256,256]{1,0:T(8,128)(2,1)S(1)}, bf16[256,256]{1,0:T(8,128)(2,1)S(1)}, u32[]{:S(2)}, u32[]{:S(2)}) collective-permute-start(bf16[256,256]{1,0:T(8,128)(2,1)S(1)} %get-tuple-element.36), channel_id=1, source_target_pairs={{0,192},{1,65},{2,194},{3,67},{4,196},{5,69},{6,198},{7,71},{8,200... | collective-permute-start | bytes 393224 | tf_op jit(solution)/shard_map/ppermute | solution.py:470
  62.8 0.0 collective-permute-done.ahead_ref
  62.8 0.0 collective-permute-done.1.back_ref
  62.8 3.7 %collective-permute-done.5.ahead2_ref = bf16[256,256]{1,0:T(8,128)(2,1)S(1)} collective-permute-done((bf16[256,256]{1,0:T(8,128)(2,1)S(1)}, bf16[256,256]{1,0:T(8,128)(2,1)S(1)}, u32[]{:S(2)}, u32[]{:S(2)}) %collective-permute-start.5) | collective-permute-done | bytes 131104 | tf_op jit(solution)/shard_map/ppermute | solution.py:470
  66.5 2.9 %collective-permute-done.6.back2_ref = bf16[256,256]{1,0:T(8,128)(2,1)S(1)} collective-permute-done((bf16[256,256]{1,0:T(8,128)(2,1)S(1)}, bf16[256,256]{1,0:T(8,128)(2,1)S(1)}, u32[]{:S(2)}, u32[]{:S(2)}) %collective-permute-start.6) | collective-permute-done | bytes 131104 | tf_op jit(solution)/shard_map/ppermute | solution.py:470
  69.4 0.8 %stack.1 = bf16[256,256]{1,0:T(8,128)(2,1)} custom-call(bf16[3,256,256]{2,1,0:T(8,128)(2,1)S(1)} %get-tuple-element.29.keep_ref, bf16[256,256]{1,0:T(8,128)(2,1)S(1)} %collective-permute-done.ahead_ref, bf16[256,256]{1,0:T(8,128)(2,1)S(1)} %collective-permute-done.1.back_ref, bf16[256,256]{1,0:T(8,128)(2,1)S(1)} %collective-permute-done.5.ahead2_ref, ...), custom_call_target="tpu_custom_call" | custom-call | tf_op jit(solution)/shard_map/stack/pallas_call | solution.py:379
Async XLA Ops:
  0.0 18.0 %copy-start = (bf16[1,128,2048]{2,1,0:T(8,128)(2,1)S(1)}, bf16[1,128,2048]{2,1,0:T(8,128)(2,1)}, u32[]{:S(2)}) copy-start(bf16[1,128,2048]{2,1,0:T(8,128)(2,1)} %param.4) | copy-start | bytes 1572868
  2.0 16.0 %all-to-all-start = ((bf16[32,8,128]{2,1,0:T(8,128)(2,1)}), bf16[32,8,128]{2,1,0:T(8,128)(2,1)S(1)}, u32[]{:S(2)}, u32[]{:S(2)}) async-start(bf16[32,8,128]{2,1,0:T(8,128)(2,1)} %get-tuple-element.21), calls=%async_computation | async-start | bytes 131072 | tf_op jit(solution)/shard_map/all_to_all | solution.py:420
  46.6 10.3 %collective-permute-start.2 = (bf16[256,256]{1,0:T(8,128)(2,1)S(1)}, bf16[256,256]{1,0:T(8,128)(2,1)S(1)}, u32[]{:S(2)}, u32[]{:S(2)}) collective-permute-start(bf16[256,256]{1,0:T(8,128)(2,1)S(1)} %get-tuple-element.32), channel_id=1, source_target_pairs={{0,64},{1,193},{2,66},{3,195},{4,68},{5,197},{6,70},{7,199},{8,72}... | collective-permute-start | bytes 393224 | tf_op jit(solution)/shard_map/ppermute | solution.py:470
  52.7 7.0 %collective-permute-start.3 = (bf16[256,256]{1,0:T(8,128)(2,1)S(1)}, bf16[256,256]{1,0:T(8,128)(2,1)S(1)}, u32[]{:S(2)}, u32[]{:S(2)}) collective-permute-start(bf16[256,256]{1,0:T(8,128)(2,1)S(1)} %get-tuple-element.33), channel_id=1, source_target_pairs={{0,32},{1,225},{2,34},{3,227},{4,36},{5,229},{6,38},{7,231},{8,40}... | collective-permute-start | bytes 393224 | tf_op jit(solution)/shard_map/ppermute | solution.py:470
  53.4 6.8 %collective-permute-start.4 = (bf16[256,256]{1,0:T(8,128)(2,1)S(1)}, bf16[256,256]{1,0:T(8,128)(2,1)S(1)}, u32[]{:S(2)}, u32[]{:S(2)}) collective-permute-start(bf16[256,256]{1,0:T(8,128)(2,1)S(1)} %get-tuple-element.34), channel_id=1, source_target_pairs={{0,224},{1,33},{2,226},{3,35},{4,228},{5,37},{6,230},{7,39},{8,232... | collective-permute-start | bytes 393224 | tf_op jit(solution)/shard_map/ppermute | solution.py:470
  54.2 8.6 %collective-permute-start = (bf16[256,256]{1,0:T(8,128)(2,1)S(1)}, bf16[256,256]{1,0:T(8,128)(2,1)S(1)}, u32[]{:S(2)}, u32[]{:S(2)}) collective-permute-start(bf16[256,256]{1,0:T(8,128)(2,1)S(1)} %get-tuple-element.30), channel_id=1, source_target_pairs={{0,32},{1,225},{2,34},{3,227},{4,36},{5,229},{6,38},{7,231},{8,40}... | collective-permute-start | bytes 393224 | tf_op jit(solution)/shard_map/ppermute | solution.py:470
  56.1 6.6 %collective-permute-start.1 = (bf16[256,256]{1,0:T(8,128)(2,1)S(1)}, bf16[256,256]{1,0:T(8,128)(2,1)S(1)}, u32[]{:S(2)}, u32[]{:S(2)}) collective-permute-start(bf16[256,256]{1,0:T(8,128)(2,1)S(1)} %get-tuple-element.31), channel_id=1, source_target_pairs={{0,224},{1,33},{2,226},{3,35},{4,228},{5,37},{6,230},{7,39},{8,232... | collective-permute-start | bytes 393224 | tf_op jit(solution)/shard_map/ppermute | solution.py:470
  60.3 6.2 %collective-permute-start.5 = (bf16[256,256]{1,0:T(8,128)(2,1)S(1)}, bf16[256,256]{1,0:T(8,128)(2,1)S(1)}, u32[]{:S(2)}, u32[]{:S(2)}) collective-permute-start(bf16[256,256]{1,0:T(8,128)(2,1)S(1)} %get-tuple-element.35), channel_id=1, source_target_pairs={{0,64},{1,193},{2,66},{3,195},{4,68},{5,197},{6,70},{7,199},{8,72}... | collective-permute-start | bytes 393224 | tf_op jit(solution)/shard_map/ppermute | solution.py:470
  61.8 7.5 %collective-permute-start.6 = (bf16[256,256]{1,0:T(8,128)(2,1)S(1)}, bf16[256,256]{1,0:T(8,128)(2,1)S(1)}, u32[]{:S(2)}, u32[]{:S(2)}) collective-permute-start(bf16[256,256]{1,0:T(8,128)(2,1)S(1)} %get-tuple-element.36), channel_id=1, source_target_pairs={{0,192},{1,65},{2,194},{3,67},{4,196},{5,69},{6,198},{7,71},{8,200... | collective-permute-start | bytes 393224 | tf_op jit(solution)/shard_map/ppermute | solution.py:470

commit v4 on v3

--- a/solution.py
+++ b/solution.py
@@ -216,10 +216,10 @@
 def _band_mean(power):
     row = lax.broadcasted_iota(jnp.int32, (LANES, LANES), 0) % (NF // RADIX) // (BAND // RADIX)
     col = lax.broadcasted_iota(jnp.int32, (LANES, LANES), 1) % (NF // RADIX) // (BAND // RADIX)
-    share = jnp.where(row == col, 1.0 / BAND, 0.0)
-    return lax.dot_general(
-        power, share, (((1,), (0,)), ((), ())), precision=lax.Precision.HIGHEST, preferred_element_type=F32
-    )
+    share = jnp.where(row == col, 1.0 / BAND, 0.0).astype(BF16)
+    high = power.astype(BF16)
+    low = (power - high.astype(F32)).astype(BF16)
+    return _dot(high, share) + _dot(low, share)
 
 
 def _one_hot(index, rows):
@@ -259,7 +259,9 @@
         want_ref[holder] = (marked[holder : holder + 1, :] == slots).astype(F32).astype(BF16)
 
 
-def position_kernel(slot_ref, where_ref, pick_ref):
+def position_kernel(slot_ref, where_ref, table_hbm, pick_ref, table_ref, sem):
+    copy = pltpu.make_async_copy(table_hbm, table_ref, sem.at[0])
+    copy.start()
     owner = where_ref[0:1, :]
     place = where_ref[1:2, :]
     holders = slot_ref.shape[0]
@@ -268,6 +270,7 @@
     slot = jnp.sum(of_pair * _one_hot(place, LANES), axis=0, keepdims=True)
     position = owner * CAP + slot.astype(jnp.int32)
     pick_ref[...] = _one_hot(position, holders * CAP).T.astype(BF16)
+    copy.wait()
 
 
 ROWS = 16
@@ -298,7 +301,7 @@
     copy.wait()
 
 
-def correlate_kernel(yh_ref, yl_ref, table_ref, pick_ref, lags_ref, spec_ref, power_ref, u_ref):
+def correlate_kernel(yh_ref, yl_ref, table_ref, inverse_ref, pick_ref, lags_ref, spec_ref, power_ref, u_ref):
     pair_count = pick_ref.shape[0] // 2
     re, im = slice(0, LANES), slice(LANES, 2 * LANES)
     for j in range(HALF):
@@ -317,11 +320,11 @@
         )
         return _dot(pick_ref[...], white)
 
-    ahead = ends_of(0)
+    queue = [ends_of(0), ends_of(1)]
     for j in range(HALF):
-        ends = ahead
-        if j + 1 < HALF:
-            ahead = ends_of(j + 1)
+        ends = queue.pop(0)
+        if j + 2 < HALF:
+            queue.append(ends_of(j + 2))
         a, c = ends[:pair_count], ends[pair_count:]
         cross = jnp.concatenate(
             [
@@ -330,7 +333,7 @@
             ],
             axis=1,
         )
-        u_ref[j] = _dot(cross, _inverse_whole(j, table_ref[2 * HALF + j]))
+        u_ref[j] = _dot(cross, _inverse_whole(j, inverse_ref[j]))
 
     me = lax.axis_index("seg")
     even = lax.axis_index("tile") % 2 == 0
@@ -418,34 +421,39 @@
         ],
     )
     asked = lax.all_to_all(want, "tile", split_axis=0, concat_axis=0, tiled=True)
-    (pick,) = _call(
-        position_kernel, "position", [VMEM] * 2, (shape((2 * pair_dev, rows), BF16),), (slot, where)
+    forward, inverse = _upper_halves(_forward_tables(), _inverse_tables(segments))
+    forward = np.stack(_split(forward), axis=1).reshape(2 * HALF, LANES, 2 * LANES)
+    inverse = jnp.asarray(inverse.astype(BF16))
+    pick, inverse = _call(
+        position_kernel,
+        "position",
+        [VMEM] * 2 + [ANY],
+        (pltpu.VMEM((2 * pair_dev, rows), BF16), pltpu.VMEM(inverse.shape, BF16)),
+        (slot, where, _in_hbm(inverse)),
+        [pltpu.SemaphoreType.DMA((1,))],
     )
     asked, pick = lax.optimization_barrier((asked, pick))
     outgoing = jnp.dot(asked.reshape(rows, sens_dev), local, preferred_element_type=F32).astype(BF16)
     arrived = lax.all_to_all(
         outgoing.reshape(tiles, CAP, seg_len), "tile", split_axis=0, concat_axis=0, tiled=True
     )
-    forward, inverse = _upper_halves(_forward_tables(), _inverse_tables(segments))
-    tables = np.stack(_split(forward), axis=1).reshape(2 * HALF, LANES, 2 * LANES)
-    tables = np.concatenate([tables, inverse.astype(BF16)])
     lag_block = (pair_dev, lags)
     spectra = pltpu.VMEM((HALF, rows, 2 * LANES), BF16)
-    yh, yl, tables = _call(
+    yh, yl, forward = _call(
         transform_kernel,
         "transform",
         [VMEM, ANY],
-        (spectra, spectra, pltpu.VMEM(tables.shape, BF16)),
-        (arrived.reshape(rows, seg_len), _in_hbm(jnp.asarray(tables))),
+        (spectra, spectra, pltpu.VMEM(forward.shape, BF16)),
+        (arrived.reshape(rows, seg_len), _in_hbm(jnp.asarray(forward))),
         [pltpu.SemaphoreType.DMA((1,))],
         limit=16,
     )
     (blocks,) = _call(
         correlate_kernel,
         "correlate",
-        [VMEM] * 4,
+        [VMEM] * 5,
         (pltpu.VMEM((segments,) + lag_block, BF16),),
-        (yh, yl, tables, pick),
+        (yh, yl, forward, inverse, pick),
         [
             pltpu.VMEM((HALF, rows, 2 * LANES), F32),
             pltpu.VMEM((rows, LANES), F32),

time: 70.8 us -> 70.9 us (level)
    ppermute x7, waiting for transfers between devices: 10.7 us -> 12.1 us  [shift(): return lax.ppermute(value, ('seg', 'tile'), ring)]
    all_to_all x1, waiting for transfers between devices: 7 us -> 6.12 us  [shards(): lax.all_to_all(want, 'tile', split_axis=0, concat_axis=0, tiled=True)]
  transfers between devices with their start and end apart: 8 -> 8, of which waited for: 6 -> 6; matrix products, arithmetic and copies ran while one was open for 0% -> 0% of each run, Pallas kernels for 1% -> 2%
where the time goes in v4:
time: 70.9 us; the launch traced here: 70.7 us
  starting transfers between devices  20.5 us (29%)
  blocking collectives  20.4 us (29%)
  waiting for transfers between devices  18.2 us (26%)
  Pallas kernels  11 us (16%)
    all_to_all x1, blocking collectives, shards(): lax.all_to_all(outgoing.reshape(tiles, CAP, seg_len), 'tile', split_axis=...  20.4 us
    ppermute x7, waiting for transfers between devices, shift(): return lax.ppermute(value, ('seg', 'tile'), ring)  12.1 us
    ppermute x7, starting transfers between devices, shift(): return lax.ppermute(value, ('seg', 'tile'), ring)  11.9 us
    pallas_call x7, Pallas kernels, _call(): pl.pallas_call(kernel, out_shape=outputs, in_specs=inputs, out_specs=(VME...  11 us
    all_to_all x1, starting transfers between devices, shards(): lax.all_to_all(want, 'tile', split_axis=0, concat_axis=0, tiled=True)  8.6 us
    all_to_all x1, waiting for transfers between devices, shards(): lax.all_to_all(want, 'tile', split_axis=0, concat_axis=0, tiled=True)  6.12 us
  transfers between devices with their start and end apart: 8, of which 6 were waited for; matrix products, arithmetic and copies ran while one was open for 0% of the time, Pallas kernels for 2%

profile of v4, /device:TPU:1, one launch (start us, length us, event | category | flops | bytes accessed | tf_op | source)
XLA Modules:
  0.0 70.7 jit_solution(6056683010957387201)
XLA Ops:
  0.0 0.0 copy-start
  0.0 2.0 %request.1 = (bf16[32,8,128]{2,1,0:T(8,128)(2,1)}, f32[32,128]{1,0:T(8,128)S(1)}, s32[2,512]{1,0:T(2,128)S(1)}) custom-call(s32[2,256]{1,0:T(2,128)} %pair_hbm.1, s32[32,128]{1,0:T(8,128)} %bitcast.11), custom_call_target="tpu_custom_call" | custom-call | tf_op jit(solution)/shard_map/request/pallas_call | solution.py:382
  2.0 8.6 %all-to-all-start = ((bf16[32,8,128]{2,1,0:T(8,128)(2,1)}), bf16[32,8,128]{2,1,0:T(8,128)(2,1)S(1)}, u32[]{:S(2)}, u32[]{:S(2)}) async-start(bf16[32,8,128]{2,1,0:T(8,128)(2,1)} %get-tuple-element.23), calls=%async_computation | async-start | bytes 131072 | tf_op jit(solution)/shard_map/all_to_all | solution.py:423
  10.6 1.2 %position.1 = (bf16[512,256]{1,0:T(8,128)(2,1)S(1)}, bf16[16,128,256]{2,1,0:T(8,128)(2,1)S(1)}) custom-call(f32[32,128]{1,0:T(8,128)S(1)} %get-tuple-element.24.slot_ref, s32[2,512]{1,0:T(2,128)S(1)} %get-tuple-element.25.where_ref, bf16[16,128,256]{2,1,0:T(8,128)(2,1)} %constant.4.clone.table_hbm), custom_call_target="tpu_custom_call" | custom-call | tf_op jit(solution)/shard_map/position/pallas_call | solution.py:382
  11.9 6.1 %all-to-all-done = bf16[32,8,128]{2,1,0:T(8,128)(2,1)S(1)} async-done(((bf16[32,8,128]{2,1,0:T(8,128)(2,1)}), bf16[32,8,128]{2,1,0:T(8,128)(2,1)S(1)}, u32[]{:S(2)}, u32[]{:S(2)}) %all-to-all-start) | async-done | bytes 65568 | tf_op jit(solution)/shard_map/all_to_all | solution.py:423
  18.0 0.0 copy-done
  18.0 0.4 fusion
  18.4 20.4 %all_to_all.10 = bf16[32,8,2048]{2,1,0:T(8,128)(2,1)S(1)} all-to-all(bf16[32,8,2048]{2,1,0:T(8,128)(2,1)S(1)} %fusion), channel_id=1, replica_groups=mesh['seg'=8,'tile'=32] {'tile'}, dimensions={0} | all-to-all | bytes 2097152 | tf_op jit(solution)/shard_map/all_to_all | solution.py:437
  38.8 1.7 %transform.1 = (bf16[16,256,256]{2,1,0:T(8,128)(2,1)S(1)}, bf16[16,256,256]{2,1,0:T(8,128)(2,1)S(1)}, bf16[32,128,256]{2,1,0:T(8,128)(2,1)S(1)}) custom-call(bf16[256,2048]{1,0:T(8,128)(2,1)S(1)} %bitcast.10, bf16[32,128,256]{2,1,0:T(8,128)(2,1)} %constant.5.clone.table_hbm), custom_call_target="tpu_custom_call" | custom-call | tf_op jit(solution)/shard_map/transform/pallas_call | solution.py:382
  40.5 5.1 %correlate.1.lags_ref = bf16[8,256,256]{2,1,0:T(8,128)(2,1)S(1)} custom-call(bf16[16,256,256]{2,1,0:T(8,128)(2,1)S(1)} %get-tuple-element.28.yh_ref, bf16[16,256,256]{2,1,0:T(8,128)(2,1)S(1)} %get-tuple-element.29.yl_ref, bf16[32,128,256]{2,1,0:T(8,128)(2,1)S(1)} %get-tuple-element.30.table_ref, bf16[16,128,256]{2,1,0:T(8,128)(2,1)S(1)} %get-tuple-element.31.inverse_ref, ...), custom_call_target="tpu_custom_call" | custom-call | tf_op jit(solution)/shard_map/correlate/pallas_call | solution.py:382
  45.7 0.1 pack.1
  45.8 6.1 %collective-permute-start.2 = (bf16[256,256]{1,0:T(8,128)(2,1)S(1)}, bf16[256,256]{1,0:T(8,128)(2,1)S(1)}, u32[]{:S(2)}, u32[]{:S(2)}) collective-permute-start(bf16[256,256]{1,0:T(8,128)(2,1)S(1)} %get-tuple-element.36), channel_id=1, source_target_pairs={{0,64},{1,193},{2,66},{3,195},{4,68},{5,197},{6,70},{7,199},{8,72}... | collective-permute-start | bytes 393224 | tf_op jit(solution)/shard_map/ppermute | solution.py:478
  51.9 0.7 %collective-permute-start.3 = (bf16[256,256]{1,0:T(8,128)(2,1)S(1)}, bf16[256,256]{1,0:T(8,128)(2,1)S(1)}, u32[]{:S(2)}, u32[]{:S(2)}) collective-permute-start(bf16[256,256]{1,0:T(8,128)(2,1)S(1)} %get-tuple-element.37), channel_id=1, source_target_pairs={{0,32},{1,225},{2,34},{3,227},{4,36},{5,229},{6,38},{7,231},{8,40}... | collective-permute-start | bytes 393224 | tf_op jit(solution)/shard_map/ppermute | solution.py:478
  52.6 0.7 %collective-permute-start.4 = (bf16[256,256]{1,0:T(8,128)(2,1)S(1)}, bf16[256,256]{1,0:T(8,128)(2,1)S(1)}, u32[]{:S(2)}, u32[]{:S(2)}) collective-permute-start(bf16[256,256]{1,0:T(8,128)(2,1)S(1)} %get-tuple-element.38), channel_id=1, source_target_pairs={{0,224},{1,33},{2,226},{3,35},{4,228},{5,37},{6,230},{7,39},{8,232... | collective-permute-start | bytes 393224 | tf_op jit(solution)/shard_map/ppermute | solution.py:478
  53.3 1.9 %collective-permute-start = (bf16[256,256]{1,0:T(8,128)(2,1)S(1)}, bf16[256,256]{1,0:T(8,128)(2,1)S(1)}, u32[]{:S(2)}, u32[]{:S(2)}) collective-permute-start(bf16[256,256]{1,0:T(8,128)(2,1)S(1)} %get-tuple-element.34), channel_id=1, source_target_pairs={{0,32},{1,225},{2,34},{3,227},{4,36},{5,229},{6,38},{7,231},{8,40}... | collective-permute-start | bytes 393224 | tf_op jit(solution)/shard_map/ppermute | solution.py:478
  55.3 0.0 collective-permute-start.1
  55.3 0.8 %collective-permute-done.2.far_ref = bf16[256,256]{1,0:T(8,128)(2,1)S(1)} collective-permute-done((bf16[256,256]{1,0:T(8,128)(2,1)S(1)}, bf16[256,256]{1,0:T(8,128)(2,1)S(1)}, u32[]{:S(2)}, u32[]{:S(2)}) %collective-permute-start.2) | collective-permute-done | bytes 131104 | tf_op jit(solution)/shard_map/ppermute | solution.py:478
  56.1 2.8 %collective-permute-done.3.ahead_ref = bf16[256,256]{1,0:T(8,128)(2,1)S(1)} collective-permute-done((bf16[256,256]{1,0:T(8,128)(2,1)S(1)}, bf16[256,256]{1,0:T(8,128)(2,1)S(1)}, u32[]{:S(2)}, u32[]{:S(2)}) %collective-permute-start.3) | collective-permute-done | bytes 131104 | tf_op jit(solution)/shard_map/ppermute | solution.py:478
  58.9 0.5 collective-permute-done.4.back_ref
  59.4 0.1 relay.1
  59.5 1.5 %collective-permute-start.5 = (bf16[256,256]{1,0:T(8,128)(2,1)S(1)}, bf16[256,256]{1,0:T(8,128)(2,1)S(1)}, u32[]{:S(2)}, u32[]{:S(2)}) collective-permute-start(bf16[256,256]{1,0:T(8,128)(2,1)S(1)} %get-tuple-element.39), channel_id=1, source_target_pairs={{0,64},{1,193},{2,66},{3,195},{4,68},{5,197},{6,70},{7,199},{8,72}... | collective-permute-start | bytes 393224 | tf_op jit(solution)/shard_map/ppermute | solution.py:478
  61.0 0.9 %collective-permute-start.6 = (bf16[256,256]{1,0:T(8,128)(2,1)S(1)}, bf16[256,256]{1,0:T(8,128)(2,1)S(1)}, u32[]{:S(2)}, u32[]{:S(2)}) collective-permute-start(bf16[256,256]{1,0:T(8,128)(2,1)S(1)} %get-tuple-element.40), channel_id=1, source_target_pairs={{0,192},{1,65},{2,194},{3,67},{4,196},{5,69},{6,198},{7,71},{8,200... | collective-permute-start | bytes 393224 | tf_op jit(solution)/shard_map/ppermute | solution.py:478
  61.9 0.0 collective-permute-done.ahead_ref
  61.9 0.0 collective-permute-done.1.back_ref
  61.9 3.7 %collective-permute-done.5.ahead2_ref = bf16[256,256]{1,0:T(8,128)(2,1)S(1)} collective-permute-done((bf16[256,256]{1,0:T(8,128)(2,1)S(1)}, bf16[256,256]{1,0:T(8,128)(2,1)S(1)}, u32[]{:S(2)}, u32[]{:S(2)}) %collective-permute-start.5) | collective-permute-done | bytes 131104 | tf_op jit(solution)/shard_map/ppermute | solution.py:478
  65.6 4.2 %collective-permute-done.6.back2_ref = bf16[256,256]{1,0:T(8,128)(2,1)S(1)} collective-permute-done((bf16[256,256]{1,0:T(8,128)(2,1)S(1)}, bf16[256,256]{1,0:T(8,128)(2,1)S(1)}, u32[]{:S(2)}, u32[]{:S(2)}) %collective-permute-start.6) | collective-permute-done | bytes 131104 | tf_op jit(solution)/shard_map/ppermute | solution.py:478
  69.9 0.8 %stack.1 = bf16[256,256]{1,0:T(8,128)(2,1)} custom-call(bf16[3,256,256]{2,1,0:T(8,128)(2,1)S(1)} %get-tuple-element.33.keep_ref, bf16[256,256]{1,0:T(8,128)(2,1)S(1)} %collective-permute-done.ahead_ref, bf16[256,256]{1,0:T(8,128)(2,1)S(1)} %collective-permute-done.1.back_ref, bf16[256,256]{1,0:T(8,128)(2,1)S(1)} %collective-permute-done.5.ahead2_ref, ...), custom_call_target="tpu_custom_call" | custom-call | tf_op jit(solution)/shard_map/stack/pallas_call | solution.py:382
Async XLA Ops:
  0.0 18.0 %copy-start = (bf16[1,128,2048]{2,1,0:T(8,128)(2,1)S(1)}, bf16[1,128,2048]{2,1,0:T(8,128)(2,1)}, u32[]{:S(2)}) copy-start(bf16[1,128,2048]{2,1,0:T(8,128)(2,1)} %param.5) | copy-start | bytes 1572868
  2.0 16.0 %all-to-all-start = ((bf16[32,8,128]{2,1,0:T(8,128)(2,1)}), bf16[32,8,128]{2,1,0:T(8,128)(2,1)S(1)}, u32[]{:S(2)}, u32[]{:S(2)}) async-start(bf16[32,8,128]{2,1,0:T(8,128)(2,1)} %get-tuple-element.23), calls=%async_computation | async-start | bytes 131072 | tf_op jit(solution)/shard_map/all_to_all | solution.py:423
  45.8 10.3 %collective-permute-start.2 = (bf16[256,256]{1,0:T(8,128)(2,1)S(1)}, bf16[256,256]{1,0:T(8,128)(2,1)S(1)}, u32[]{:S(2)}, u32[]{:S(2)}) collective-permute-start(bf16[256,256]{1,0:T(8,128)(2,1)S(1)} %get-tuple-element.36), channel_id=1, source_target_pairs={{0,64},{1,193},{2,66},{3,195},{4,68},{5,197},{6,70},{7,199},{8,72}... | collective-permute-start | bytes 393224 | tf_op jit(solution)/shard_map/ppermute | solution.py:478
  51.9 7.0 %collective-permute-start.3 = (bf16[256,256]{1,0:T(8,128)(2,1)S(1)}, bf16[256,256]{1,0:T(8,128)(2,1)S(1)}, u32[]{:S(2)}, u32[]{:S(2)}) collective-permute-start(bf16[256,256]{1,0:T(8,128)(2,1)S(1)} %get-tuple-element.37), channel_id=1, source_target_pairs={{0,32},{1,225},{2,34},{3,227},{4,36},{5,229},{6,38},{7,231},{8,40}... | collective-permute-start | bytes 393224 | tf_op jit(solution)/shard_map/ppermute | solution.py:478
  52.6 6.8 %collective-permute-start.4 = (bf16[256,256]{1,0:T(8,128)(2,1)S(1)}, bf16[256,256]{1,0:T(8,128)(2,1)S(1)}, u32[]{:S(2)}, u32[]{:S(2)}) collective-permute-start(bf16[256,256]{1,0:T(8,128)(2,1)S(1)} %get-tuple-element.38), channel_id=1, source_target_pairs={{0,224},{1,33},{2,226},{3,35},{4,228},{5,37},{6,230},{7,39},{8,232... | collective-permute-start | bytes 393224 | tf_op jit(solution)/shard_map/ppermute | solution.py:478
  53.3 8.6 %collective-permute-start = (bf16[256,256]{1,0:T(8,128)(2,1)S(1)}, bf16[256,256]{1,0:T(8,128)(2,1)S(1)}, u32[]{:S(2)}, u32[]{:S(2)}) collective-permute-start(bf16[256,256]{1,0:T(8,128)(2,1)S(1)} %get-tuple-element.34), channel_id=1, source_target_pairs={{0,32},{1,225},{2,34},{3,227},{4,36},{5,229},{6,38},{7,231},{8,40}... | collective-permute-start | bytes 393224 | tf_op jit(solution)/shard_map/ppermute | solution.py:478
  55.3 6.6 %collective-permute-start.1 = (bf16[256,256]{1,0:T(8,128)(2,1)S(1)}, bf16[256,256]{1,0:T(8,128)(2,1)S(1)}, u32[]{:S(2)}, u32[]{:S(2)}) collective-permute-start(bf16[256,256]{1,0:T(8,128)(2,1)S(1)} %get-tuple-element.35), channel_id=1, source_target_pairs={{0,224},{1,33},{2,226},{3,35},{4,228},{5,37},{6,230},{7,39},{8,232... | collective-permute-start | bytes 393224 | tf_op jit(solution)/shard_map/ppermute | solution.py:478
  59.5 6.2 %collective-permute-start.5 = (bf16[256,256]{1,0:T(8,128)(2,1)S(1)}, bf16[256,256]{1,0:T(8,128)(2,1)S(1)}, u32[]{:S(2)}, u32[]{:S(2)}) collective-permute-start(bf16[256,256]{1,0:T(8,128)(2,1)S(1)} %get-tuple-element.39), channel_id=1, source_target_pairs={{0,64},{1,193},{2,66},{3,195},{4,68},{5,197},{6,70},{7,199},{8,72}... | collective-permute-start | bytes 393224 | tf_op jit(solution)/shard_map/ppermute | solution.py:478
  61.0 8.9 %collective-permute-start.6 = (bf16[256,256]{1,0:T(8,128)(2,1)S(1)}, bf16[256,256]{1,0:T(8,128)(2,1)S(1)}, u32[]{:S(2)}, u32[]{:S(2)}) collective-permute-start(bf16[256,256]{1,0:T(8,128)(2,1)S(1)} %get-tuple-element.40), channel_id=1, source_target_pairs={{0,192},{1,65},{2,194},{3,67},{4,196},{5,69},{6,198},{7,71},{8,200... | collective-permute-start | bytes 393224 | tf_op jit(solution)/shard_map/ppermute | solution.py:478

commit v5 on v4

--- a/solution.py
+++ b/solution.py
@@ -237,13 +237,12 @@
         copy.wait()
     pairs = jnp.concatenate([pair_ref[0:1, :], pair_ref[1:2, :]], axis=1)
     home = home_ref[...]
-    high = _one_hot(pairs // LANES, home.shape[0]).astype(BF16)
-    low = _one_hot(pairs % LANES, LANES)
-    first = ((0,), (0,))
-    owner = jnp.sum(_dot((home // LANES).astype(F32).astype(BF16), high, first) * low, axis=0, keepdims=True)
-    place = jnp.sum(_dot((home % LANES).astype(F32).astype(BF16), high, first) * low, axis=0, keepdims=True)
-    owner = owner.astype(jnp.int32)
-    place = place.astype(jnp.int32)
+    high = _one_hot(pairs // LANES, home.shape[0])
+    low = _one_hot(pairs % LANES, LANES).astype(BF16)
+    stored = jnp.concatenate([home // LANES, home % LANES], axis=0).astype(F32).astype(BF16)
+    columns = _dot(stored, low)
+    owner = jnp.sum(columns[: home.shape[0]] * high, axis=0, keepdims=True).astype(jnp.int32)
+    place = jnp.sum(columns[home.shape[0] :] * high, axis=0, keepdims=True).astype(jnp.int32)
     where_ref[0:1, :] = owner
     where_ref[1:2, :] = place
     owners = _one_hot(owner, holders).astype(BF16)
@@ -301,7 +300,7 @@
     copy.wait()
 
 
-def correlate_kernel(yh_ref, yl_ref, table_ref, inverse_ref, pick_ref, lags_ref, spec_ref, power_ref, u_ref):
+def correlate_kernel(yh_ref, yl_ref, table_ref, inverse_ref, pick_ref, lags_ref, spec_ref, power_ref, u_ref, cross_ref):
     pair_count = pick_ref.shape[0] // 2
     re, im = slice(0, LANES), slice(LANES, 2 * LANES)
     for j in range(HALF):
@@ -320,6 +319,7 @@
         )
         return _dot(pick_ref[...], white)
 
+    half = pair_count // 2
     queue = [ends_of(0), ends_of(1)]
     for j in range(HALF):
         ends = queue.pop(0)
@@ -333,16 +333,15 @@
             ],
             axis=1,
         )
-        u_ref[j] = _dot(cross, _inverse_whole(j, inverse_ref[j]))
+        u_ref[j, :half] = _dot(cross[:half], _inverse_whole(j, inverse_ref[j]))
+        cross_ref[j] = cross[half:]
 
     me = lax.axis_index("seg")
     even = lax.axis_index("tile") % 2 == 0
     blocks = lags_ref.shape[0]
     width = lags_ref.shape[2] // LANES
 
-    @pl.loop(0, pair_count // ROWS)
-    def _(i):
-        rows = pl.ds(pl.multiple_of(i * ROWS, ROWS), ROWS)
+    def lags_of(rows):
         u = [(u_ref[0, rows, re], None)]
         u += [(u_ref[j, rows, re], u_ref[j, rows, im]) for j in range(1, HALF)]
         u += [(u_ref[0, rows, im], None)]
@@ -352,6 +351,16 @@
             for h in range(width):
                 lags_ref[place, rows, h * LANES : (h + 1) * LANES] = lags[s * width + h].astype(BF16)
 
+    steps = half // ROWS
+    for j in range(HALF):
+        u_ref[j, half:] = _dot(cross_ref[j], _inverse_whole(j, inverse_ref[j]))
+        for i in range(j * steps // HALF, (j + 1) * steps // HALF):
+            lags_of(slice(i * ROWS, (i + 1) * ROWS))
+
+    @pl.loop(steps, pair_count // ROWS)
+    def _(i):
+        lags_of(pl.ds(pl.multiple_of(i * ROWS, ROWS), ROWS))
+
 
 def pack_kernel(lags_ref, far_ref, ahead_ref, back_ref, ahead1_ref, back1_ref, keep_ref):
     far_ref[...] = lags_ref[4]
@@ -367,10 +376,18 @@
     back_out_ref[...] = back.astype(BF16)
 
 
-def sum_kernel(keep_ref, ahead_ref, back_ref, ahead2_ref, back2_ref, out_ref):
-    total = keep_ref[0].astype(F32) + ahead_ref[...].astype(F32) + back_ref[...].astype(F32)
-    total = total + ahead2_ref[...].astype(F32) + back2_ref[...].astype(F32)
-    out_ref[...] = total.T.astype(BF16)
+def sum_kernel(keep_ref, ahead_ref, back_ref, ahead2_ref, back2_ref, out_hbm, out_ref, sems):
+    half = out_ref.shape[0] // 2
+    copies = []
+    for i in range(2):
+        part = slice(i * half, (i + 1) * half)
+        total = keep_ref[0, :, part].astype(F32) + ahead_ref[:, part].astype(F32) + back_ref[:, part].astype(F32)
+        total = total + ahead2_ref[:, part].astype(F32) + back2_ref[:, part].astype(F32)
+        out_ref[part] = total.T.astype(BF16)
+        copies.append(pltpu.make_async_copy(out_ref.at[part], out_hbm.at[part], sems.at[i]))
+        copies[i].start()
+    for copy in copies:
+        copy.wait()
 
 
 VMEM = pl.BlockSpec(memory_space=pltpu.VMEM)
@@ -378,12 +395,12 @@
 MIB = 1024 * 1024
 
 
-def _call(kernel, name, inputs, outputs, args, scratch=(), limit=4):
+def _call(kernel, name, inputs, outputs, args, scratch=(), limit=4, place=VMEM):
     return pl.pallas_call(
         kernel,
         out_shape=outputs,
         in_specs=inputs,
-        out_specs=(VMEM,) * len(outputs),
+        out_specs=(place,) * len(outputs),
         scratch_shapes=scratch,
         compiler_params=pltpu.CompilerParams(vmem_limit_bytes=limit * MIB),
         name=name,
@@ -409,9 +426,9 @@
         "request",
         [ANY] * 2,
         (
-            shape((tiles, CAP, sens_dev), BF16),
-            shape((tiles, sens_dev), F32),
-            shape((2, 2 * pair_dev), jnp.int32),
+            pltpu.VMEM((tiles, CAP, sens_dev), BF16),
+            pltpu.VMEM((tiles, sens_dev), F32),
+            pltpu.VMEM((2, 2 * pair_dev), jnp.int32),
         ),
         (_in_hbm(pair_list), _in_hbm(home)),
         [
@@ -458,6 +475,7 @@
             pltpu.VMEM((HALF, rows, 2 * LANES), F32),
             pltpu.VMEM((rows, LANES), F32),
             pltpu.VMEM((HALF, pair_dev, 2 * LANES), F32),
+            pltpu.VMEM((HALF, pair_dev // 2, 2 * LANES), BF16),
         ],
         limit=24,
     )
@@ -493,6 +511,8 @@
         [VMEM] * 5,
         (shape((lags, pair_dev), BF16),),
         (keep, ahead1, back1, ahead2, back2),
+        [pltpu.VMEM((lags, pair_dev), BF16), pltpu.SemaphoreType.DMA((2,))],
+        place=ANY,
     )
     return out
 

time: 70.9 us -> 69.7 us (0.983)
  waiting for transfers between devices: 18.2 us -> 16.9 us
    ppermute x7, waiting for transfers between devices: 12.1 us -> 10.7 us  [shift(): return lax.ppermute(value, ('seg', 'tile'), ring)]
where the time goes in v5:
time: 69.7 us; the launch traced here: 69.1 us
  starting transfers between devices  20.5 us (29%)
  blocking collectives  20.4 us (29%)
  waiting for transfers between devices  16.9 us (24%)
  Pallas kernels  10.8 us (15%)
    all_to_all x1, blocking collectives, shards(): lax.all_to_all(outgoing.reshape(tiles, CAP, seg_len), 'tile', split_axis=...  20.4 us
    ppermute x7, starting transfers between devices, shift(): return lax.ppermute(value, ('seg', 'tile'), ring)  11.9 us
    pallas_call x7, Pallas kernels, _call(): pl.pallas_call(kernel, out_shape=outputs, in_specs=inputs, out_specs=(pla...  10.8 us
    ppermute x7, waiting for transfers between devices, shift(): return lax.ppermute(value, ('seg', 'tile'), ring)  10.7 us
    all_to_all x1, starting transfers between devices, shards(): lax.all_to_all(want, 'tile', split_axis=0, concat_axis=0, tiled=True)  8.6 us
    all_to_all x1, waiting for transfers between devices, shards(): lax.all_to_all(want, 'tile', split_axis=0, concat_axis=0, tiled=True)  6.12 us
  transfers between devices with their start and end apart: 8, of which 6 were waited for; matrix products, arithmetic and copies ran while one was open for 0% of the time, Pallas kernels for 2%

profile of v5, /device:TPU:1, one launch (start us, length us, event | category | flops | bytes accessed | tf_op | source)
XLA Modules:
  0.0 69.1 jit_solution(13532955742342279247)
XLA Ops:
  0.0 0.0 copy-start
  0.0 1.9 %request.1 = (bf16[32,8,128]{2,1,0:T(8,128)(2,1)}, f32[32,128]{1,0:T(8,128)S(1)}, s32[2,512]{1,0:T(2,128)S(1)}) custom-call(s32[2,256]{1,0:T(2,128)} %pair_hbm.1, s32[32,128]{1,0:T(8,128)} %bitcast.11), custom_call_target="tpu_custom_call" | custom-call | tf_op jit(solution)/shard_map/request/pallas_call | solution.py:399
  1.9 8.6 %all-to-all-start = ((bf16[32,8,128]{2,1,0:T(8,128)(2,1)}), bf16[32,8,128]{2,1,0:T(8,128)(2,1)S(1)}, u32[]{:S(2)}, u32[]{:S(2)}) async-start(bf16[32,8,128]{2,1,0:T(8,128)(2,1)} %get-tuple-element.23), calls=%async_computation | async-start | bytes 131072 | tf_op jit(solution)/shard_map/all_to_all | solution.py:440
  10.5 1.2 %position.1 = (bf16[512,256]{1,0:T(8,128)(2,1)S(1)}, bf16[16,128,256]{2,1,0:T(8,128)(2,1)S(1)}) custom-call(f32[32,128]{1,0:T(8,128)S(1)} %get-tuple-element.24.slot_ref, s32[2,512]{1,0:T(2,128)S(1)} %get-tuple-element.25.where_ref, bf16[16,128,256]{2,1,0:T(8,128)(2,1)} %constant.4.clone.table_hbm), custom_call_target="tpu_custom_call" | custom-call | tf_op jit(solution)/shard_map/position/pallas_call | solution.py:399
  11.8 6.1 %all-to-all-done = bf16[32,8,128]{2,1,0:T(8,128)(2,1)S(1)} async-done(((bf16[32,8,128]{2,1,0:T(8,128)(2,1)}), bf16[32,8,128]{2,1,0:T(8,128)(2,1)S(1)}, u32[]{:S(2)}, u32[]{:S(2)}) %all-to-all-start) | async-done | bytes 65568 | tf_op jit(solution)/shard_map/all_to_all | solution.py:440
  17.9 0.0 copy-done
  17.9 0.4 fusion
  18.3 20.4 %all_to_all.10 = bf16[32,8,2048]{2,1,0:T(8,128)(2,1)S(1)} all-to-all(bf16[32,8,2048]{2,1,0:T(8,128)(2,1)S(1)} %fusion), channel_id=1, replica_groups=mesh['seg'=8,'tile'=32] {'tile'}, dimensions={0} | all-to-all | bytes 2097152 | tf_op jit(solution)/shard_map/all_to_all | solution.py:454
  38.8 1.7 %transform.1 = (bf16[16,256,256]{2,1,0:T(8,128)(2,1)S(1)}, bf16[16,256,256]{2,1,0:T(8,128)(2,1)S(1)}, bf16[32,128,256]{2,1,0:T(8,128)(2,1)S(1)}) custom-call(bf16[256,2048]{1,0:T(8,128)(2,1)S(1)} %bitcast.10, bf16[32,128,256]{2,1,0:T(8,128)(2,1)} %constant.5.clone.table_hbm), custom_call_target="tpu_custom_call" | custom-call | tf_op jit(solution)/shard_map/transform/pallas_call | solution.py:399
  40.5 5.0 %correlate.1.lags_ref = bf16[8,256,256]{2,1,0:T(8,128)(2,1)S(1)} custom-call(bf16[16,256,256]{2,1,0:T(8,128)(2,1)S(1)} %get-tuple-element.28.yh_ref, bf16[16,256,256]{2,1,0:T(8,128)(2,1)S(1)} %get-tuple-element.29.yl_ref, bf16[32,128,256]{2,1,0:T(8,128)(2,1)S(1)} %get-tuple-element.30.table_ref, bf16[16,128,256]{2,1,0:T(8,128)(2,1)S(1)} %get-tuple-element.31.inverse_ref, ...), custom_call_target="tpu_custom_call" | custom-call | tf_op jit(solution)/shard_map/correlate/pallas_call | solution.py:399
  45.5 0.1 pack.1
  45.6 6.1 %collective-permute-start.2 = (bf16[256,256]{1,0:T(8,128)(2,1)S(1)}, bf16[256,256]{1,0:T(8,128)(2,1)S(1)}, u32[]{:S(2)}, u32[]{:S(2)}) collective-permute-start(bf16[256,256]{1,0:T(8,128)(2,1)S(1)} %get-tuple-element.36), channel_id=1, source_target_pairs={{0,64},{1,193},{2,66},{3,195},{4,68},{5,197},{6,70},{7,199},{8,72}... | collective-permute-start | bytes 393224 | tf_op jit(solution)/shard_map/ppermute | solution.py:496
  51.6 0.7 %collective-permute-start.3 = (bf16[256,256]{1,0:T(8,128)(2,1)S(1)}, bf16[256,256]{1,0:T(8,128)(2,1)S(1)}, u32[]{:S(2)}, u32[]{:S(2)}) collective-permute-start(bf16[256,256]{1,0:T(8,128)(2,1)S(1)} %get-tuple-element.37), channel_id=1, source_target_pairs={{0,32},{1,225},{2,34},{3,227},{4,36},{5,229},{6,38},{7,231},{8,40}... | collective-permute-start | bytes 393224 | tf_op jit(solution)/shard_map/ppermute | solution.py:496
  52.4 0.7 %collective-permute-start.4 = (bf16[256,256]{1,0:T(8,128)(2,1)S(1)}, bf16[256,256]{1,0:T(8,128)(2,1)S(1)}, u32[]{:S(2)}, u32[]{:S(2)}) collective-permute-start(bf16[256,256]{1,0:T(8,128)(2,1)S(1)} %get-tuple-element.38), channel_id=1, source_target_pairs={{0,224},{1,33},{2,226},{3,35},{4,228},{5,37},{6,230},{7,39},{8,232... | collective-permute-start | bytes 393224 | tf_op jit(solution)/shard_map/ppermute | solution.py:496
  53.1 1.9 %collective-permute-start = (bf16[256,256]{1,0:T(8,128)(2,1)S(1)}, bf16[256,256]{1,0:T(8,128)(2,1)S(1)}, u32[]{:S(2)}, u32[]{:S(2)}) collective-permute-start(bf16[256,256]{1,0:T(8,128)(2,1)S(1)} %get-tuple-element.34), channel_id=1, source_target_pairs={{0,32},{1,225},{2,34},{3,227},{4,36},{5,229},{6,38},{7,231},{8,40}... | collective-permute-start | bytes 393224 | tf_op jit(solution)/shard_map/ppermute | solution.py:496
  55.1 0.0 collective-permute-start.1
  55.1 0.8 %collective-permute-done.2.far_ref = bf16[256,256]{1,0:T(8,128)(2,1)S(1)} collective-permute-done((bf16[256,256]{1,0:T(8,128)(2,1)S(1)}, bf16[256,256]{1,0:T(8,128)(2,1)S(1)}, u32[]{:S(2)}, u32[]{:S(2)}) %collective-permute-start.2) | collective-permute-done | bytes 131104 | tf_op jit(solution)/shard_map/ppermute | solution.py:496
  55.8 2.8 %collective-permute-done.3.ahead_ref = bf16[256,256]{1,0:T(8,128)(2,1)S(1)} collective-permute-done((bf16[256,256]{1,0:T(8,128)(2,1)S(1)}, bf16[256,256]{1,0:T(8,128)(2,1)S(1)}, u32[]{:S(2)}, u32[]{:S(2)}) %collective-permute-start.3) | collective-permute-done | bytes 131104 | tf_op jit(solution)/shard_map/ppermute | solution.py:496
  58.6 0.5 collective-permute-done.4.back_ref
  59.2 0.1 relay.1
  59.3 1.5 %collective-permute-start.5 = (bf16[256,256]{1,0:T(8,128)(2,1)S(1)}, bf16[256,256]{1,0:T(8,128)(2,1)S(1)}, u32[]{:S(2)}, u32[]{:S(2)}) collective-permute-start(bf16[256,256]{1,0:T(8,128)(2,1)S(1)} %get-tuple-element.39), channel_id=1, source_target_pairs={{0,64},{1,193},{2,66},{3,195},{4,68},{5,197},{6,70},{7,199},{8,72}... | collective-permute-start | bytes 393224 | tf_op jit(solution)/shard_map/ppermute | solution.py:496
  60.8 0.9 %collective-permute-start.6 = (bf16[256,256]{1,0:T(8,128)(2,1)S(1)}, bf16[256,256]{1,0:T(8,128)(2,1)S(1)}, u32[]{:S(2)}, u32[]{:S(2)}) collective-permute-start(bf16[256,256]{1,0:T(8,128)(2,1)S(1)} %get-tuple-element.40), channel_id=1, source_target_pairs={{0,192},{1,65},{2,194},{3,67},{4,196},{5,69},{6,198},{7,71},{8,200... | collective-permute-start | bytes 393224 | tf_op jit(solution)/shard_map/ppermute | solution.py:496
  61.7 0.0 collective-permute-done.ahead_ref
  61.7 0.0 collective-permute-done.1.back_ref
  61.7 3.7 %collective-permute-done.5.ahead2_ref = bf16[256,256]{1,0:T(8,128)(2,1)S(1)} collective-permute-done((bf16[256,256]{1,0:T(8,128)(2,1)S(1)}, bf16[256,256]{1,0:T(8,128)(2,1)S(1)}, u32[]{:S(2)}, u32[]{:S(2)}) %collective-permute-start.5) | collective-permute-done | bytes 131104 | tf_op jit(solution)/shard_map/ppermute | solution.py:496
  65.4 2.9 %collective-permute-done.6.back2_ref = bf16[256,256]{1,0:T(8,128)(2,1)S(1)} collective-permute-done((bf16[256,256]{1,0:T(8,128)(2,1)S(1)}, bf16[256,256]{1,0:T(8,128)(2,1)S(1)}, u32[]{:S(2)}, u32[]{:S(2)}) %collective-permute-start.6) | collective-permute-done | bytes 131104 | tf_op jit(solution)/shard_map/ppermute | solution.py:496
  68.3 0.8 %stack.1 = bf16[256,256]{1,0:T(8,128)(2,1)} custom-call(bf16[3,256,256]{2,1,0:T(8,128)(2,1)S(1)} %get-tuple-element.33.keep_ref, bf16[256,256]{1,0:T(8,128)(2,1)S(1)} %collective-permute-done.ahead_ref, bf16[256,256]{1,0:T(8,128)(2,1)S(1)} %collective-permute-done.1.back_ref, bf16[256,256]{1,0:T(8,128)(2,1)S(1)} %collective-permute-done.5.ahead2_ref, ...), custom_call_target="tpu_custom_call" | custom-call | tf_op jit(solution)/shard_map/stack/pallas_call | solution.py:399
Async XLA Ops:
  0.0 17.9 %copy-start = (bf16[1,128,2048]{2,1,0:T(8,128)(2,1)S(1)}, bf16[1,128,2048]{2,1,0:T(8,128)(2,1)}, u32[]{:S(2)}) copy-start(bf16[1,128,2048]{2,1,0:T(8,128)(2,1)} %param.5) | copy-start | bytes 1572868
  1.9 16.0 %all-to-all-start = ((bf16[32,8,128]{2,1,0:T(8,128)(2,1)}), bf16[32,8,128]{2,1,0:T(8,128)(2,1)S(1)}, u32[]{:S(2)}, u32[]{:S(2)}) async-start(bf16[32,8,128]{2,1,0:T(8,128)(2,1)} %get-tuple-element.23), calls=%async_computation | async-start | bytes 131072 | tf_op jit(solution)/shard_map/all_to_all | solution.py:440
  45.6 10.3 %collective-permute-start.2 = (bf16[256,256]{1,0:T(8,128)(2,1)S(1)}, bf16[256,256]{1,0:T(8,128)(2,1)S(1)}, u32[]{:S(2)}, u32[]{:S(2)}) collective-permute-start(bf16[256,256]{1,0:T(8,128)(2,1)S(1)} %get-tuple-element.36), channel_id=1, source_target_pairs={{0,64},{1,193},{2,66},{3,195},{4,68},{5,197},{6,70},{7,199},{8,72}... | collective-permute-start | bytes 393224 | tf_op jit(solution)/shard_map/ppermute | solution.py:496
  51.6 7.0 %collective-permute-start.3 = (bf16[256,256]{1,0:T(8,128)(2,1)S(1)}, bf16[256,256]{1,0:T(8,128)(2,1)S(1)}, u32[]{:S(2)}, u32[]{:S(2)}) collective-permute-start(bf16[256,256]{1,0:T(8,128)(2,1)S(1)} %get-tuple-element.37), channel_id=1, source_target_pairs={{0,32},{1,225},{2,34},{3,227},{4,36},{5,229},{6,38},{7,231},{8,40}... | collective-permute-start | bytes 393224 | tf_op jit(solution)/shard_map/ppermute | solution.py:496
  52.4 6.8 %collective-permute-start.4 = (bf16[256,256]{1,0:T(8,128)(2,1)S(1)}, bf16[256,256]{1,0:T(8,128)(2,1)S(1)}, u32[]{:S(2)}, u32[]{:S(2)}) collective-permute-start(bf16[256,256]{1,0:T(8,128)(2,1)S(1)} %get-tuple-element.38), channel_id=1, source_target_pairs={{0,224},{1,33},{2,226},{3,35},{4,228},{5,37},{6,230},{7,39},{8,232... | collective-permute-start | bytes 393224 | tf_op jit(solution)/shard_map/ppermute | solution.py:496
  53.1 8.6 %collective-permute-start = (bf16[256,256]{1,0:T(8,128)(2,1)S(1)}, bf16[256,256]{1,0:T(8,128)(2,1)S(1)}, u32[]{:S(2)}, u32[]{:S(2)}) collective-permute-start(bf16[256,256]{1,0:T(8,128)(2,1)S(1)} %get-tuple-element.34), channel_id=1, source_target_pairs={{0,32},{1,225},{2,34},{3,227},{4,36},{5,229},{6,38},{7,231},{8,40}... | collective-permute-start | bytes 393224 | tf_op jit(solution)/shard_map/ppermute | solution.py:496
  55.1 6.6 %collective-permute-start.1 = (bf16[256,256]{1,0:T(8,128)(2,1)S(1)}, bf16[256,256]{1,0:T(8,128)(2,1)S(1)}, u32[]{:S(2)}, u32[]{:S(2)}) collective-permute-start(bf16[256,256]{1,0:T(8,128)(2,1)S(1)} %get-tuple-element.35), channel_id=1, source_target_pairs={{0,224},{1,33},{2,226},{3,35},{4,228},{5,37},{6,230},{7,39},{8,232... | collective-permute-start | bytes 393224 | tf_op jit(solution)/shard_map/ppermute | solution.py:496
  59.3 6.2 %collective-permute-start.5 = (bf16[256,256]{1,0:T(8,128)(2,1)S(1)}, bf16[256,256]{1,0:T(8,128)(2,1)S(1)}, u32[]{:S(2)}, u32[]{:S(2)}) collective-permute-start(bf16[256,256]{1,0:T(8,128)(2,1)S(1)} %get-tuple-element.39), channel_id=1, source_target_pairs={{0,64},{1,193},{2,66},{3,195},{4,68},{5,197},{6,70},{7,199},{8,72}... | collective-permute-start | bytes 393224 | tf_op jit(solution)/shard_map/ppermute | solution.py:496
  60.8 7.5 %collective-permute-start.6 = (bf16[256,256]{1,0:T(8,128)(2,1)S(1)}, bf16[256,256]{1,0:T(8,128)(2,1)S(1)}, u32[]{:S(2)}, u32[]{:S(2)}) collective-permute-start(bf16[256,256]{1,0:T(8,128)(2,1)S(1)} %get-tuple-element.40), channel_id=1, source_target_pairs={{0,192},{1,65},{2,194},{3,67},{4,196},{5,69},{6,198},{7,71},{8,200... | collective-permute-start | bytes 393224 | tf_op jit(solution)/shard_map/ppermute | solution.py:496

commit v6 on v5

--- a/solution.py
+++ b/solution.py
@@ -226,14 +226,18 @@
     return (lax.broadcasted_iota(jnp.int32, (rows, index.shape[1]), 0) == index).astype(F32)
 
 
-def request_kernel(holders, pair_hbm, home_hbm, want_ref, slot_ref, where_ref, pair_ref, home_ref, sems):
+def request_kernel(
+    holders, pair_hbm, home_hbm, table_hbm, want_ref, pick_ref, table_ref, pair_ref, home_ref, sems
+):
     copies = [
-        pltpu.make_async_copy(pair_hbm, pair_ref, sems.at[0]),
-        pltpu.make_async_copy(home_hbm, home_ref, sems.at[1]),
+        pltpu.make_async_copy(src, dst, sems.at[i])
+        for i, (src, dst) in enumerate(
+            ((pair_hbm, pair_ref), (home_hbm, home_ref), (table_hbm, table_ref))
+        )
     ]
     for copy in copies:
         copy.start()
-    for copy in copies:
+    for copy in copies[:2]:
         copy.wait()
     pairs = jnp.concatenate([pair_ref[0:1, :], pair_ref[1:2, :]], axis=1)
     home = home_ref[...]
@@ -243,33 +247,22 @@
     columns = _dot(stored, low)
     owner = jnp.sum(columns[: home.shape[0]] * high, axis=0, keepdims=True).astype(jnp.int32)
     place = jnp.sum(columns[home.shape[0] :] * high, axis=0, keepdims=True).astype(jnp.int32)
-    where_ref[0:1, :] = owner
-    where_ref[1:2, :] = place
     owners = _one_hot(owner, holders).astype(BF16)
     places = _one_hot(place, LANES).astype(BF16)
     needed = jnp.minimum(_dot(owners, places, ((1,), (1,))), 1.0)
     row = lax.broadcasted_iota(jnp.int32, (LANES, LANES), 0)
     col = lax.broadcasted_iota(jnp.int32, (LANES, LANES), 1)
     slot = _dot(needed.astype(BF16), (row < col).astype(F32).astype(BF16))
-    slot_ref[...] = slot
     marked = jnp.where(needed > 0.0, slot, -1.0)
     slots = lax.broadcasted_iota(jnp.int32, (CAP, LANES), 0).astype(F32)
     for holder in range(holders):
         want_ref[holder] = (marked[holder : holder + 1, :] == slots).astype(F32).astype(BF16)
-
-
-def position_kernel(slot_ref, where_ref, table_hbm, pick_ref, table_ref, sem):
-    copy = pltpu.make_async_copy(table_hbm, table_ref, sem.at[0])
-    copy.start()
-    owner = where_ref[0:1, :]
-    place = where_ref[1:2, :]
-    holders = slot_ref.shape[0]
-    slot = jnp.minimum(slot_ref[...], CAP - 1.0)
-    of_pair = _dot(slot.astype(BF16), _one_hot(owner, holders).astype(BF16), ((0,), (0,)))
+    slot = jnp.minimum(slot, CAP - 1.0)
+    of_pair = _dot(slot.astype(BF16), owners, ((0,), (0,)))
     slot = jnp.sum(of_pair * _one_hot(place, LANES), axis=0, keepdims=True)
     position = owner * CAP + slot.astype(jnp.int32)
     pick_ref[...] = _one_hot(position, holders * CAP).T.astype(BF16)
-    copy.wait()
+    copies[2].wait()
 
 
 ROWS = 16
@@ -421,35 +414,26 @@
     lags = NLAG // segments
     shape = jax.ShapeDtypeStruct
     home = sensor_home.reshape(-1, LANES)
-    want, slot, where = _call(
+    forward, inverse = _upper_halves(_forward_tables(), _inverse_tables(segments))
+    forward = np.stack(_split(forward), axis=1).reshape(2 * HALF, LANES, 2 * LANES)
+    inverse = jnp.asarray(inverse.astype(BF16))
+    want, pick, inverse = _call(
         functools.partial(request_kernel, tiles),
         "request",
-        [ANY] * 2,
+        [ANY] * 3,
         (
             pltpu.VMEM((tiles, CAP, sens_dev), BF16),
-            pltpu.VMEM((tiles, sens_dev), F32),
-            pltpu.VMEM((2, 2 * pair_dev), jnp.int32),
+            pltpu.VMEM((2 * pair_dev, rows), BF16),
+            pltpu.VMEM(inverse.shape, BF16),
         ),
-        (_in_hbm(pair_list), _in_hbm(home)),
+        (_in_hbm(pair_list), _in_hbm(home), _in_hbm(inverse)),
         [
             pltpu.VMEM(pair_list.shape, jnp.int32),
             pltpu.VMEM(home.shape, jnp.int32),
-            pltpu.SemaphoreType.DMA((2,)),
+            pltpu.SemaphoreType.DMA((3,)),
         ],
     )
     asked = lax.all_to_all(want, "tile", split_axis=0, concat_axis=0, tiled=True)
-    forward, inverse = _upper_halves(_forward_tables(), _inverse_tables(segments))
-    forward = np.stack(_split(forward), axis=1).reshape(2 * HALF, LANES, 2 * LANES)
-    inverse = jnp.asarray(inverse.astype(BF16))
-    pick, inverse = _call(
-        position_kernel,
-        "position",
-        [VMEM] * 2 + [ANY],
-        (pltpu.VMEM((2 * pair_dev, rows), BF16), pltpu.VMEM(inverse.shape, BF16)),
-        (slot, where, _in_hbm(inverse)),
-        [pltpu.SemaphoreType.DMA((1,))],
-    )
-    asked, pick = lax.optimization_barrier((asked, pick))
     outgoing = jnp.dot(asked.reshape(rows, sens_dev), local, preferred_element_type=F32).astype(BF16)
     arrived = lax.all_to_all(
         outgoing.reshape(tiles, CAP, seg_len), "tile", split_axis=0, concat_axis=0, tiled=True

time: 69.7 us -> 70.2 us (level)
  blocking collectives: 20.4 us -> 36.2 us
  starting transfers between devices: 20.5 us -> 11.9 us
  waiting for transfers between devices: 16.9 us -> 12.1 us
  Pallas kernels: 10.8 us -> 9.35 us
    all_to_all x0 -> x1, blocking collectives: none -> 15.8 us  [shards(): lax.all_to_all(want, 'tile', split_axis=0, concat_axis=0, tiled=True)]
    all_to_all x1 -> x0, starting transfers between devices: 8.6 us -> none  [shards(): lax.all_to_all(want, 'tile', split_axis=0, concat_axis=0, tiled=True)]
    all_to_all x1 -> x0, waiting for transfers between devices: 6.12 us -> none  [shards(): lax.all_to_all(want, 'tile', split_axis=0, concat_axis=0, tiled=True)]
    pallas_call x7 -> x6, Pallas kernels: 10.8 us -> 9.35 us  [_call(): pl.pallas_call(kernel, out_shape=outputs, in_specs=inputs, out_specs=(pla...]
    ppermute x7, waiting for transfers between devices: 10.7 us -> 12.1 us  [shift(): return lax.ppermute(value, ('seg', 'tile'), ring)]
  transfers between devices with their start and end apart: 8 -> 7, of which waited for: 6 -> 5; matrix products, arithmetic and copies ran while one was open for 0% -> 0% of each run, Pallas kernels for 2% -> 0%
where the time goes in v6:
time: 70.2 us; the launch traced here: 70 us
  blocking collectives  36.2 us (52%)
  waiting for transfers between devices  12.1 us (17%)
  starting transfers between devices  11.9 us (17%)
  Pallas kernels  9.35 us (13%)
    all_to_all x1, blocking collectives, shards(): lax.all_to_all(outgoing.reshape(tiles, CAP, seg_len), 'tile', split_axis=...  20.4 us
    all_to_all x1, blocking collectives, shards(): lax.all_to_all(want, 'tile', split_axis=0, concat_axis=0, tiled=True)  15.8 us
    ppermute x7, waiting for transfers between devices, shift(): return lax.ppermute(value, ('seg', 'tile'), ring)  12.1 us
    ppermute x7, starting transfers between devices, shift(): return lax.ppermute(value, ('seg', 'tile'), ring)  11.9 us
    pallas_call x6, Pallas kernels, _call(): pl.pallas_call(kernel, out_shape=outputs, in_specs=inputs, out_specs=(pla...  9.35 us
  transfers between devices with their start and end apart: 7, of which 5 were waited for; matrix products, arithmetic and copies ran while one was open for 0% of the time, Pallas kernels for 0%

profile of v6, /device:TPU:1, one launch (start us, length us, event | category | flops | bytes accessed | tf_op | source)
XLA Modules:
  0.0 70.0 jit_solution(3321648563097566635)
XLA Ops:
  0.0 0.0 copy-start
  0.0 1.7 %request.1 = (bf16[32,8,128]{2,1,0:T(8,128)(2,1)S(1)}, bf16[512,256]{1,0:T(8,128)(2,1)S(1)}, bf16[16,128,256]{2,1,0:T(8,128)(2,1)S(1)}) custom-call(s32[2,256]{1,0:T(2,128)} %pair_hbm.1, s32[32,128]{1,0:T(8,128)} %bitcast.11, bf16[16,128,256]{2,1,0:T(8,128)(2,1)} %constant.4.clone.table_hbm), custom_call_target="tpu_custom_call" | custom-call | tf_op jit(solution)/shard_map/request/pallas_call | solution.py:392
  1.7 15.8 %all_to_all.10 = bf16[32,8,128]{2,1,0:T(8,128)(2,1)S(1)} all-to-all(bf16[32,8,128]{2,1,0:T(8,128)(2,1)S(1)} %get-tuple-element.19), channel_id=1, replica_groups=mesh['seg'=8,'tile'=32] {'tile'}, dimensions={0} | all-to-all | bytes 131072 | tf_op jit(solution)/shard_map/all_to_all | solution.py:436
  17.5 0.0 copy-done
  17.5 0.4 fusion
  17.9 20.4 %all_to_all.11 = bf16[32,8,2048]{2,1,0:T(8,128)(2,1)S(1)} all-to-all(bf16[32,8,2048]{2,1,0:T(8,128)(2,1)S(1)} %fusion), channel_id=1, replica_groups=mesh['seg'=8,'tile'=32] {'tile'}, dimensions={0} | all-to-all | bytes 2097152 | tf_op jit(solution)/shard_map/all_to_all | solution.py:438
  38.3 1.7 %transform.1 = (bf16[16,256,256]{2,1,0:T(8,128)(2,1)S(1)}, bf16[16,256,256]{2,1,0:T(8,128)(2,1)S(1)}, bf16[32,128,256]{2,1,0:T(8,128)(2,1)S(1)}) custom-call(bf16[256,2048]{1,0:T(8,128)(2,1)S(1)} %bitcast.10, bf16[32,128,256]{2,1,0:T(8,128)(2,1)} %constant.5.clone.table_hbm), custom_call_target="tpu_custom_call" | custom-call | tf_op jit(solution)/shard_map/transform/pallas_call | solution.py:392
  40.0 5.0 %correlate.1.lags_ref = bf16[8,256,256]{2,1,0:T(8,128)(2,1)S(1)} custom-call(bf16[16,256,256]{2,1,0:T(8,128)(2,1)S(1)} %get-tuple-element.20.yh_ref, bf16[16,256,256]{2,1,0:T(8,128)(2,1)S(1)} %get-tuple-element.21.yl_ref, bf16[32,128,256]{2,1,0:T(8,128)(2,1)S(1)} %get-tuple-element.22.table_ref, bf16[16,128,256]{2,1,0:T(8,128)(2,1)S(1)} %get-tuple-element.23.inverse_ref, ...), custom_call_target="tpu_custom_call" | custom-call | tf_op jit(solution)/shard_map/correlate/pallas_call | solution.py:392
  45.0 0.1 pack.1
  45.1 6.1 %collective-permute-start.2 = (bf16[256,256]{1,0:T(8,128)(2,1)S(1)}, bf16[256,256]{1,0:T(8,128)(2,1)S(1)}, u32[]{:S(2)}, u32[]{:S(2)}) collective-permute-start(bf16[256,256]{1,0:T(8,128)(2,1)S(1)} %get-tuple-element.28), channel_id=1, source_target_pairs={{0,64},{1,193},{2,66},{3,195},{4,68},{5,197},{6,70},{7,199},{8,72}... | collective-permute-start | bytes 393224 | tf_op jit(solution)/shard_map/ppermute | solution.py:480
  51.2 0.7 %collective-permute-start.3 = (bf16[256,256]{1,0:T(8,128)(2,1)S(1)}, bf16[256,256]{1,0:T(8,128)(2,1)S(1)}, u32[]{:S(2)}, u32[]{:S(2)}) collective-permute-start(bf16[256,256]{1,0:T(8,128)(2,1)S(1)} %get-tuple-element.29), channel_id=1, source_target_pairs={{0,32},{1,225},{2,34},{3,227},{4,36},{5,229},{6,38},{7,231},{8,40}... | collective-permute-start | bytes 393224 | tf_op jit(solution)/shard_map/ppermute | solution.py:480
  51.9 0.7 %collective-permute-start.4 = (bf16[256,256]{1,0:T(8,128)(2,1)S(1)}, bf16[256,256]{1,0:T(8,128)(2,1)S(1)}, u32[]{:S(2)}, u32[]{:S(2)}) collective-permute-start(bf16[256,256]{1,0:T(8,128)(2,1)S(1)} %get-tuple-element.30), channel_id=1, source_target_pairs={{0,224},{1,33},{2,226},{3,35},{4,228},{5,37},{6,230},{7,39},{8,232... | collective-permute-start | bytes 393224 | tf_op jit(solution)/shard_map/ppermute | solution.py:480
  52.7 1.9 %collective-permute-start = (bf16[256,256]{1,0:T(8,128)(2,1)S(1)}, bf16[256,256]{1,0:T(8,128)(2,1)S(1)}, u32[]{:S(2)}, u32[]{:S(2)}) collective-permute-start(bf16[256,256]{1,0:T(8,128)(2,1)S(1)} %get-tuple-element.26), channel_id=1, source_target_pairs={{0,32},{1,225},{2,34},{3,227},{4,36},{5,229},{6,38},{7,231},{8,40}... | collective-permute-start | bytes 393224 | tf_op jit(solution)/shard_map/ppermute | solution.py:480
  54.6 0.0 collective-permute-start.1
  54.6 0.8 %collective-permute-done.2.far_ref = bf16[256,256]{1,0:T(8,128)(2,1)S(1)} collective-permute-done((bf16[256,256]{1,0:T(8,128)(2,1)S(1)}, bf16[256,256]{1,0:T(8,128)(2,1)S(1)}, u32[]{:S(2)}, u32[]{:S(2)}) %collective-permute-start.2) | collective-permute-done | bytes 131104 | tf_op jit(solution)/shard_map/ppermute | solution.py:480
  55.4 2.8 %collective-permute-done.3.ahead_ref = bf16[256,256]{1,0:T(8,128)(2,1)S(1)} collective-permute-done((bf16[256,256]{1,0:T(8,128)(2,1)S(1)}, bf16[256,256]{1,0:T(8,128)(2,1)S(1)}, u32[]{:S(2)}, u32[]{:S(2)}) %collective-permute-start.3) | collective-permute-done | bytes 131104 | tf_op jit(solution)/shard_map/ppermute | solution.py:480
  58.2 0.5 collective-permute-done.4.back_ref
  58.7 0.1 relay.1
  58.8 1.5 %collective-permute-start.5 = (bf16[256,256]{1,0:T(8,128)(2,1)S(1)}, bf16[256,256]{1,0:T(8,128)(2,1)S(1)}, u32[]{:S(2)}, u32[]{:S(2)}) collective-permute-start(bf16[256,256]{1,0:T(8,128)(2,1)S(1)} %get-tuple-element.31), channel_id=1, source_target_pairs={{0,64},{1,193},{2,66},{3,195},{4,68},{5,197},{6,70},{7,199},{8,72}... | collective-permute-start | bytes 393224 | tf_op jit(solution)/shard_map/ppermute | solution.py:480
  60.3 0.9 %collective-permute-start.6 = (bf16[256,256]{1,0:T(8,128)(2,1)S(1)}, bf16[256,256]{1,0:T(8,128)(2,1)S(1)}, u32[]{:S(2)}, u32[]{:S(2)}) collective-permute-start(bf16[256,256]{1,0:T(8,128)(2,1)S(1)} %get-tuple-element.32), channel_id=1, source_target_pairs={{0,192},{1,65},{2,194},{3,67},{4,196},{5,69},{6,198},{7,71},{8,200... | collective-permute-start | bytes 393224 | tf_op jit(solution)/shard_map/ppermute | solution.py:480
  61.2 0.0 collective-permute-done.ahead_ref
  61.2 0.0 collective-permute-done.1.back_ref
  61.2 3.7 %collective-permute-done.5.ahead2_ref = bf16[256,256]{1,0:T(8,128)(2,1)S(1)} collective-permute-done((bf16[256,256]{1,0:T(8,128)(2,1)S(1)}, bf16[256,256]{1,0:T(8,128)(2,1)S(1)}, u32[]{:S(2)}, u32[]{:S(2)}) %collective-permute-start.5) | collective-permute-done | bytes 131104 | tf_op jit(solution)/shard_map/ppermute | solution.py:480
  65.0 4.2 %collective-permute-done.6.back2_ref = bf16[256,256]{1,0:T(8,128)(2,1)S(1)} collective-permute-done((bf16[256,256]{1,0:T(8,128)(2,1)S(1)}, bf16[256,256]{1,0:T(8,128)(2,1)S(1)}, u32[]{:S(2)}, u32[]{:S(2)}) %collective-permute-start.6) | collective-permute-done | bytes 131104 | tf_op jit(solution)/shard_map/ppermute | solution.py:480
  69.2 0.8 %stack.1 = bf16[256,256]{1,0:T(8,128)(2,1)} custom-call(bf16[3,256,256]{2,1,0:T(8,128)(2,1)S(1)} %get-tuple-element.25.keep_ref, bf16[256,256]{1,0:T(8,128)(2,1)S(1)} %collective-permute-done.ahead_ref, bf16[256,256]{1,0:T(8,128)(2,1)S(1)} %collective-permute-done.1.back_ref, bf16[256,256]{1,0:T(8,128)(2,1)S(1)} %collective-permute-done.5.ahead2_ref, ...), custom_call_target="tpu_custom_call" | custom-call | tf_op jit(solution)/shard_map/stack/pallas_call | solution.py:392
Async XLA Ops:
  0.0 17.5 %copy-start = (bf16[1,128,2048]{2,1,0:T(8,128)(2,1)S(1)}, bf16[1,128,2048]{2,1,0:T(8,128)(2,1)}, u32[]{:S(2)}) copy-start(bf16[1,128,2048]{2,1,0:T(8,128)(2,1)} %param.5) | copy-start | bytes 1572868
  45.1 10.3 %collective-permute-start.2 = (bf16[256,256]{1,0:T(8,128)(2,1)S(1)}, bf16[256,256]{1,0:T(8,128)(2,1)S(1)}, u32[]{:S(2)}, u32[]{:S(2)}) collective-permute-start(bf16[256,256]{1,0:T(8,128)(2,1)S(1)} %get-tuple-element.28), channel_id=1, source_target_pairs={{0,64},{1,193},{2,66},{3,195},{4,68},{5,197},{6,70},{7,199},{8,72}... | collective-permute-start | bytes 393224 | tf_op jit(solution)/shard_map/ppermute | solution.py:480
  51.2 7.0 %collective-permute-start.3 = (bf16[256,256]{1,0:T(8,128)(2,1)S(1)}, bf16[256,256]{1,0:T(8,128)(2,1)S(1)}, u32[]{:S(2)}, u32[]{:S(2)}) collective-permute-start(bf16[256,256]{1,0:T(8,128)(2,1)S(1)} %get-tuple-element.29), channel_id=1, source_target_pairs={{0,32},{1,225},{2,34},{3,227},{4,36},{5,229},{6,38},{7,231},{8,40}... | collective-permute-start | bytes 393224 | tf_op jit(solution)/shard_map/ppermute | solution.py:480
  51.9 6.8 %collective-permute-start.4 = (bf16[256,256]{1,0:T(8,128)(2,1)S(1)}, bf16[256,256]{1,0:T(8,128)(2,1)S(1)}, u32[]{:S(2)}, u32[]{:S(2)}) collective-permute-start(bf16[256,256]{1,0:T(8,128)(2,1)S(1)} %get-tuple-element.30), channel_id=1, source_target_pairs={{0,224},{1,33},{2,226},{3,35},{4,228},{5,37},{6,230},{7,39},{8,232... | collective-permute-start | bytes 393224 | tf_op jit(solution)/shard_map/ppermute | solution.py:480
  52.7 8.6 %collective-permute-start = (bf16[256,256]{1,0:T(8,128)(2,1)S(1)}, bf16[256,256]{1,0:T(8,128)(2,1)S(1)}, u32[]{:S(2)}, u32[]{:S(2)}) collective-permute-start(bf16[256,256]{1,0:T(8,128)(2,1)S(1)} %get-tuple-element.26), channel_id=1, source_target_pairs={{0,32},{1,225},{2,34},{3,227},{4,36},{5,229},{6,38},{7,231},{8,40}... | collective-permute-start | bytes 393224 | tf_op jit(solution)/shard_map/ppermute | solution.py:480
  54.6 6.6 %collective-permute-start.1 = (bf16[256,256]{1,0:T(8,128)(2,1)S(1)}, bf16[256,256]{1,0:T(8,128)(2,1)S(1)}, u32[]{:S(2)}, u32[]{:S(2)}) collective-permute-start(bf16[256,256]{1,0:T(8,128)(2,1)S(1)} %get-tuple-element.27), channel_id=1, source_target_pairs={{0,224},{1,33},{2,226},{3,35},{4,228},{5,37},{6,230},{7,39},{8,232... | collective-permute-start | bytes 393224 | tf_op jit(solution)/shard_map/ppermute | solution.py:480
  58.8 6.2 %collective-permute-start.5 = (bf16[256,256]{1,0:T(8,128)(2,1)S(1)}, bf16[256,256]{1,0:T(8,128)(2,1)S(1)}, u32[]{:S(2)}, u32[]{:S(2)}) collective-permute-start(bf16[256,256]{1,0:T(8,128)(2,1)S(1)} %get-tuple-element.31), channel_id=1, source_target_pairs={{0,64},{1,193},{2,66},{3,195},{4,68},{5,197},{6,70},{7,199},{8,72}... | collective-permute-start | bytes 393224 | tf_op jit(solution)/shard_map/ppermute | solution.py:480
  60.3 8.9 %collective-permute-start.6 = (bf16[256,256]{1,0:T(8,128)(2,1)S(1)}, bf16[256,256]{1,0:T(8,128)(2,1)S(1)}, u32[]{:S(2)}, u32[]{:S(2)}) collective-permute-start(bf16[256,256]{1,0:T(8,128)(2,1)S(1)} %get-tuple-element.32), channel_id=1, source_target_pairs={{0,192},{1,65},{2,194},{3,67},{4,196},{5,69},{6,198},{7,71},{8,200... | collective-permute-start | bytes 393224 | tf_op jit(solution)/shard_map/ppermute | solution.py:480

commit v7 on v6

--- a/solution.py
+++ b/solution.py
@@ -369,7 +369,7 @@
     back_out_ref[...] = back.astype(BF16)
 
 
-def sum_kernel(keep_ref, ahead_ref, back_ref, ahead2_ref, back2_ref, out_hbm, out_ref, sems):
+def sum_kernel(keep_ref, ahead_ref, back_ref, back2_ref, ahead2_ref, out_hbm, out_ref, sems):
     half = out_ref.shape[0] // 2
     copies = []
     for i in range(2):
@@ -494,7 +494,7 @@
         "stack",
         [VMEM] * 5,
         (shape((lags, pair_dev), BF16),),
-        (keep, ahead1, back1, ahead2, back2),
+        (keep, ahead1, back1, back2, ahead2),
         [pltpu.VMEM((lags, pair_dev), BF16), pltpu.SemaphoreType.DMA((2,))],
         place=ANY,
     )

time: 70.2 us -> 69.2 us (0.986)
  waiting for transfers between devices: 12.1 us -> 9.86 us
  starting transfers between devices: 11.9 us -> 13.2 us
    ppermute x7, waiting for transfers between devices: 12.1 us -> 9.86 us  [shift(): return lax.ppermute(value, ('seg', 'tile'), ring)]
    ppermute x7, starting transfers between devices: 11.9 us -> 13.2 us  [shift(): return lax.ppermute(value, ('seg', 'tile'), ring)]
where the time goes in v7:
time: 69.2 us; the launch traced here: 69 us
  blocking collectives  36.2 us (52%)
  starting transfers between devices  13.2 us (19%)
  waiting for transfers between devices  9.86 us (14%)
  Pallas kernels  9.35 us (14%)
    all_to_all x1, blocking collectives, shards(): lax.all_to_all(outgoing.reshape(tiles, CAP, seg_len), 'tile', split_axis=...  20.4 us
    all_to_all x1, blocking collectives, shards(): lax.all_to_all(want, 'tile', split_axis=0, concat_axis=0, tiled=True)  15.8 us
    ppermute x7, starting transfers between devices, shift(): return lax.ppermute(value, ('seg', 'tile'), ring)  13.2 us
    ppermute x7, waiting for transfers between devices, shift(): return lax.ppermute(value, ('seg', 'tile'), ring)  9.86 us
    pallas_call x6, Pallas kernels, _call(): pl.pallas_call(kernel, out_shape=outputs, in_specs=inputs, out_specs=(pla...  9.35 us
  transfers between devices with their start and end apart: 7, of which 5 were waited for; matrix products, arithmetic and copies ran while one was open for 0% of the time, Pallas kernels for 0%

profile of v7, /device:TPU:1, one launch (start us, length us, event | category | flops | bytes accessed | tf_op | source)
XLA Modules:
  0.0 69.0 jit_solution(7464125549885272692)
XLA Ops:
  0.0 0.0 copy-start
  0.0 1.7 %request.1 = (bf16[32,8,128]{2,1,0:T(8,128)(2,1)S(1)}, bf16[512,256]{1,0:T(8,128)(2,1)S(1)}, bf16[16,128,256]{2,1,0:T(8,128)(2,1)S(1)}) custom-call(s32[2,256]{1,0:T(2,128)} %pair_hbm.1, s32[32,128]{1,0:T(8,128)} %bitcast.11, bf16[16,128,256]{2,1,0:T(8,128)(2,1)} %constant.4.clone.table_hbm), custom_call_target="tpu_custom_call" | custom-call | tf_op jit(solution)/shard_map/request/pallas_call | solution.py:392
  1.7 15.8 %all_to_all.10 = bf16[32,8,128]{2,1,0:T(8,128)(2,1)S(1)} all-to-all(bf16[32,8,128]{2,1,0:T(8,128)(2,1)S(1)} %get-tuple-element.19), channel_id=1, replica_groups=mesh['seg'=8,'tile'=32] {'tile'}, dimensions={0} | all-to-all | bytes 131072 | tf_op jit(solution)/shard_map/all_to_all | solution.py:436
  17.5 0.0 copy-done
  17.5 0.4 fusion
  17.9 20.4 %all_to_all.11 = bf16[32,8,2048]{2,1,0:T(8,128)(2,1)S(1)} all-to-all(bf16[32,8,2048]{2,1,0:T(8,128)(2,1)S(1)} %fusion), channel_id=1, replica_groups=mesh['seg'=8,'tile'=32] {'tile'}, dimensions={0} | all-to-all | bytes 2097152 | tf_op jit(solution)/shard_map/all_to_all | solution.py:438
  38.3 1.7 %transform.1 = (bf16[16,256,256]{2,1,0:T(8,128)(2,1)S(1)}, bf16[16,256,256]{2,1,0:T(8,128)(2,1)S(1)}, bf16[32,128,256]{2,1,0:T(8,128)(2,1)S(1)}) custom-call(bf16[256,2048]{1,0:T(8,128)(2,1)S(1)} %bitcast.10, bf16[32,128,256]{2,1,0:T(8,128)(2,1)} %constant.5.clone.table_hbm), custom_call_target="tpu_custom_call" | custom-call | tf_op jit(solution)/shard_map/transform/pallas_call | solution.py:392
  40.0 5.0 %correlate.1.lags_ref = bf16[8,256,256]{2,1,0:T(8,128)(2,1)S(1)} custom-call(bf16[16,256,256]{2,1,0:T(8,128)(2,1)S(1)} %get-tuple-element.20.yh_ref, bf16[16,256,256]{2,1,0:T(8,128)(2,1)S(1)} %get-tuple-element.21.yl_ref, bf16[32,128,256]{2,1,0:T(8,128)(2,1)S(1)} %get-tuple-element.22.table_ref, bf16[16,128,256]{2,1,0:T(8,128)(2,1)S(1)} %get-tuple-element.23.inverse_ref, ...), custom_call_target="tpu_custom_call" | custom-call | tf_op jit(solution)/shard_map/correlate/pallas_call | solution.py:392
  45.0 0.1 pack.1
  45.1 6.1 %collective-permute-start.2 = (bf16[256,256]{1,0:T(8,128)(2,1)S(1)}, bf16[256,256]{1,0:T(8,128)(2,1)S(1)}, u32[]{:S(2)}, u32[]{:S(2)}) collective-permute-start(bf16[256,256]{1,0:T(8,128)(2,1)S(1)} %get-tuple-element.28), channel_id=1, source_target_pairs={{0,64},{1,193},{2,66},{3,195},{4,68},{5,197},{6,70},{7,199},{8,72}... | collective-permute-start | bytes 393224 | tf_op jit(solution)/shard_map/ppermute | solution.py:480
  51.2 0.7 %collective-permute-start.3 = (bf16[256,256]{1,0:T(8,128)(2,1)S(1)}, bf16[256,256]{1,0:T(8,128)(2,1)S(1)}, u32[]{:S(2)}, u32[]{:S(2)}) collective-permute-start(bf16[256,256]{1,0:T(8,128)(2,1)S(1)} %get-tuple-element.29), channel_id=1, source_target_pairs={{0,32},{1,225},{2,34},{3,227},{4,36},{5,229},{6,38},{7,231},{8,40}... | collective-permute-start | bytes 393224 | tf_op jit(solution)/shard_map/ppermute | solution.py:480
  51.9 0.7 %collective-permute-start.4 = (bf16[256,256]{1,0:T(8,128)(2,1)S(1)}, bf16[256,256]{1,0:T(8,128)(2,1)S(1)}, u32[]{:S(2)}, u32[]{:S(2)}) collective-permute-start(bf16[256,256]{1,0:T(8,128)(2,1)S(1)} %get-tuple-element.30), channel_id=1, source_target_pairs={{0,224},{1,33},{2,226},{3,35},{4,228},{5,37},{6,230},{7,39},{8,232... | collective-permute-start | bytes 393224 | tf_op jit(solution)/shard_map/ppermute | solution.py:480
  52.7 1.9 %collective-permute-start = (bf16[256,256]{1,0:T(8,128)(2,1)S(1)}, bf16[256,256]{1,0:T(8,128)(2,1)S(1)}, u32[]{:S(2)}, u32[]{:S(2)}) collective-permute-start(bf16[256,256]{1,0:T(8,128)(2,1)S(1)} %get-tuple-element.26), channel_id=1, source_target_pairs={{0,32},{1,225},{2,34},{3,227},{4,36},{5,229},{6,38},{7,231},{8,40}... | collective-permute-start | bytes 393224 | tf_op jit(solution)/shard_map/ppermute | solution.py:480
  54.6 0.0 collective-permute-start.1
  54.6 0.8 %collective-permute-done.2.far_ref = bf16[256,256]{1,0:T(8,128)(2,1)S(1)} collective-permute-done((bf16[256,256]{1,0:T(8,128)(2,1)S(1)}, bf16[256,256]{1,0:T(8,128)(2,1)S(1)}, u32[]{:S(2)}, u32[]{:S(2)}) %collective-permute-start.2) | collective-permute-done | bytes 131104 | tf_op jit(solution)/shard_map/ppermute | solution.py:480
  55.4 2.8 %collective-permute-done.3.ahead_ref = bf16[256,256]{1,0:T(8,128)(2,1)S(1)} collective-permute-done((bf16[256,256]{1,0:T(8,128)(2,1)S(1)}, bf16[256,256]{1,0:T(8,128)(2,1)S(1)}, u32[]{:S(2)}, u32[]{:S(2)}) %collective-permute-start.3) | collective-permute-done | bytes 131104 | tf_op jit(solution)/shard_map/ppermute | solution.py:480
  58.2 0.5 collective-permute-done.4.back_ref
  58.7 0.1 relay.1
  58.8 0.1 collective-permute-start.5
  58.9 3.6 %collective-permute-start.6 = (bf16[256,256]{1,0:T(8,128)(2,1)S(1)}, bf16[256,256]{1,0:T(8,128)(2,1)S(1)}, u32[]{:S(2)}, u32[]{:S(2)}) collective-permute-start(bf16[256,256]{1,0:T(8,128)(2,1)S(1)} %get-tuple-element.32), channel_id=1, source_target_pairs={{0,64},{1,193},{2,66},{3,195},{4,68},{5,197},{6,70},{7,199},{8,72}... | collective-permute-start | bytes 393224 | tf_op jit(solution)/shard_map/ppermute | solution.py:480
  62.4 0.0 collective-permute-done.ahead_ref
  62.4 0.0 collective-permute-done.1.back_ref
  62.4 2.4 %collective-permute-done.5.back2_ref = bf16[256,256]{1,0:T(8,128)(2,1)S(1)} collective-permute-done((bf16[256,256]{1,0:T(8,128)(2,1)S(1)}, bf16[256,256]{1,0:T(8,128)(2,1)S(1)}, u32[]{:S(2)}, u32[]{:S(2)}) %collective-permute-start.5) | collective-permute-done | bytes 131104 | tf_op jit(solution)/shard_map/ppermute | solution.py:480
  64.9 3.3 %collective-permute-done.6.ahead2_ref = bf16[256,256]{1,0:T(8,128)(2,1)S(1)} collective-permute-done((bf16[256,256]{1,0:T(8,128)(2,1)S(1)}, bf16[256,256]{1,0:T(8,128)(2,1)S(1)}, u32[]{:S(2)}, u32[]{:S(2)}) %collective-permute-start.6) | collective-permute-done | bytes 131104 | tf_op jit(solution)/shard_map/ppermute | solution.py:480
  68.2 0.8 %stack.1 = bf16[256,256]{1,0:T(8,128)(2,1)} custom-call(bf16[3,256,256]{2,1,0:T(8,128)(2,1)S(1)} %get-tuple-element.25.keep_ref, bf16[256,256]{1,0:T(8,128)(2,1)S(1)} %collective-permute-done.ahead_ref, bf16[256,256]{1,0:T(8,128)(2,1)S(1)} %collective-permute-done.1.back_ref, bf16[256,256]{1,0:T(8,128)(2,1)S(1)} %collective-permute-done.5.back2_ref, ...), custom_call_target="tpu_custom_call" | custom-call | tf_op jit(solution)/shard_map/stack/pallas_call | solution.py:392
Async XLA Ops:
  0.0 17.5 %copy-start = (bf16[1,128,2048]{2,1,0:T(8,128)(2,1)S(1)}, bf16[1,128,2048]{2,1,0:T(8,128)(2,1)}, u32[]{:S(2)}) copy-start(bf16[1,128,2048]{2,1,0:T(8,128)(2,1)} %param.5) | copy-start | bytes 1572868
  45.1 10.3 %collective-permute-start.2 = (bf16[256,256]{1,0:T(8,128)(2,1)S(1)}, bf16[256,256]{1,0:T(8,128)(2,1)S(1)}, u32[]{:S(2)}, u32[]{:S(2)}) collective-permute-start(bf16[256,256]{1,0:T(8,128)(2,1)S(1)} %get-tuple-element.28), channel_id=1, source_target_pairs={{0,64},{1,193},{2,66},{3,195},{4,68},{5,197},{6,70},{7,199},{8,72}... | collective-permute-start | bytes 393224 | tf_op jit(solution)/shard_map/ppermute | solution.py:480
  51.2 7.0 %collective-permute-start.3 = (bf16[256,256]{1,0:T(8,128)(2,1)S(1)}, bf16[256,256]{1,0:T(8,128)(2,1)S(1)}, u32[]{:S(2)}, u32[]{:S(2)}) collective-permute-start(bf16[256,256]{1,0:T(8,128)(2,1)S(1)} %get-tuple-element.29), channel_id=1, source_target_pairs={{0,32},{1,225},{2,34},{3,227},{4,36},{5,229},{6,38},{7,231},{8,40}... | collective-permute-start | bytes 393224 | tf_op jit(solution)/shard_map/ppermute | solution.py:480
  51.9 6.8 %collective-permute-start.4 = (bf16[256,256]{1,0:T(8,128)(2,1)S(1)}, bf16[256,256]{1,0:T(8,128)(2,1)S(1)}, u32[]{:S(2)}, u32[]{:S(2)}) collective-permute-start(bf16[256,256]{1,0:T(8,128)(2,1)S(1)} %get-tuple-element.30), channel_id=1, source_target_pairs={{0,224},{1,33},{2,226},{3,35},{4,228},{5,37},{6,230},{7,39},{8,232... | collective-permute-start | bytes 393224 | tf_op jit(solution)/shard_map/ppermute | solution.py:480
  52.7 9.8 %collective-permute-start = (bf16[256,256]{1,0:T(8,128)(2,1)S(1)}, bf16[256,256]{1,0:T(8,128)(2,1)S(1)}, u32[]{:S(2)}, u32[]{:S(2)}) collective-permute-start(bf16[256,256]{1,0:T(8,128)(2,1)S(1)} %get-tuple-element.26), channel_id=1, source_target_pairs={{0,32},{1,225},{2,34},{3,227},{4,36},{5,229},{6,38},{7,231},{8,40}... | collective-permute-start | bytes 393224 | tf_op jit(solution)/shard_map/ppermute | solution.py:480
  54.6 7.9 %collective-permute-start.1 = (bf16[256,256]{1,0:T(8,128)(2,1)S(1)}, bf16[256,256]{1,0:T(8,128)(2,1)S(1)}, u32[]{:S(2)}, u32[]{:S(2)}) collective-permute-start(bf16[256,256]{1,0:T(8,128)(2,1)S(1)} %get-tuple-element.27), channel_id=1, source_target_pairs={{0,224},{1,33},{2,226},{3,35},{4,228},{5,37},{6,230},{7,39},{8,232... | collective-permute-start | bytes 393224 | tf_op jit(solution)/shard_map/ppermute | solution.py:480
  58.8 6.1 %collective-permute-start.5 = (bf16[256,256]{1,0:T(8,128)(2,1)S(1)}, bf16[256,256]{1,0:T(8,128)(2,1)S(1)}, u32[]{:S(2)}, u32[]{:S(2)}) collective-permute-start(bf16[256,256]{1,0:T(8,128)(2,1)S(1)} %get-tuple-element.31), channel_id=1, source_target_pairs={{0,192},{1,65},{2,194},{3,67},{4,196},{5,69},{6,198},{7,71},{8,200... | collective-permute-start | bytes 393224 | tf_op jit(solution)/shard_map/ppermute | solution.py:480
  58.9 9.3 %collective-permute-start.6 = (bf16[256,256]{1,0:T(8,128)(2,1)S(1)}, bf16[256,256]{1,0:T(8,128)(2,1)S(1)}, u32[]{:S(2)}, u32[]{:S(2)}) collective-permute-start(bf16[256,256]{1,0:T(8,128)(2,1)S(1)} %get-tuple-element.32), channel_id=1, source_target_pairs={{0,64},{1,193},{2,66},{3,195},{4,68},{5,197},{6,70},{7,199},{8,72}... | collective-permute-start | bytes 393224 | tf_op jit(solution)/shard_map/ppermute | solution.py:480

commit v8 on v7

--- a/solution.py
+++ b/solution.py
@@ -369,7 +369,7 @@
     back_out_ref[...] = back.astype(BF16)
 
 
-def sum_kernel(keep_ref, ahead_ref, back_ref, back2_ref, ahead2_ref, out_hbm, out_ref, sems):
+def sum_kernel(keep_ref, back_ref, ahead_ref, back2_ref, ahead2_ref, out_hbm, out_ref, sems):
     half = out_ref.shape[0] // 2
     copies = []
     for i in range(2):
@@ -494,7 +494,7 @@
         "stack",
         [VMEM] * 5,
         (shape((lags, pair_dev), BF16),),
-        (keep, ahead1, back1, back2, ahead2),
+        (keep, back1, ahead1, back2, ahead2),
         [pltpu.VMEM((lags, pair_dev), BF16), pltpu.SemaphoreType.DMA((2,))],
         place=ANY,
     )

time: 69.2 us -> 68.4 us (0.988)
  waiting for transfers between devices: 9.86 us -> 8.39 us
  starting transfers between devices: 13.2 us -> 13.9 us
    ppermute x7, waiting for transfers between devices: 9.86 us -> 8.39 us  [shift(): return lax.ppermute(value, ('seg', 'tile'), ring)]
    ppermute x7, starting transfers between devices: 13.2 us -> 13.9 us  [shift(): return lax.ppermute(value, ('seg', 'tile'), ring)]
  transfers between devices with their start and end apart: 7 -> 7, of which waited for: 5 -> 3; matrix products, arithmetic and copies ran while one was open for 0% -> 0% of each run, Pallas kernels for 0% -> 0%
where the time goes in v8:
time: 68.4 us; the launch traced here: 68.3 us
  blocking collectives  36.2 us (53%)
  starting transfers between devices  13.9 us (20%)
  Pallas kernels  9.35 us (14%)
  waiting for transfers between devices  8.39 us (12%)
    all_to_all x1, blocking collectives, shards(): lax.all_to_all(outgoing.reshape(tiles, CAP, seg_len), 'tile', split_axis=...  20.4 us
    all_to_all x1, blocking collectives, shards(): lax.all_to_all(want, 'tile', split_axis=0, concat_axis=0, tiled=True)  15.8 us
    ppermute x7, starting transfers between devices, shift(): return lax.ppermute(value, ('seg', 'tile'), ring)  13.9 us
    pallas_call x6, Pallas kernels, _call(): pl.pallas_call(kernel, out_shape=outputs, in_specs=inputs, out_specs=(pla...  9.35 us
    ppermute x7, waiting for transfers between devices, shift(): return lax.ppermute(value, ('seg', 'tile'), ring)  8.39 us
  transfers between devices with their start and end apart: 7, of which 3 were waited for; matrix products, arithmetic and copies ran while one was open for 0% of the time, Pallas kernels for 0%

profile of v8, /device:TPU:1, one launch (start us, length us, event | category | flops | bytes accessed | tf_op | source)
XLA Modules:
  0.0 68.3 jit_solution(9239612978346993010)
XLA Ops:
  0.0 0.0 copy-start
  0.0 1.7 %request.1 = (bf16[32,8,128]{2,1,0:T(8,128)(2,1)S(1)}, bf16[512,256]{1,0:T(8,128)(2,1)S(1)}, bf16[16,128,256]{2,1,0:T(8,128)(2,1)S(1)}) custom-call(s32[2,256]{1,0:T(2,128)} %pair_hbm.1, s32[32,128]{1,0:T(8,128)} %bitcast.11, bf16[16,128,256]{2,1,0:T(8,128)(2,1)} %constant.4.clone.table_hbm), custom_call_target="tpu_custom_call" | custom-call | tf_op jit(solution)/shard_map/request/pallas_call | solution.py:392
  1.7 15.8 %all_to_all.10 = bf16[32,8,128]{2,1,0:T(8,128)(2,1)S(1)} all-to-all(bf16[32,8,128]{2,1,0:T(8,128)(2,1)S(1)} %get-tuple-element.19), channel_id=1, replica_groups=mesh['seg'=8,'tile'=32] {'tile'}, dimensions={0} | all-to-all | bytes 131072 | tf_op jit(solution)/shard_map/all_to_all | solution.py:436
  17.5 0.0 copy-done
  17.5 0.4 fusion
  17.9 20.4 %all_to_all.11 = bf16[32,8,2048]{2,1,0:T(8,128)(2,1)S(1)} all-to-all(bf16[32,8,2048]{2,1,0:T(8,128)(2,1)S(1)} %fusion), channel_id=1, replica_groups=mesh['seg'=8,'tile'=32] {'tile'}, dimensions={0} | all-to-all | bytes 2097152 | tf_op jit(solution)/shard_map/all_to_all | solution.py:438
  38.3 1.7 %transform.1 = (bf16[16,256,256]{2,1,0:T(8,128)(2,1)S(1)}, bf16[16,256,256]{2,1,0:T(8,128)(2,1)S(1)}, bf16[32,128,256]{2,1,0:T(8,128)(2,1)S(1)}) custom-call(bf16[256,2048]{1,0:T(8,128)(2,1)S(1)} %bitcast.10, bf16[32,128,256]{2,1,0:T(8,128)(2,1)} %constant.5.clone.table_hbm), custom_call_target="tpu_custom_call" | custom-call | tf_op jit(solution)/shard_map/transform/pallas_call | solution.py:392
  40.0 5.0 %correlate.1.lags_ref = bf16[8,256,256]{2,1,0:T(8,128)(2,1)S(1)} custom-call(bf16[16,256,256]{2,1,0:T(8,128)(2,1)S(1)} %get-tuple-element.20.yh_ref, bf16[16,256,256]{2,1,0:T(8,128)(2,1)S(1)} %get-tuple-element.21.yl_ref, bf16[32,128,256]{2,1,0:T(8,128)(2,1)S(1)} %get-tuple-element.22.table_ref, bf16[16,128,256]{2,1,0:T(8,128)(2,1)S(1)} %get-tuple-element.23.inverse_ref, ...), custom_call_target="tpu_custom_call" | custom-call | tf_op jit(solution)/shard_map/correlate/pallas_call | solution.py:392
  45.0 0.1 pack.1
  45.1 6.1 %collective-permute-start.2 = (bf16[256,256]{1,0:T(8,128)(2,1)S(1)}, bf16[256,256]{1,0:T(8,128)(2,1)S(1)}, u32[]{:S(2)}, u32[]{:S(2)}) collective-permute-start(bf16[256,256]{1,0:T(8,128)(2,1)S(1)} %get-tuple-element.28), channel_id=1, source_target_pairs={{0,64},{1,193},{2,66},{3,195},{4,68},{5,197},{6,70},{7,199},{8,72}... | collective-permute-start | bytes 393224 | tf_op jit(solution)/shard_map/ppermute | solution.py:480
  51.2 0.7 %collective-permute-start.3 = (bf16[256,256]{1,0:T(8,128)(2,1)S(1)}, bf16[256,256]{1,0:T(8,128)(2,1)S(1)}, u32[]{:S(2)}, u32[]{:S(2)}) collective-permute-start(bf16[256,256]{1,0:T(8,128)(2,1)S(1)} %get-tuple-element.29), channel_id=1, source_target_pairs={{0,32},{1,225},{2,34},{3,227},{4,36},{5,229},{6,38},{7,231},{8,40}... | collective-permute-start | bytes 393224 | tf_op jit(solution)/shard_map/ppermute | solution.py:480
  51.9 0.7 %collective-permute-start.4 = (bf16[256,256]{1,0:T(8,128)(2,1)S(1)}, bf16[256,256]{1,0:T(8,128)(2,1)S(1)}, u32[]{:S(2)}, u32[]{:S(2)}) collective-permute-start(bf16[256,256]{1,0:T(8,128)(2,1)S(1)} %get-tuple-element.30), channel_id=1, source_target_pairs={{0,224},{1,33},{2,226},{3,35},{4,228},{5,37},{6,230},{7,39},{8,232... | collective-permute-start | bytes 393224 | tf_op jit(solution)/shard_map/ppermute | solution.py:480
  52.7 0.7 %collective-permute-start = (bf16[256,256]{1,0:T(8,128)(2,1)S(1)}, bf16[256,256]{1,0:T(8,128)(2,1)S(1)}, u32[]{:S(2)}, u32[]{:S(2)}) collective-permute-start(bf16[256,256]{1,0:T(8,128)(2,1)S(1)} %get-tuple-element.26), channel_id=1, source_target_pairs={{0,224},{1,33},{2,226},{3,35},{4,228},{5,37},{6,230},{7,39},{8,232... | collective-permute-start | bytes 393224 | tf_op jit(solution)/shard_map/ppermute | solution.py:480
  53.4 1.9 %collective-permute-start.1 = (bf16[256,256]{1,0:T(8,128)(2,1)S(1)}, bf16[256,256]{1,0:T(8,128)(2,1)S(1)}, u32[]{:S(2)}, u32[]{:S(2)}) collective-permute-start(bf16[256,256]{1,0:T(8,128)(2,1)S(1)} %get-tuple-element.27), channel_id=1, source_target_pairs={{0,32},{1,225},{2,34},{3,227},{4,36},{5,229},{6,38},{7,231},{8,40}... | collective-permute-start | bytes 393224 | tf_op jit(solution)/shard_map/ppermute | solution.py:480
  55.3 0.0 collective-permute-done.2.far_ref
  55.4 2.8 %collective-permute-done.3.ahead_ref = bf16[256,256]{1,0:T(8,128)(2,1)S(1)} collective-permute-done((bf16[256,256]{1,0:T(8,128)(2,1)S(1)}, bf16[256,256]{1,0:T(8,128)(2,1)S(1)}, u32[]{:S(2)}, u32[]{:S(2)}) %collective-permute-start.3) | collective-permute-done | bytes 131104 | tf_op jit(solution)/shard_map/ppermute | solution.py:480
  58.2 0.0 collective-permute-done.4.back_ref
  58.2 0.1 relay.1
  58.3 0.4 collective-permute-start.5
  58.7 3.3 %collective-permute-start.6 = (bf16[256,256]{1,0:T(8,128)(2,1)S(1)}, bf16[256,256]{1,0:T(8,128)(2,1)S(1)}, u32[]{:S(2)}, u32[]{:S(2)}) collective-permute-start(bf16[256,256]{1,0:T(8,128)(2,1)S(1)} %get-tuple-element.32), channel_id=1, source_target_pairs={{0,64},{1,193},{2,66},{3,195},{4,68},{5,197},{6,70},{7,199},{8,72}... | collective-permute-start | bytes 393224 | tf_op jit(solution)/shard_map/ppermute | solution.py:480
  61.9 0.0 collective-permute-done.back_ref
  61.9 0.0 collective-permute-done.1.ahead_ref
  61.9 2.4 %collective-permute-done.5.back2_ref = bf16[256,256]{1,0:T(8,128)(2,1)S(1)} collective-permute-done((bf16[256,256]{1,0:T(8,128)(2,1)S(1)}, bf16[256,256]{1,0:T(8,128)(2,1)S(1)}, u32[]{:S(2)}, u32[]{:S(2)}) %collective-permute-start.5) | collective-permute-done | bytes 131104 | tf_op jit(solution)/shard_map/ppermute | solution.py:480
  64.4 3.1 %collective-permute-done.6.ahead2_ref = bf16[256,256]{1,0:T(8,128)(2,1)S(1)} collective-permute-done((bf16[256,256]{1,0:T(8,128)(2,1)S(1)}, bf16[256,256]{1,0:T(8,128)(2,1)S(1)}, u32[]{:S(2)}, u32[]{:S(2)}) %collective-permute-start.6) | collective-permute-done | bytes 131104 | tf_op jit(solution)/shard_map/ppermute | solution.py:480
  67.5 0.8 %stack.1 = bf16[256,256]{1,0:T(8,128)(2,1)} custom-call(bf16[3,256,256]{2,1,0:T(8,128)(2,1)S(1)} %get-tuple-element.25.keep_ref, bf16[256,256]{1,0:T(8,128)(2,1)S(1)} %collective-permute-done.back_ref, bf16[256,256]{1,0:T(8,128)(2,1)S(1)} %collective-permute-done.1.ahead_ref, bf16[256,256]{1,0:T(8,128)(2,1)S(1)} %collective-permute-done.5.back2_ref, ...), custom_call_target="tpu_custom_call" | custom-call | tf_op jit(solution)/shard_map/stack/pallas_call | solution.py:392
Async XLA Ops:
  0.0 17.5 %copy-start = (bf16[1,128,2048]{2,1,0:T(8,128)(2,1)S(1)}, bf16[1,128,2048]{2,1,0:T(8,128)(2,1)}, u32[]{:S(2)}) copy-start(bf16[1,128,2048]{2,1,0:T(8,128)(2,1)} %param.5) | copy-start | bytes 1572868
  45.1 10.3 %collective-permute-start.2 = (bf16[256,256]{1,0:T(8,128)(2,1)S(1)}, bf16[256,256]{1,0:T(8,128)(2,1)S(1)}, u32[]{:S(2)}, u32[]{:S(2)}) collective-permute-start(bf16[256,256]{1,0:T(8,128)(2,1)S(1)} %get-tuple-element.28), channel_id=1, source_target_pairs={{0,64},{1,193},{2,66},{3,195},{4,68},{5,197},{6,70},{7,199},{8,72}... | collective-permute-start | bytes 393224 | tf_op jit(solution)/shard_map/ppermute | solution.py:480
  51.2 7.0 %collective-permute-start.3 = (bf16[256,256]{1,0:T(8,128)(2,1)S(1)}, bf16[256,256]{1,0:T(8,128)(2,1)S(1)}, u32[]{:S(2)}, u32[]{:S(2)}) collective-permute-start(bf16[256,256]{1,0:T(8,128)(2,1)S(1)} %get-tuple-element.29), channel_id=1, source_target_pairs={{0,32},{1,225},{2,34},{3,227},{4,36},{5,229},{6,38},{7,231},{8,40}... | collective-permute-start | bytes 393224 | tf_op jit(solution)/shard_map/ppermute | solution.py:480
  51.9 6.3 %collective-permute-start.4 = (bf16[256,256]{1,0:T(8,128)(2,1)S(1)}, bf16[256,256]{1,0:T(8,128)(2,1)S(1)}, u32[]{:S(2)}, u32[]{:S(2)}) collective-permute-start(bf16[256,256]{1,0:T(8,128)(2,1)S(1)} %get-tuple-element.30), channel_id=1, source_target_pairs={{0,224},{1,33},{2,226},{3,35},{4,228},{5,37},{6,230},{7,39},{8,232... | collective-permute-start | bytes 393224 | tf_op jit(solution)/shard_map/ppermute | solution.py:480
  52.7 9.3 %collective-permute-start = (bf16[256,256]{1,0:T(8,128)(2,1)S(1)}, bf16[256,256]{1,0:T(8,128)(2,1)S(1)}, u32[]{:S(2)}, u32[]{:S(2)}) collective-permute-start(bf16[256,256]{1,0:T(8,128)(2,1)S(1)} %get-tuple-element.26), channel_id=1, source_target_pairs={{0,224},{1,33},{2,226},{3,35},{4,228},{5,37},{6,230},{7,39},{8,232... | collective-permute-start | bytes 393224 | tf_op jit(solution)/shard_map/ppermute | solution.py:480
  53.4 8.5 %collective-permute-start.1 = (bf16[256,256]{1,0:T(8,128)(2,1)S(1)}, bf16[256,256]{1,0:T(8,128)(2,1)S(1)}, u32[]{:S(2)}, u32[]{:S(2)}) collective-permute-start(bf16[256,256]{1,0:T(8,128)(2,1)S(1)} %get-tuple-element.27), channel_id=1, source_target_pairs={{0,32},{1,225},{2,34},{3,227},{4,36},{5,229},{6,38},{7,231},{8,40}... | collective-permute-start | bytes 393224 | tf_op jit(solution)/shard_map/ppermute | solution.py:480
  58.3 6.1 %collective-permute-start.5 = (bf16[256,256]{1,0:T(8,128)(2,1)S(1)}, bf16[256,256]{1,0:T(8,128)(2,1)S(1)}, u32[]{:S(2)}, u32[]{:S(2)}) collective-permute-start(bf16[256,256]{1,0:T(8,128)(2,1)S(1)} %get-tuple-element.31), channel_id=1, source_target_pairs={{0,192},{1,65},{2,194},{3,67},{4,196},{5,69},{6,198},{7,71},{8,200... | collective-permute-start | bytes 393224 | tf_op jit(solution)/shard_map/ppermute | solution.py:480
  58.7 8.8 %collective-permute-start.6 = (bf16[256,256]{1,0:T(8,128)(2,1)S(1)}, bf16[256,256]{1,0:T(8,128)(2,1)S(1)}, u32[]{:S(2)}, u32[]{:S(2)}) collective-permute-start(bf16[256,256]{1,0:T(8,128)(2,1)S(1)} %get-tuple-element.32), channel_id=1, source_target_pairs={{0,64},{1,193},{2,66},{3,195},{4,68},{5,197},{6,70},{7,199},{8,72}... | collective-permute-start | bytes 393224 | tf_op jit(solution)/shard_map/ppermute | solution.py:480

commit v9 on v8

--- a/solution.py
+++ b/solution.py
@@ -261,7 +261,10 @@
     of_pair = _dot(slot.astype(BF16), owners, ((0,), (0,)))
     slot = jnp.sum(of_pair * _one_hot(place, LANES), axis=0, keepdims=True)
     position = owner * CAP + slot.astype(jnp.int32)
-    pick_ref[...] = _one_hot(position, holders * CAP).T.astype(BF16)
+    position = jnp.broadcast_to(position.astype(F32), (LANES, position.shape[1])).T
+    lane = lax.broadcasted_iota(jnp.int32, position.shape, 1).astype(F32)
+    for start in range(0, holders * CAP, LANES):
+        pick_ref[:, start : start + LANES] = (position - start == lane).astype(F32).astype(BF16)
     copies[2].wait()
 
 

time: 68.4 us -> 68.5 us (level)
  transfers between devices with their start and end apart: 7 -> 7, of which waited for: 3 -> 4; matrix products, arithmetic and copies ran while one was open for 0% -> 0% of each run, Pallas kernels for 0% -> 0%
where the time goes in v9:
time: 68.5 us; the launch traced here: 68.3 us
  blocking collectives  36.2 us (53%)
  starting transfers between devices  13.9 us (20%)
  Pallas kernels  9.31 us (14%)
  waiting for transfers between devices  8.44 us (12%)
    all_to_all x1, blocking collectives, shards(): lax.all_to_all(outgoing.reshape(tiles, CAP, seg_len), 'tile', split_axis=...  20.4 us
    all_to_all x1, blocking collectives, shards(): lax.all_to_all(want, 'tile', split_axis=0, concat_axis=0, tiled=True)  15.8 us
    ppermute x7, starting transfers between devices, shift(): return lax.ppermute(value, ('seg', 'tile'), ring)  13.9 us
    pallas_call x6, Pallas kernels, _call(): pl.pallas_call(kernel, out_shape=outputs, in_specs=inputs, out_specs=(pla...  9.31 us
    ppermute x7, waiting for transfers between devices, shift(): return lax.ppermute(value, ('seg', 'tile'), ring)  8.44 us
  transfers between devices with their start and end apart: 7, of which 4 were waited for; matrix products, arithmetic and copies ran while one was open for 0% of the time, Pallas kernels for 0%

profile of v9, /device:TPU:1, one launch (start us, length us, event | category | flops | bytes accessed | tf_op | source)
XLA Modules:
  0.0 68.3 jit_solution(15734336450602164373)
XLA Ops:
  0.0 0.0 copy-start
  0.0 1.7 %request.1 = (bf16[32,8,128]{2,1,0:T(8,128)(2,1)S(1)}, bf16[512,256]{1,0:T(8,128)(2,1)S(1)}, bf16[16,128,256]{2,1,0:T(8,128)(2,1)S(1)}) custom-call(s32[2,256]{1,0:T(2,128)} %pair_hbm.1, s32[32,128]{1,0:T(8,128)} %bitcast.11, bf16[16,128,256]{2,1,0:T(8,128)(2,1)} %constant.4.clone.table_hbm), custom_call_target="tpu_custom_call" | custom-call | tf_op jit(solution)/shard_map/request/pallas_call | solution.py:395
  1.7 15.8 %all_to_all.10 = bf16[32,8,128]{2,1,0:T(8,128)(2,1)S(1)} all-to-all(bf16[32,8,128]{2,1,0:T(8,128)(2,1)S(1)} %get-tuple-element.19), channel_id=1, replica_groups=mesh['seg'=8,'tile'=32] {'tile'}, dimensions={0} | all-to-all | bytes 131072 | tf_op jit(solution)/shard_map/all_to_all | solution.py:439
  17.4 0.0 copy-done
  17.4 0.4 fusion
  17.9 20.4 %all_to_all.11 = bf16[32,8,2048]{2,1,0:T(8,128)(2,1)S(1)} all-to-all(bf16[32,8,2048]{2,1,0:T(8,128)(2,1)S(1)} %fusion), channel_id=1, replica_groups=mesh['seg'=8,'tile'=32] {'tile'}, dimensions={0} | all-to-all | bytes 2097152 | tf_op jit(solution)/shard_map/all_to_all | solution.py:441
  38.3 1.7 %transform.1 = (bf16[16,256,256]{2,1,0:T(8,128)(2,1)S(1)}, bf16[16,256,256]{2,1,0:T(8,128)(2,1)S(1)}, bf16[32,128,256]{2,1,0:T(8,128)(2,1)S(1)}) custom-call(bf16[256,2048]{1,0:T(8,128)(2,1)S(1)} %bitcast.10, bf16[32,128,256]{2,1,0:T(8,128)(2,1)} %constant.5.clone.table_hbm), custom_call_target="tpu_custom_call" | custom-call | tf_op jit(solution)/shard_map/transform/pallas_call | solution.py:395
  40.0 5.0 %correlate.1.lags_ref = bf16[8,256,256]{2,1,0:T(8,128)(2,1)S(1)} custom-call(bf16[16,256,256]{2,1,0:T(8,128)(2,1)S(1)} %get-tuple-element.20.yh_ref, bf16[16,256,256]{2,1,0:T(8,128)(2,1)S(1)} %get-tuple-element.21.yl_ref, bf16[32,128,256]{2,1,0:T(8,128)(2,1)S(1)} %get-tuple-element.22.table_ref, bf16[16,128,256]{2,1,0:T(8,128)(2,1)S(1)} %get-tuple-element.23.inverse_ref, ...), custom_call_target="tpu_custom_call" | custom-call | tf_op jit(solution)/shard_map/correlate/pallas_call | solution.py:395
  45.0 0.1 pack.1
  45.0 6.1 %collective-permute-start.2 = (bf16[256,256]{1,0:T(8,128)(2,1)S(1)}, bf16[256,256]{1,0:T(8,128)(2,1)S(1)}, u32[]{:S(2)}, u32[]{:S(2)}) collective-permute-start(bf16[256,256]{1,0:T(8,128)(2,1)S(1)} %get-tuple-element.28), channel_id=1, source_target_pairs={{0,64},{1,193},{2,66},{3,195},{4,68},{5,197},{6,70},{7,199},{8,72}... | collective-permute-start | bytes 393224 | tf_op jit(solution)/shard_map/ppermute | solution.py:483
  51.2 0.7 %collective-permute-start.3 = (bf16[256,256]{1,0:T(8,128)(2,1)S(1)}, bf16[256,256]{1,0:T(8,128)(2,1)S(1)}, u32[]{:S(2)}, u32[]{:S(2)}) collective-permute-start(bf16[256,256]{1,0:T(8,128)(2,1)S(1)} %get-tuple-element.29), channel_id=1, source_target_pairs={{0,32},{1,225},{2,34},{3,227},{4,36},{5,229},{6,38},{7,231},{8,40}... | collective-permute-start | bytes 393224 | tf_op jit(solution)/shard_map/ppermute | solution.py:483
  51.9 0.7 %collective-permute-start.4 = (bf16[256,256]{1,0:T(8,128)(2,1)S(1)}, bf16[256,256]{1,0:T(8,128)(2,1)S(1)}, u32[]{:S(2)}, u32[]{:S(2)}) collective-permute-start(bf16[256,256]{1,0:T(8,128)(2,1)S(1)} %get-tuple-element.30), channel_id=1, source_target_pairs={{0,224},{1,33},{2,226},{3,35},{4,228},{5,37},{6,230},{7,39},{8,232... | collective-permute-start | bytes 393224 | tf_op jit(solution)/shard_map/ppermute | solution.py:483
  52.6 0.7 %collective-permute-start = (bf16[256,256]{1,0:T(8,128)(2,1)S(1)}, bf16[256,256]{1,0:T(8,128)(2,1)S(1)}, u32[]{:S(2)}, u32[]{:S(2)}) collective-permute-start(bf16[256,256]{1,0:T(8,128)(2,1)S(1)} %get-tuple-element.26), channel_id=1, source_target_pairs={{0,224},{1,33},{2,226},{3,35},{4,228},{5,37},{6,230},{7,39},{8,232... | collective-permute-start | bytes 393224 | tf_op jit(solution)/shard_map/ppermute | solution.py:483
  53.3 1.9 %collective-permute-start.1 = (bf16[256,256]{1,0:T(8,128)(2,1)S(1)}, bf16[256,256]{1,0:T(8,128)(2,1)S(1)}, u32[]{:S(2)}, u32[]{:S(2)}) collective-permute-start(bf16[256,256]{1,0:T(8,128)(2,1)S(1)} %get-tuple-element.27), channel_id=1, source_target_pairs={{0,32},{1,225},{2,34},{3,227},{4,36},{5,229},{6,38},{7,231},{8,40}... | collective-permute-start | bytes 393224 | tf_op jit(solution)/shard_map/ppermute | solution.py:483
  55.3 0.1 collective-permute-done.2.far_ref
  55.4 2.8 %collective-permute-done.3.ahead_ref = bf16[256,256]{1,0:T(8,128)(2,1)S(1)} collective-permute-done((bf16[256,256]{1,0:T(8,128)(2,1)S(1)}, bf16[256,256]{1,0:T(8,128)(2,1)S(1)}, u32[]{:S(2)}, u32[]{:S(2)}) %collective-permute-start.3) | collective-permute-done | bytes 131104 | tf_op jit(solution)/shard_map/ppermute | solution.py:483
  58.2 0.0 collective-permute-done.4.back_ref
  58.2 0.1 relay.1
  58.3 0.3 collective-permute-start.5
  58.6 3.3 %collective-permute-start.6 = (bf16[256,256]{1,0:T(8,128)(2,1)S(1)}, bf16[256,256]{1,0:T(8,128)(2,1)S(1)}, u32[]{:S(2)}, u32[]{:S(2)}) collective-permute-start(bf16[256,256]{1,0:T(8,128)(2,1)S(1)} %get-tuple-element.32), channel_id=1, source_target_pairs={{0,64},{1,193},{2,66},{3,195},{4,68},{5,197},{6,70},{7,199},{8,72}... | collective-permute-start | bytes 393224 | tf_op jit(solution)/shard_map/ppermute | solution.py:483
  61.9 0.0 collective-permute-done.back_ref
  61.9 0.0 collective-permute-done.1.ahead_ref
  61.9 2.4 %collective-permute-done.5.back2_ref = bf16[256,256]{1,0:T(8,128)(2,1)S(1)} collective-permute-done((bf16[256,256]{1,0:T(8,128)(2,1)S(1)}, bf16[256,256]{1,0:T(8,128)(2,1)S(1)}, u32[]{:S(2)}, u32[]{:S(2)}) %collective-permute-start.5) | collective-permute-done | bytes 131104 | tf_op jit(solution)/shard_map/ppermute | solution.py:483
  64.4 3.1 %collective-permute-done.6.ahead2_ref = bf16[256,256]{1,0:T(8,128)(2,1)S(1)} collective-permute-done((bf16[256,256]{1,0:T(8,128)(2,1)S(1)}, bf16[256,256]{1,0:T(8,128)(2,1)S(1)}, u32[]{:S(2)}, u32[]{:S(2)}) %collective-permute-start.6) | collective-permute-done | bytes 131104 | tf_op jit(solution)/shard_map/ppermute | solution.py:483
  67.5 0.8 %stack.1 = bf16[256,256]{1,0:T(8,128)(2,1)} custom-call(bf16[3,256,256]{2,1,0:T(8,128)(2,1)S(1)} %get-tuple-element.25.keep_ref, bf16[256,256]{1,0:T(8,128)(2,1)S(1)} %collective-permute-done.back_ref, bf16[256,256]{1,0:T(8,128)(2,1)S(1)} %collective-permute-done.1.ahead_ref, bf16[256,256]{1,0:T(8,128)(2,1)S(1)} %collective-permute-done.5.back2_ref, ...), custom_call_target="tpu_custom_call" | custom-call | tf_op jit(solution)/shard_map/stack/pallas_call | solution.py:395
Async XLA Ops:
  0.0 17.4 %copy-start = (bf16[1,128,2048]{2,1,0:T(8,128)(2,1)S(1)}, bf16[1,128,2048]{2,1,0:T(8,128)(2,1)}, u32[]{:S(2)}) copy-start(bf16[1,128,2048]{2,1,0:T(8,128)(2,1)} %param.5) | copy-start | bytes 1572868
  45.0 10.3 %collective-permute-start.2 = (bf16[256,256]{1,0:T(8,128)(2,1)S(1)}, bf16[256,256]{1,0:T(8,128)(2,1)S(1)}, u32[]{:S(2)}, u32[]{:S(2)}) collective-permute-start(bf16[256,256]{1,0:T(8,128)(2,1)S(1)} %get-tuple-element.28), channel_id=1, source_target_pairs={{0,64},{1,193},{2,66},{3,195},{4,68},{5,197},{6,70},{7,199},{8,72}... | collective-permute-start | bytes 393224 | tf_op jit(solution)/shard_map/ppermute | solution.py:483
  51.2 7.0 %collective-permute-start.3 = (bf16[256,256]{1,0:T(8,128)(2,1)S(1)}, bf16[256,256]{1,0:T(8,128)(2,1)S(1)}, u32[]{:S(2)}, u32[]{:S(2)}) collective-permute-start(bf16[256,256]{1,0:T(8,128)(2,1)S(1)} %get-tuple-element.29), channel_id=1, source_target_pairs={{0,32},{1,225},{2,34},{3,227},{4,36},{5,229},{6,38},{7,231},{8,40}... | collective-permute-start | bytes 393224 | tf_op jit(solution)/shard_map/ppermute | solution.py:483
  51.9 6.3 %collective-permute-start.4 = (bf16[256,256]{1,0:T(8,128)(2,1)S(1)}, bf16[256,256]{1,0:T(8,128)(2,1)S(1)}, u32[]{:S(2)}, u32[]{:S(2)}) collective-permute-start(bf16[256,256]{1,0:T(8,128)(2,1)S(1)} %get-tuple-element.30), channel_id=1, source_target_pairs={{0,224},{1,33},{2,226},{3,35},{4,228},{5,37},{6,230},{7,39},{8,232... | collective-permute-start | bytes 393224 | tf_op jit(solution)/shard_map/ppermute | solution.py:483
  52.6 9.3 %collective-permute-start = (bf16[256,256]{1,0:T(8,128)(2,1)S(1)}, bf16[256,256]{1,0:T(8,128)(2,1)S(1)}, u32[]{:S(2)}, u32[]{:S(2)}) collective-permute-start(bf16[256,256]{1,0:T(8,128)(2,1)S(1)} %get-tuple-element.26), channel_id=1, source_target_pairs={{0,224},{1,33},{2,226},{3,35},{4,228},{5,37},{6,230},{7,39},{8,232... | collective-permute-start | bytes 393224 | tf_op jit(solution)/shard_map/ppermute | solution.py:483
  53.3 8.6 %collective-permute-start.1 = (bf16[256,256]{1,0:T(8,128)(2,1)S(1)}, bf16[256,256]{1,0:T(8,128)(2,1)S(1)}, u32[]{:S(2)}, u32[]{:S(2)}) collective-permute-start(bf16[256,256]{1,0:T(8,128)(2,1)S(1)} %get-tuple-element.27), channel_id=1, source_target_pairs={{0,32},{1,225},{2,34},{3,227},{4,36},{5,229},{6,38},{7,231},{8,40}... | collective-permute-start | bytes 393224 | tf_op jit(solution)/shard_map/ppermute | solution.py:483
  58.3 6.1 %collective-permute-start.5 = (bf16[256,256]{1,0:T(8,128)(2,1)S(1)}, bf16[256,256]{1,0:T(8,128)(2,1)S(1)}, u32[]{:S(2)}, u32[]{:S(2)}) collective-permute-start(bf16[256,256]{1,0:T(8,128)(2,1)S(1)} %get-tuple-element.31), channel_id=1, source_target_pairs={{0,192},{1,65},{2,194},{3,67},{4,196},{5,69},{6,198},{7,71},{8,200... | collective-permute-start | bytes 393224 | tf_op jit(solution)/shard_map/ppermute | solution.py:483
  58.6 8.9 %collective-permute-start.6 = (bf16[256,256]{1,0:T(8,128)(2,1)S(1)}, bf16[256,256]{1,0:T(8,128)(2,1)S(1)}, u32[]{:S(2)}, u32[]{:S(2)}) collective-permute-start(bf16[256,256]{1,0:T(8,128)(2,1)S(1)} %get-tuple-element.32), channel_id=1, source_target_pairs={{0,64},{1,193},{2,66},{3,195},{4,68},{5,197},{6,70},{7,199},{8,72}... | collective-permute-start | bytes 393224 | tf_op jit(solution)/shard_map/ppermute | solution.py:483

commit v10 on v9

--- a/solution.py
+++ b/solution.py
@@ -372,18 +372,14 @@
     back_out_ref[...] = back.astype(BF16)
 
 
-def sum_kernel(keep_ref, back_ref, ahead_ref, back2_ref, ahead2_ref, out_hbm, out_ref, sems):
-    half = out_ref.shape[0] // 2
-    copies = []
-    for i in range(2):
-        part = slice(i * half, (i + 1) * half)
-        total = keep_ref[0, :, part].astype(F32) + ahead_ref[:, part].astype(F32) + back_ref[:, part].astype(F32)
-        total = total + ahead2_ref[:, part].astype(F32) + back2_ref[:, part].astype(F32)
-        out_ref[part] = total.T.astype(BF16)
-        copies.append(pltpu.make_async_copy(out_ref.at[part], out_hbm.at[part], sems.at[i]))
-        copies[i].start()
-    for copy in copies:
-        copy.wait()
+def early_kernel(keep_ref, back_ref, ahead_ref, out_ref):
+    total = keep_ref[0].astype(F32) + back_ref[...].astype(F32) + ahead_ref[...].astype(F32)
+    out_ref[...] = total.T
+
+
+def sum_kernel(back2_ref, ahead2_ref, early_ref, out_ref):
+    late = back2_ref[...].astype(F32) + ahead2_ref[...].astype(F32)
+    out_ref[...] = (early_ref[...] + late.T).astype(BF16)
 
 
 VMEM = pl.BlockSpec(memory_space=pltpu.VMEM)
@@ -391,12 +387,12 @@
 MIB = 1024 * 1024
 
 
-def _call(kernel, name, inputs, outputs, args, scratch=(), limit=4, place=VMEM):
+def _call(kernel, name, inputs, outputs, args, scratch=(), limit=4):
     return pl.pallas_call(
         kernel,
         out_shape=outputs,
         in_specs=inputs,
-        out_specs=(place,) * len(outputs),
+        out_specs=(VMEM,) * len(outputs),
         scratch_shapes=scratch,
         compiler_params=pltpu.CompilerParams(vmem_limit_bytes=limit * MIB),
         name=name,
@@ -492,14 +488,11 @@
         (keep, far, ahead, back),
     )
     ahead2, back2 = shift(ahead2, 2), shift(back2, -2)
+    (early,) = _call(
+        early_kernel, "early", [VMEM] * 3, (pltpu.VMEM((lags, pair_dev), F32),), (keep, back1, ahead1)
+    )
     (out,) = _call(
-        sum_kernel,
-        "stack",
-        [VMEM] * 5,
-        (shape((lags, pair_dev), BF16),),
-        (keep, back1, ahead1, back2, ahead2),
-        [pltpu.VMEM((lags, pair_dev), BF16), pltpu.SemaphoreType.DMA((2,))],
-        place=ANY,
+        sum_kernel, "stack", [VMEM] * 3, (shape((lags, pair_dev), BF16),), (back2, ahead2, early)
     )
     return out
 

time: 68.5 us -> 68.4 us (level)
    pallas_call x6 -> x7, Pallas kernels: 9.31 us -> 9.41 us  [_call(): pl.pallas_call(kernel, out_shape=outputs, in_specs=inputs, out_specs=(VME...]
where the time goes in v10:
time: 68.4 us; the launch traced here: 68.3 us
  blocking collectives  36.2 us (53%)
  starting transfers between devices  13.9 us (20%)
  Pallas kernels  9.41 us (14%)
  waiting for transfers between devices  8.31 us (12%)
    all_to_all x1, blocking collectives, shards(): lax.all_to_all(outgoing.reshape(tiles, CAP, seg_len), 'tile', split_axis=...  20.4 us
    all_to_all x1, blocking collectives, shards(): lax.all_to_all(want, 'tile', split_axis=0, concat_axis=0, tiled=True)  15.8 us
    ppermute x7, starting transfers between devices, shift(): return lax.ppermute(value, ('seg', 'tile'), ring)  13.9 us
    pallas_call x7, Pallas kernels, _call(): pl.pallas_call(kernel, out_shape=outputs, in_specs=inputs, out_specs=(VME...  9.41 us
    ppermute x7, waiting for transfers between devices, shift(): return lax.ppermute(value, ('seg', 'tile'), ring)  8.31 us
  transfers between devices with their start and end apart: 7, of which 4 were waited for; matrix products, arithmetic and copies ran while one was open for 0% of the time, Pallas kernels for 0%

profile of v10, /device:TPU:1, one launch (start us, length us, event | category | flops | bytes accessed | tf_op | source)
XLA Modules:
  0.0 68.3 jit_solution(11020986849292283321)
XLA Ops:
  0.0 0.0 copy-start
  0.0 1.7 %request.1 = (bf16[32,8,128]{2,1,0:T(8,128)(2,1)S(1)}, bf16[512,256]{1,0:T(8,128)(2,1)S(1)}, bf16[16,128,256]{2,1,0:T(8,128)(2,1)S(1)}) custom-call(s32[2,256]{1,0:T(2,128)} %pair_hbm.1, s32[32,128]{1,0:T(8,128)} %bitcast.11, bf16[16,128,256]{2,1,0:T(8,128)(2,1)} %constant.4.clone.table_hbm), custom_call_target="tpu_custom_call" | custom-call | tf_op jit(solution)/shard_map/request/pallas_call | solution.py:391
  1.7 15.8 %all_to_all.10 = bf16[32,8,128]{2,1,0:T(8,128)(2,1)S(1)} all-to-all(bf16[32,8,128]{2,1,0:T(8,128)(2,1)S(1)} %get-tuple-element.19), channel_id=1, replica_groups=mesh['seg'=8,'tile'=32] {'tile'}, dimensions={0} | all-to-all | bytes 131072 | tf_op jit(solution)/shard_map/all_to_all | solution.py:435
  17.4 0.0 copy-done
  17.4 0.4 fusion
  17.9 20.4 %all_to_all.11 = bf16[32,8,2048]{2,1,0:T(8,128)(2,1)S(1)} all-to-all(bf16[32,8,2048]{2,1,0:T(8,128)(2,1)S(1)} %fusion), channel_id=1, replica_groups=mesh['seg'=8,'tile'=32] {'tile'}, dimensions={0} | all-to-all | bytes 2097152 | tf_op jit(solution)/shard_map/all_to_all | solution.py:437
  38.3 1.7 %transform.1 = (bf16[16,256,256]{2,1,0:T(8,128)(2,1)S(1)}, bf16[16,256,256]{2,1,0:T(8,128)(2,1)S(1)}, bf16[32,128,256]{2,1,0:T(8,128)(2,1)S(1)}) custom-call(bf16[256,2048]{1,0:T(8,128)(2,1)S(1)} %bitcast.10, bf16[32,128,256]{2,1,0:T(8,128)(2,1)} %constant.5.clone.table_hbm), custom_call_target="tpu_custom_call" | custom-call | tf_op jit(solution)/shard_map/transform/pallas_call | solution.py:391
  40.0 5.0 %correlate.1.lags_ref = bf16[8,256,256]{2,1,0:T(8,128)(2,1)S(1)} custom-call(bf16[16,256,256]{2,1,0:T(8,128)(2,1)S(1)} %get-tuple-element.20.yh_ref, bf16[16,256,256]{2,1,0:T(8,128)(2,1)S(1)} %get-tuple-element.21.yl_ref, bf16[32,128,256]{2,1,0:T(8,128)(2,1)S(1)} %get-tuple-element.22.table_ref, bf16[16,128,256]{2,1,0:T(8,128)(2,1)S(1)} %get-tuple-element.23.inverse_ref, ...), custom_call_target="tpu_custom_call" | custom-call | tf_op jit(solution)/shard_map/correlate/pallas_call | solution.py:391
  45.0 0.1 pack.1
  45.0 6.1 %collective-permute-start = (bf16[256,256]{1,0:T(8,128)(2,1)S(1)}, bf16[256,256]{1,0:T(8,128)(2,1)S(1)}, u32[]{:S(2)}, u32[]{:S(2)}) collective-permute-start(bf16[256,256]{1,0:T(8,128)(2,1)S(1)} %get-tuple-element.26), channel_id=1, source_target_pairs={{0,64},{1,193},{2,66},{3,195},{4,68},{5,197},{6,70},{7,199},{8,72}... | collective-permute-start | bytes 393224 | tf_op jit(solution)/shard_map/ppermute | solution.py:479
  51.2 0.7 %collective-permute-start.1 = (bf16[256,256]{1,0:T(8,128)(2,1)S(1)}, bf16[256,256]{1,0:T(8,128)(2,1)S(1)}, u32[]{:S(2)}, u32[]{:S(2)}) collective-permute-start(bf16[256,256]{1,0:T(8,128)(2,1)S(1)} %get-tuple-element.27), channel_id=1, source_target_pairs={{0,32},{1,225},{2,34},{3,227},{4,36},{5,229},{6,38},{7,231},{8,40}... | collective-permute-start | bytes 393224 | tf_op jit(solution)/shard_map/ppermute | solution.py:479
  51.9 0.7 %collective-permute-start.2 = (bf16[256,256]{1,0:T(8,128)(2,1)S(1)}, bf16[256,256]{1,0:T(8,128)(2,1)S(1)}, u32[]{:S(2)}, u32[]{:S(2)}) collective-permute-start(bf16[256,256]{1,0:T(8,128)(2,1)S(1)} %get-tuple-element.28), channel_id=1, source_target_pairs={{0,224},{1,33},{2,226},{3,35},{4,228},{5,37},{6,230},{7,39},{8,232... | collective-permute-start | bytes 393224 | tf_op jit(solution)/shard_map/ppermute | solution.py:479
  52.6 0.7 %collective-permute-start.5 = (bf16[256,256]{1,0:T(8,128)(2,1)S(1)}, bf16[256,256]{1,0:T(8,128)(2,1)S(1)}, u32[]{:S(2)}, u32[]{:S(2)}) collective-permute-start(bf16[256,256]{1,0:T(8,128)(2,1)S(1)} %get-tuple-element.31), channel_id=1, source_target_pairs={{0,224},{1,33},{2,226},{3,35},{4,228},{5,37},{6,230},{7,39},{8,232... | collective-permute-start | bytes 393224 | tf_op jit(solution)/shard_map/ppermute | solution.py:479
  53.3 1.9 %collective-permute-start.6 = (bf16[256,256]{1,0:T(8,128)(2,1)S(1)}, bf16[256,256]{1,0:T(8,128)(2,1)S(1)}, u32[]{:S(2)}, u32[]{:S(2)}) collective-permute-start(bf16[256,256]{1,0:T(8,128)(2,1)S(1)} %get-tuple-element.32), channel_id=1, source_target_pairs={{0,32},{1,225},{2,34},{3,227},{4,36},{5,229},{6,38},{7,231},{8,40}... | collective-permute-start | bytes 393224 | tf_op jit(solution)/shard_map/ppermute | solution.py:479
  55.3 0.1 collective-permute-done.far_ref
  55.4 2.8 %collective-permute-done.1.ahead_ref = bf16[256,256]{1,0:T(8,128)(2,1)S(1)} collective-permute-done((bf16[256,256]{1,0:T(8,128)(2,1)S(1)}, bf16[256,256]{1,0:T(8,128)(2,1)S(1)}, u32[]{:S(2)}, u32[]{:S(2)}) %collective-permute-start.1) | collective-permute-done | bytes 131104 | tf_op jit(solution)/shard_map/ppermute | solution.py:479
  58.2 0.0 collective-permute-done.2.back_ref
  58.2 0.1 relay.1
  58.3 0.3 collective-permute-start.3
  58.6 3.3 %collective-permute-start.4 = (bf16[256,256]{1,0:T(8,128)(2,1)S(1)}, bf16[256,256]{1,0:T(8,128)(2,1)S(1)}, u32[]{:S(2)}, u32[]{:S(2)}) collective-permute-start(bf16[256,256]{1,0:T(8,128)(2,1)S(1)} %get-tuple-element.30), channel_id=1, source_target_pairs={{0,64},{1,193},{2,66},{3,195},{4,68},{5,197},{6,70},{7,199},{8,72}... | collective-permute-start | bytes 393224 | tf_op jit(solution)/shard_map/ppermute | solution.py:479
  61.9 0.0 collective-permute-done.5.back_ref
  61.9 0.0 collective-permute-done.6.ahead_ref
  61.9 0.1 early.1.early_ref
  62.1 2.3 %collective-permute-done.3.back2_ref = bf16[256,256]{1,0:T(8,128)(2,1)S(1)} collective-permute-done((bf16[256,256]{1,0:T(8,128)(2,1)S(1)}, bf16[256,256]{1,0:T(8,128)(2,1)S(1)}, u32[]{:S(2)}, u32[]{:S(2)}) %collective-permute-start.3) | collective-permute-done | bytes 131104 | tf_op jit(solution)/shard_map/ppermute | solution.py:479
  64.4 3.1 %collective-permute-done.4.ahead2_ref = bf16[256,256]{1,0:T(8,128)(2,1)S(1)} collective-permute-done((bf16[256,256]{1,0:T(8,128)(2,1)S(1)}, bf16[256,256]{1,0:T(8,128)(2,1)S(1)}, u32[]{:S(2)}, u32[]{:S(2)}) %collective-permute-start.4) | collective-permute-done | bytes 131104 | tf_op jit(solution)/shard_map/ppermute | solution.py:479
  67.5 0.8 %stack.1 = bf16[256,256]{1,0:T(8,128)(2,1)} custom-call(bf16[256,256]{1,0:T(8,128)(2,1)S(1)} %collective-permute-done.3.back2_ref, bf16[256,256]{1,0:T(8,128)(2,1)S(1)} %collective-permute-done.4.ahead2_ref, f32[256,256]{1,0:T(8,128)S(1)} %early.1.early_ref), custom_call_target="tpu_custom_call" | custom-call | tf_op jit(solution)/shard_map/stack/pallas_call | solution.py:391
Async XLA Ops:
  0.0 17.4 %copy-start = (bf16[1,128,2048]{2,1,0:T(8,128)(2,1)S(1)}, bf16[1,128,2048]{2,1,0:T(8,128)(2,1)}, u32[]{:S(2)}) copy-start(bf16[1,128,2048]{2,1,0:T(8,128)(2,1)} %param.5) | copy-start | bytes 1572868
  45.0 10.3 %collective-permute-start = (bf16[256,256]{1,0:T(8,128)(2,1)S(1)}, bf16[256,256]{1,0:T(8,128)(2,1)S(1)}, u32[]{:S(2)}, u32[]{:S(2)}) collective-permute-start(bf16[256,256]{1,0:T(8,128)(2,1)S(1)} %get-tuple-element.26), channel_id=1, source_target_pairs={{0,64},{1,193},{2,66},{3,195},{4,68},{5,197},{6,70},{7,199},{8,72}... | collective-permute-start | bytes 393224 | tf_op jit(solution)/shard_map/ppermute | solution.py:479
  51.2 7.0 %collective-permute-start.1 = (bf16[256,256]{1,0:T(8,128)(2,1)S(1)}, bf16[256,256]{1,0:T(8,128)(2,1)S(1)}, u32[]{:S(2)}, u32[]{:S(2)}) collective-permute-start(bf16[256,256]{1,0:T(8,128)(2,1)S(1)} %get-tuple-element.27), channel_id=1, source_target_pairs={{0,32},{1,225},{2,34},{3,227},{4,36},{5,229},{6,38},{7,231},{8,40}... | collective-permute-start | bytes 393224 | tf_op jit(solution)/shard_map/ppermute | solution.py:479
  51.9 6.3 %collective-permute-start.2 = (bf16[256,256]{1,0:T(8,128)(2,1)S(1)}, bf16[256,256]{1,0:T(8,128)(2,1)S(1)}, u32[]{:S(2)}, u32[]{:S(2)}) collective-permute-start(bf16[256,256]{1,0:T(8,128)(2,1)S(1)} %get-tuple-element.28), channel_id=1, source_target_pairs={{0,224},{1,33},{2,226},{3,35},{4,228},{5,37},{6,230},{7,39},{8,232... | collective-permute-start | bytes 393224 | tf_op jit(solution)/shard_map/ppermute | solution.py:479
  52.6 9.3 %collective-permute-start.5 = (bf16[256,256]{1,0:T(8,128)(2,1)S(1)}, bf16[256,256]{1,0:T(8,128)(2,1)S(1)}, u32[]{:S(2)}, u32[]{:S(2)}) collective-permute-start(bf16[256,256]{1,0:T(8,128)(2,1)S(1)} %get-tuple-element.31), channel_id=1, source_target_pairs={{0,224},{1,33},{2,226},{3,35},{4,228},{5,37},{6,230},{7,39},{8,232... | collective-permute-start | bytes 393224 | tf_op jit(solution)/shard_map/ppermute | solution.py:479
  53.3 8.6 %collective-permute-start.6 = (bf16[256,256]{1,0:T(8,128)(2,1)S(1)}, bf16[256,256]{1,0:T(8,128)(2,1)S(1)}, u32[]{:S(2)}, u32[]{:S(2)}) collective-permute-start(bf16[256,256]{1,0:T(8,128)(2,1)S(1)} %get-tuple-element.32), channel_id=1, source_target_pairs={{0,32},{1,225},{2,34},{3,227},{4,36},{5,229},{6,38},{7,231},{8,40}... | collective-permute-start | bytes 393224 | tf_op jit(solution)/shard_map/ppermute | solution.py:479
  58.3 6.1 %collective-permute-start.3 = (bf16[256,256]{1,0:T(8,128)(2,1)S(1)}, bf16[256,256]{1,0:T(8,128)(2,1)S(1)}, u32[]{:S(2)}, u32[]{:S(2)}) collective-permute-start(bf16[256,256]{1,0:T(8,128)(2,1)S(1)} %get-tuple-element.29), channel_id=1, source_target_pairs={{0,192},{1,65},{2,194},{3,67},{4,196},{5,69},{6,198},{7,71},{8,200... | collective-permute-start | bytes 393224 | tf_op jit(solution)/shard_map/ppermute | solution.py:479
  58.6 8.9 %collective-permute-start.4 = (bf16[256,256]{1,0:T(8,128)(2,1)S(1)}, bf16[256,256]{1,0:T(8,128)(2,1)S(1)}, u32[]{:S(2)}, u32[]{:S(2)}) collective-permute-start(bf16[256,256]{1,0:T(8,128)(2,1)S(1)} %get-tuple-element.30), channel_id=1, source_target_pairs={{0,64},{1,193},{2,66},{3,195},{4,68},{5,197},{6,70},{7,199},{8,72}... | collective-permute-start | bytes 393224 | tf_op jit(solution)/shard_map/ppermute | solution.py:479
